TPU v7x, 128 devices: a whole 4x4x4 slice. The times are simulated.
128 devices in a mesh: band: 16 (over y, z), patch: 8 (over x, core).
Axes of the slice: x: 4, y: 4, z: 4, core: 2. Of those that a mesh axis runs over, the one named last changes fastest.
Arguments:
- grid_state: bfloat16 [64, 2048, 512], P('band', 'patch'), may hold values from -6 to 6
- mesh_state: bfloat16 [16, 8, 256, 512], P('band', 'patch'), may hold values from -6 to 6
- g2m_features: bfloat16 [16, 8, 2048, 512], P('band', 'patch'), may hold values from -6 to 6
- g2m_sender: int32 [16, 8, 2048], P('band', 'patch'), may hold values from 0 to 2079, as said below
- g2m_receiver: int32 [16, 8, 2048], P('band', 'patch'), may hold values from 0 to 255
- g2m_blocks: int32 [16, 8], replicated, may hold values from 4 to 16, as said below
- proc_features: bfloat16 [16, 8, 2048, 512], P('band', 'patch'), may hold values from -6 to 6
- proc_sender: int32 [16, 8, 2048], P('band', 'patch'), may hold values from 0 to 4351, as said below
- proc_receiver: int32 [16, 8, 2048], P('band', 'patch'), may hold values from 0 to 255
- dec_features: bfloat16 [3, 64, 2048, 512], P(None, 'band', 'patch'), may hold values from -6 to 6
- dec_sender: int32 [3, 64, 2048], P(None, 'band', 'patch'), may hold values from 0 to 2111, as said below
- enc_weights: bfloat16 [9, 512, 512], replicated, may hold values from -0.25 to 0.25
- proc_weights: bfloat16 [7, 512, 512], replicated, may hold values from -0.25 to 0.25
- dec_weights: bfloat16 [7, 512, 512], replicated, may hold values from -0.25 to 0.25
Outputs:
- grid_out: bfloat16 [64, 2048, 512], P('band', 'patch')
Inputs may be any that keep to these rules, and one draw needn't show every extreme that they name: `g2m_blocks`: the bands at both poles hold 16 live blocks in every sector. `g2m_sender`: never a latitude row before the first or after the last of the grid. `proc_sender`: below 2304, s % 256 is below 64 unless s // 256 = 4; never a band before the first or after the last. `dec_sender`: s % 256 is below 64 unless s // 256 = 4; never a band before the first or after the last.
All inputs are finite; a program needn't handle non-finite values.
Results may differ from a plain program's by a relative error of at most 0.0095.
Values may be sent and summed in bfloat16 or wider, within the bound.
No kernel may reach another device: no remote copies, remote signals or barrier semaphores. Data moves between devices by JAX's collectives and lax.ppermute only.
A program may use at most 128 MiB of HBM per device.

v0:
```python
import jax
import jax.numpy as jnp
from jax import lax
from jax.sharding import PartitionSpec as P

COARSE_DEV = 16
HALO = 2


epsilon = 1e-05


def padded_2(cells, sides, width):
    for axis, dim in sides:
        count = lax.axis_size(axis)
        head = lax.slice_in_dim(cells, 0, width, axis=dim)
        tail = lax.slice_in_dim(cells, cells.shape[dim] - width, cells.shape[dim], axis=dim)
        cells = jnp.concatenate(
            [
                lax.ppermute(tail, axis, [(i, (i + 1) % count) for i in range(count)]),
                cells,
                lax.ppermute(head, axis, [((i + 1) % count, i) for i in range(count)]),
            ],
            axis=dim,
        )
    return cells


def layer_norm(values):
    average = jnp.mean(values, axis=-1, keepdims=True)
    centred = values - average
    spread = jnp.mean(centred * centred, axis=-1, keepdims=True)
    return centred * lax.rsqrt(spread + epsilon)


def project(values, weight):
    return jnp.dot(values, weight, preferred_element_type=jnp.float32)


def edge_message(features, send_rows, recv_rows, w_edge, w_out):
    before = (
        project(features, w_edge) + send_rows.astype(jnp.float32) + recv_rows.astype(jnp.float32)
    )
    hidden = jax.nn.silu(before).astype(jnp.bfloat16)
    return layer_norm(project(hidden, w_out)).astype(jnp.bfloat16)


def node_update(current, summed, w_self, w_total, w_out):
    before = project(current, w_self) + project(summed.astype(jnp.bfloat16), w_total)
    hidden = jax.nn.silu(before).astype(jnp.bfloat16)
    return (current.astype(jnp.float32) + layer_norm(project(hidden, w_out))).astype(jnp.bfloat16)


def self_update(current, w_first, w_out):
    hidden = jax.nn.silu(project(current, w_first)).astype(jnp.bfloat16)
    return (current.astype(jnp.float32) + layer_norm(project(hidden, w_out))).astype(jnp.bfloat16)


def one_hot_sum(summed, message, receiver):
    matches = (
        lax.broadcasted_iota(jnp.int32, (summed.shape[0], receiver.shape[0]), 0)
        == receiver[None, :]
    )
    return summed + jnp.dot(
        matches.astype(jnp.bfloat16), message, preferred_element_type=jnp.float32
    )


def shards(
    grid_state,
    mesh_state,
    g2m_features,
    g2m_sender,
    g2m_receiver,
    g2m_blocks,
    proc_features,
    proc_sender,
    proc_receiver,
    dec_features,
    dec_sender,
    enc_weights,
    proc_weights,
    dec_weights,
):
    lat_rows, lon_cols, latent = grid_state.shape
    node_count = mesh_state.shape[2]
    cell_count = lat_rows * lon_cols
    grid_flat = grid_state.reshape(cell_count, latent)
    mesh_flat = mesh_state.reshape(node_count, latent)
    grid_send = (
        project(grid_flat, enc_weights[0]).astype(jnp.bfloat16).reshape(lat_rows, lon_cols, latent)
    )
    padded = padded_2(grid_send, (("band", 0), ("patch", 1)), HALO)
    send_table = padded.reshape(-1, latent)
    mesh_recv = project(mesh_flat, enc_weights[1]).astype(jnp.bfloat16)
    enc_feats = g2m_features.reshape(-1, latent)
    enc_senders = g2m_sender.reshape(-1)
    enc_receivers = g2m_receiver.reshape(-1)
    band_index = lax.axis_index("band")
    patch_index = lax.axis_index("patch")
    own_blocks = g2m_blocks[band_index, patch_index]
    w_edge = enc_weights[2]
    w_out = enc_weights[3]

    def own_step(block, summed):
        start = block * 128
        features = lax.dynamic_slice_in_dim(enc_feats, start, 128, 0)
        sender = lax.dynamic_slice_in_dim(enc_senders, start, 128, 0)
        receiver = lax.dynamic_slice_in_dim(enc_receivers, start, 128, 0)
        send_rows = jnp.take(send_table, sender, axis=0)
        recv_rows = jnp.take(mesh_recv, receiver, axis=0)
        return one_hot_sum(
            summed, edge_message(features, send_rows, recv_rows, w_edge, w_out), receiver
        )

    empty = jnp.zeros((node_count, latent), jnp.float32)
    summed = lax.fori_loop(0, own_blocks, own_step, empty)
    mesh_next = node_update(mesh_flat, summed, enc_weights[4], enc_weights[5], enc_weights[6])
    grid_next = self_update(grid_flat, enc_weights[7], enc_weights[8])
    proc_send = project(mesh_next, proc_weights[0]).astype(jnp.bfloat16)
    proc_recv = project(mesh_next, proc_weights[1]).astype(jnp.bfloat16)
    coarse_all = lax.all_gather(
        proc_send[node_count - COARSE_DEV :], ("band", "patch"), axis=0, tiled=True
    )
    proc_senders = proc_sender.reshape(-1)
    rim_rows = padded_2(proc_send.reshape(1, 1, node_count, latent), (("band", 0), ("patch", 1)), 1)
    source = jnp.concatenate([rim_rows.reshape(-1, latent), coarse_all], axis=0)
    proc_receivers = proc_receiver.reshape(-1)
    message = edge_message(
        proc_features.reshape(-1, latent),
        jnp.take(source, proc_senders, axis=0),
        jnp.take(proc_recv, proc_receivers, axis=0),
        proc_weights[2],
        proc_weights[3],
    )
    proc_total = one_hot_sum(empty, message, proc_receivers)
    mesh_last = node_update(
        mesh_next, proc_total, proc_weights[4], proc_weights[5], proc_weights[6]
    )
    dec_send = project(mesh_last, dec_weights[0]).astype(jnp.bfloat16)
    dec_senders = dec_sender.reshape(-1)
    dec_rows = padded_2(dec_send.reshape(1, 1, node_count, latent), (("band", 0), ("patch", 1)), 1)
    dec_source = dec_rows.reshape(-1, latent)
    dec_recv = project(grid_next, dec_weights[1]).astype(jnp.bfloat16)
    before = project(dec_features.reshape(-1, latent), dec_weights[2]).reshape(
        3, cell_count, latent
    )
    before = before + jnp.take(dec_source, dec_senders, axis=0).astype(jnp.float32).reshape(
        3, cell_count, latent
    )
    before = before + dec_recv.astype(jnp.float32)[None]
    hidden = jax.nn.silu(before).astype(jnp.bfloat16).reshape(-1, latent)
    dec_message = (
        layer_norm(project(hidden, dec_weights[3]))
        .astype(jnp.bfloat16)
        .reshape(3, cell_count, latent)
    )
    dec_total = jnp.sum(dec_message.astype(jnp.float32), axis=0)
    result = node_update(grid_next, dec_total, dec_weights[4], dec_weights[5], dec_weights[6])
    return result.reshape(lat_rows, lon_cols, latent)


def solution(mesh):
    placed = (
        P("band", "patch", None),
        P("band", "patch", None, None),
        P("band", "patch", None, None),
        P("band", "patch", None),
        P("band", "patch", None),
        P(),
        P("band", "patch", None, None),
        P("band", "patch", None),
        P("band", "patch", None),
        P(None, "band", "patch", None),
        P(None, "band", "patch"),
        P(),
        P(),
        P(),
    )
    return jax.shard_map(
        shards, mesh=mesh, in_specs=placed, out_specs=P("band", "patch", None), check_vma=False
    )
```

profile of v0, /device:TPU:7, one launch (start us, length us, event | category | flops | bytes accessed | tf_op | source)
XLA Modules:
  0.0 421.7 jit_solution(17111387502629533043)
XLA Ops:
  11.5 4.6 %collective-permute-start.1 = (bf16[2,256,512]{2,1,0:T(8,128)(2,1)}, bf16[2,256,512]{2,1,0:T(8,128)(2,1)}, u32[]{:S(2)}, u32[]{:S(2)}) collective-permute-start(bf16[2,256,512]{2,1,0:T(8,128)(2,1)} %bitcast.17), channel_id=1, source_target_pairs={{8,0},{16,8},{24,16},{32,24},{40,32},{48,40},{56,48},{64,56},{72,6... | collective-permute-start | bytes 1572872 | tf_op jit(solution)/shard_map/ppermute | solution.py:22
  21.9 4.2 %fusion.117 = (f32[1024]{0:T(1024)S(1)}, f32[1024,512]{1,0:T(8,128)}) fusion(bf16[9,512,512]{2,1,0:T(8,128)(2,1)} %param.27, bf16[1024,512]{1,0:T(8,128)(2,1)} %bitcast.173), kind=kOutput, calls=%fused_computation.174 | convolution fusion | flops 1076886528 | bytes 4198400 | tf_op jit(solution)/shard_map/dot_general | solution.py:37
  34.6 3.1 pad_maximum_fusion.3
  37.7 3.9 reshape.277
  42.5 195.5 %while.10 = (s32[]{:T(128)}, f32[256,512]{1,0:T(8,128)}, s32[]{:T(128)}, s32[2048]{0:T(1024)}, bf16[2048,512]{1,0:T(8,128)(2,1)}, /*index=5*/bf16[512,512]{1,0:T...) while((s32[]{:T(128)}, f32[256,512]{1,0:T(8,128)}, ...), condition=%wide.region_5.6_spmd, body=%wide.region_2.5_spmd.sunk | while | flops 169119744 | bytes 3820987 | solution.py:117
  45.4 3.4 gather_fusion.1
  48.8 2.4 fusion.155
  57.6 3.4 gather_fusion.1
  61.0 2.4 fusion.155
  69.8 3.4 gather_fusion.1
  81.9 3.4 gather_fusion.1
  94.1 3.4 gather_fusion.1
  106.3 3.4 gather_fusion.1
  118.5 3.4 gather_fusion.1
  130.7 3.4 gather_fusion.1
  142.8 3.4 gather_fusion.1
  155.0 3.4 gather_fusion.1
  167.2 3.4 gather_fusion.1
  179.4 3.4 gather_fusion.1
  191.5 3.4 gather_fusion.1
  203.7 3.4 gather_fusion.1
  215.9 3.4 gather_fusion.1
  228.1 3.4 gather_fusion.1
  238.0 2.9 fusion.120
  250.2 5.0 %collective-permute-start.5 = (bf16[1,1,256,512]{3,2,1,0:T(8,128)(2,1)S(1)}, bf16[1,1,256,512]{3,2,1,0:T(8,128)(2,1)S(1)}, u32[]{:S(2)}, u32[]{:S(2)}) collective-permute-start(bf16[1,1,256,512]{3,2,1,0:T(8,128)(2,1)S(1)} %bitcast.169), channel_id=1, source_target_pairs={{8,0},{16,8},{24,16},{32,24},{40,32},{48,40},{56,48},{64,56},{72,6... | collective-permute-start | bytes 786440 | tf_op jit(solution)/shard_map/ppermute | solution.py:22
  255.3 6.0 %collective-permute-done.4 = bf16[1,1,256,512]{3,2,1,0:T(8,128)(2,1)S(1)} collective-permute-done((bf16[1,1,256,512]{3,2,1,0:T(8,128)(2,1)S(1)}, bf16[1,1,256,512]{3,2,1,0:T(8,128)(2,1)S(1)}, u32[]{:S(2)}, u32[]{:S(2)}) %collective-permute-start.4) | collective-permute-done | bytes 262176 | tf_op jit(solution)/shard_map/ppermute | solution.py:20
  263.3 3.2 fusion.26
  267.8 9.2 %gather_fusion.3 = bf16[2048,512]{1,0:T(8,128)(2,1)} fusion(bf16[256,512]{1,0:T(8,128)(2,1)S(1)} %convolution_convert_fusion.3, s32[2048]{0:T(1024)S(1)} %broadcast_clamp_fusion.1), kind=kCustom, calls=%fused_computation.3 | custom fusion | bytes 4202496 | tf_op jit(solution)/shard_map/jit(_take)/gather | solution.py:132
  279.3 2.8 pad_maximum_fusion.1
  282.1 28.1 %all-gather.2.cloned.1.call-done = bf16[2048,512]{1,0:T(8,128)(2,1)} async-done(((bf16[16,512]{1,0:T(8,128)(2,1)}), bf16[2048,512]{1,0:T(8,128)(2,1)}) %all-gather.2.cloned.1.call-update) | async-done | bytes 2097168 | tf_op jit(solution)/shard_map/all_gather | solution.py:122
  310.1 4.6 %pad_maximum_fusion = bf16[4352,512]{1,0:T(8,128)(2,1)} fusion(bf16[2048,512]{1,0:T(8,128)(2,1)} %all-gather.2.cloned.1.call-done, bf16[2304,512]{1,0:T(8,128)(2,1)} %bitcast.165), kind=kLoop, calls=%fused_computation.39 | loop fusion | flops 8912896 | bytes 8912896 | tf_op jit(solution)/shard_map/concatenate | solution.py:127
  314.8 12.1 %gather_fusion.2 = bf16[2048,512]{1,0:T(8,128)(2,1)} fusion(bf16[4352,512]{1,0:T(8,128)(2,1)} %pad_maximum_fusion, s32[2048]{0:T(1024)S(1)} %broadcast_clamp_fusion.2), kind=kCustom, calls=%fused_computation.2 | custom fusion | bytes 4202496 | tf_op jit(solution)/shard_map/jit(_take)/gather | solution.py:131
  326.9 7.3 %fusion.125 = (f32[2048]{0:T(1024)S(1)}, f32[2048,512]{0,1:T(8,128)}) fusion(bf16[7,512,512]{2,1,0:T(8,128)(2,1)} %param.28, bf16[1,1,2048,512]{3,2,1,0:T(8,128)(2,1)} %param.22, bf16[2048,512]{1,0:T(8,128)(2,1)} %gather_fusion.3, bf16[2048,512]{1,0:T(8,128)(2,1)} %gather_fusion.2, pred[2048]{0:T(1024)(128)(4,1)S(1)} %get-tuple-element.105, ...), kind=kOutput, calls=%fused_computation.176 | convolution fusion | flops 2160064512 | bytes 11546624 | tf_op jit(solution)/shard_map/dot_general | solution.py:37
  334.2 2.6 multiply_reduce_fusion.2
  336.8 4.3 %multiply_convert_fusion.15 = bf16[256,512]{1,0:T(8,128)(2,1)} fusion(f32[256,512]{1,0:T(8,128)} %fusion.50, f32[2048,512]{0,1:T(8,128)} %get-tuple-element.98, f32[2048]{0:T(1024)S(1)} %add_rsqrt_fusion.2, f32[2048]{0:T(1024)S(1)} %broadcast_multiply_fusion.2, s32[2048]{0:T(1024)S(1)} %bitcast.179, bf16[7,512,512]{2,1,0:T(8,128)(2,1)} %param.28), kind=kOutput, calls=%fused_computation.113 | convolution fusion | flops 675676160 | bytes 5529600 | tf_op jit(solution)/shard_map/dot_general | solution.py:37
  345.4 3.9 collective-permute-start.9
  349.3 6.2 %collective-permute-done.8 = bf16[1,1,256,512]{3,2,1,0:T(8,128)(2,1)S(1)} collective-permute-done((bf16[1,1,256,512]{3,2,1,0:T(8,128)(2,1)S(1)}, bf16[1,1,256,512]{3,2,1,0:T(8,128)(2,1)S(1)}, u32[]{:S(2)}, u32[]{:S(2)}) %collective-permute-start.8) | collective-permute-done | bytes 262176 | tf_op jit(solution)/shard_map/ppermute | solution.py:20
  355.6 3.0 collective-permute-start.10
  358.6 3.1 fusion.61
  361.7 5.5 %fusion.59 = f32[3,1024,512]{2,1,0:T(8,128)} fusion(bf16[3,1024,512]{2,1,0:T(8,128)(2,1)S(1)} %bitcast.160, bf16[7,512,512]{2,1,0:T(8,128)(2,1)} %param.29), kind=kOutput, calls=%fused_computation.98 | convolution fusion | flops 1610612736 | bytes 9961472 | tf_op jit(solution)/shard_map/dot_general | solution.py:37
  367.5 3.7 collective-permute-done.11
  372.8 15.3 %gather_fusion.4 = bf16[3072,512]{1,0:T(8,128)(2,1)} fusion(bf16[2304,512]{1,0:T(8,128)(2,1)} %bitcast.161, s32[3072]{0:T(1024)S(1)} %broadcast_clamp_fusion), kind=kCustom, calls=%fused_computation.4 | custom fusion | bytes 6303744 | tf_op jit(solution)/shard_map/jit(_take)/gather | solution.py:148
  388.1 5.4 %multiply_convert_fusion.4 = bf16[3,1024,512]{2,1,0:T(8,128)(2,1)S(1)} fusion(f32[3,1024,512]{2,1,0:T(8,128)} %fusion.59, f32[1024,512]{1,0:T(8,128)} %fusion.26, bf16[3,1024,512]{2,1,0:T(8,128)(2,1)} %bitcast.164, pred[3,1024]{1,0:T(4,128)(4,1)S(1)} %compare_and_fusion.2), kind=kLoop, calls=%fused_computation.38 | loop fusion | flops 14155776 | bytes 14683136 | tf_op jit(solution)/shard_map/convert_element_type | solution.py:152
  393.6 2.9 fusion.131
  398.6 2.8 multiply_convert_fusion.3
  401.5 3.7 reduce_sum.148
  405.2 4.9 %fusion.132 = (f32[1024]{0:T(1024)S(1)}, f32[1024,512]{1,0:T(8,128)}) fusion(bf16[7,512,512]{2,1,0:T(8,128)(2,1)} %param.29, f32[1024,512]{1,0:T(8,128)} %fusion.61, bf16[1024,512]{1,0:T(8,128)(2,1)} %reduce_sum.148), kind=kOutput, calls=%fused_computation.179 | convolution fusion | flops 1077410816 | bytes 6295552 | tf_op jit(solution)/shard_map/dot_general | solution.py:37
  412.3 2.6 add_convert_fusion
  (261 shorter events, 168.8 us)
Async XLA Ops:
  6.5 355.1 %copy-start = (bf16[3,4,256,512]{3,2,1,0:T(8,128)(2,1)S(1)}, bf16[3,4,256,512]{3,2,1,0:T(8,128)(2,1)}, u32[]{:S(2)}) copy-start(bf16[3,4,256,512]{3,2,1,0:T(8,128)(2,1)} %param.25) | copy-start | bytes 9437188
  6.5 303.6 %all-gather.2.cloned.1.call-start = ((), (), s32[]{:S(2)}) async-start(), calls=%async_computation | async-start | bytes 2113536 | tf_op jit(solution)/shard_map/all_gather | solution.py:122
  6.5 11.8 %copy-start.10 = (bf16[1,1,256,512]{3,2,1,0:T(8,128)(2,1)S(1)}, bf16[1,1,256,512]{3,2,1,0:T(8,128)(2,1)}, u32[]{:S(2)}) copy-start(bf16[1,1,256,512]{3,2,1,0:T(8,128)(2,1)} %param.17) | copy-start | bytes 786436
  8.8 7.3 %copy-start.3 = (bf16[1024,512]{1,0:T(8,128)(2,1)}, bf16[1024,512]{1,0:T(8,128)(2,1)S(1)}, u32[]{:S(2)}) copy-start(bf16[1024,512]{1,0:T(8,128)(2,1)S(1)} %convolution_convert_fusion.1) | copy-start | bytes 3145732
  9.9 18.2 %collective-permute-start = (bf16[2,256,512]{2,1,0:T(8,128)(2,1)}, bf16[2,256,512]{2,1,0:T(8,128)(2,1)}, u32[]{:S(2)}, u32[]{:S(2)}) collective-permute-start(bf16[2,256,512]{2,1,0:T(8,128)(2,1)} %bitcast.15), channel_id=1, source_target_pairs={{0,8},{8,16},{16,24},{24,32},{32,40},{40,48},{48,56},{56,64},{64,7... | collective-permute-start | bytes 1572872 | tf_op jit(solution)/shard_map/ppermute | solution.py:20
  11.5 16.5 %collective-permute-start.1 = (bf16[2,256,512]{2,1,0:T(8,128)(2,1)}, bf16[2,256,512]{2,1,0:T(8,128)(2,1)}, u32[]{:S(2)}, u32[]{:S(2)}) collective-permute-start(bf16[2,256,512]{2,1,0:T(8,128)(2,1)} %bitcast.17), channel_id=1, source_target_pairs={{8,0},{16,8},{24,16},{32,24},{40,32},{48,40},{56,48},{64,56},{72,6... | collective-permute-start | bytes 1572872 | tf_op jit(solution)/shard_map/ppermute | solution.py:22
  21.8 8.4 %copy-start.14 = (s32[3,4,256]{2,1,0:T(4,128)S(1)}, s32[3,4,256]{2,1,0:T(4,128)}, u32[]{:S(2)}) copy-start(s32[3,4,256]{2,1,0:T(4,128)} %param.26) | copy-start | bytes 36868
  28.9 3.3 collective-permute-start.2
  30.2 4.4 %collective-permute-start.3 = (bf16[8,2,512]{2,1,0:T(2,128)(2,1)S(1)}, bf16[8,2,512]{2,1,0:T(2,128)(2,1)S(1)}, u32[]{:S(2)}, u32[]{:S(2)}) collective-permute-start(bf16[8,2,512]{2,1,0:T(2,128)(2,1)S(1)} %get-tuple-element.90), channel_id=1, source_target_pairs={{1,0},{2,1},{3,2},{4,3},{5,4},{6,5},{7,6},{0,7},{9,8},{10,9},{11,1... | collective-permute-start | bytes 49160 | tf_op jit(solution)/shard_map/ppermute | solution.py:22
  238.0 4.2 copy-start.11
  240.9 7.4 %copy-start.17 = (s32[1,1,2048]{2,1,0:T(1,128)S(1)}, s32[1,1,2048]{2,1,0:T(1,128)}, u32[]{:S(2)}) copy-start(s32[1,1,2048]{2,1,0:T(1,128)} %param.23) | copy-start | bytes 24580
  243.4 0.7 copy-start.6
  245.5 15.9 %copy-start.9 = (bf16[256,512]{1,0:T(8,128)(2,1)}, bf16[256,512]{1,0:T(8,128)(2,1)S(1)}, u32[]{:S(2)}) copy-start(bf16[256,512]{1,0:T(8,128)(2,1)S(1)} %convolution_convert_fusion.4) | copy-start | bytes 786436
  246.1 2.2 copy-start.4
  246.2 3.9 copy-start.18
  246.2 3.9 copy-start.16
  246.2 9.1 %copy-start.15 = (s32[3,4,256]{2,1,0:T(4,128)S(1)}, s32[3,4,256]{2,1,0:T(4,128)}, u32[]{:S(2)}) copy-start(s32[3,4,256]{2,1,0:T(4,128)} %param.26) | copy-start | bytes 36868
  250.1 13.2 %copy-start.1 = (bf16[1024,512]{1,0:T(8,128)(2,1)}, bf16[1024,512]{1,0:T(8,128)(2,1)S(1)}, u32[]{:S(2)}) copy-start(bf16[1024,512]{1,0:T(8,128)(2,1)S(1)} %add_convert_fusion.1) | copy-start | bytes 3145732
  250.1 16.4 %copy-start.7 = (bf16[256,512]{1,0:T(8,128)(2,1)S(1)}, bf16[256,512]{1,0:T(8,128)(2,1)}, u32[]{:S(2)}) copy-start(bf16[256,512]{1,0:T(8,128)(2,1)} %copy-done.6) | copy-start | bytes 786436
  250.1 11.2 %collective-permute-start.4 = (bf16[1,1,256,512]{3,2,1,0:T(8,128)(2,1)S(1)}, bf16[1,1,256,512]{3,2,1,0:T(8,128)(2,1)S(1)}, u32[]{:S(2)}, u32[]{:S(2)}) collective-permute-start(bf16[1,1,256,512]{3,2,1,0:T(8,128)(2,1)S(1)} %bitcast.168), channel_id=1, source_target_pairs={{0,8},{8,16},{16,24},{24,32},{32,40},{40,48},{48,56},{56,64},{64,7... | collective-permute-start | bytes 786440 | tf_op jit(solution)/shard_map/ppermute | solution.py:20
  250.2 11.1 %collective-permute-start.5 = (bf16[1,1,256,512]{3,2,1,0:T(8,128)(2,1)S(1)}, bf16[1,1,256,512]{3,2,1,0:T(8,128)(2,1)S(1)}, u32[]{:S(2)}, u32[]{:S(2)}) collective-permute-start(bf16[1,1,256,512]{3,2,1,0:T(8,128)(2,1)S(1)} %bitcast.169), channel_id=1, source_target_pairs={{8,0},{16,8},{24,16},{32,24},{40,32},{48,40},{56,48},{64,56},{72,6... | collective-permute-start | bytes 786440 | tf_op jit(solution)/shard_map/ppermute | solution.py:22
  261.3 5.1 %copy-start.12 = (bf16[1,1,256,512]{3,2,1,0:T(8,128)(2,1)}, bf16[1,1,256,512]{3,2,1,0:T(8,128)(2,1)S(1)}, u32[]{:S(2)}) copy-start(bf16[1,1,256,512]{3,2,1,0:T(8,128)(2,1)S(1)} %collective-permute-done.4) | copy-start | bytes 786436
  261.3 5.1 %copy-start.13 = (bf16[1,1,256,512]{3,2,1,0:T(8,128)(2,1)}, bf16[1,1,256,512]{3,2,1,0:T(8,128)(2,1)S(1)}, u32[]{:S(2)}) copy-start(bf16[1,1,256,512]{3,2,1,0:T(8,128)(2,1)S(1)} %collective-permute-done.5) | copy-start | bytes 786436
  262.4 16.9 %collective-permute-start.6 = (bf16[3,1,256,512]{3,2,1,0:T(8,128)(2,1)}, bf16[3,1,256,512]{3,2,1,0:T(8,128)(2,1)}, u32[]{:S(2)}, u32[]{:S(2)}) collective-permute-start(bf16[3,1,256,512]{3,2,1,0:T(8,128)(2,1)} %pad_maximum_fusion.4), channel_id=1, source_target_pairs={{0,1},{1,2},{2,3},{3,4},{4,5},{5,6},{6,7},{7,0},{8,9},{9,10},{10,1... | collective-permute-start | bytes 2359304 | tf_op jit(solution)/shard_map/ppermute | solution.py:20
  263.3 16.0 %collective-permute-start.7 = (bf16[3,1,256,512]{3,2,1,0:T(8,128)(2,1)}, bf16[3,1,256,512]{3,2,1,0:T(8,128)(2,1)}, u32[]{:S(2)}, u32[]{:S(2)}) collective-permute-start(bf16[3,1,256,512]{3,2,1,0:T(8,128)(2,1)} %pad_maximum_fusion.4), channel_id=1, source_target_pairs={{1,0},{2,1},{3,2},{4,3},{5,4},{6,5},{7,6},{0,7},{9,8},{10,9},{11,1... | collective-permute-start | bytes 2359304 | tf_op jit(solution)/shard_map/ppermute | solution.py:22
  336.8 6.2 %copy-start.8 = (bf16[256,512]{1,0:T(8,128)(2,1)S(1)}, bf16[256,512]{1,0:T(8,128)(2,1)}, u32[]{:S(2)}) copy-start(bf16[256,512]{1,0:T(8,128)(2,1)} %copy-done.6) | copy-start | bytes 786436
  341.2 17.4 %copy-start.2 = (bf16[1024,512]{1,0:T(8,128)(2,1)S(1)}, bf16[1024,512]{1,0:T(8,128)(2,1)}, u32[]{:S(2)}) copy-start(bf16[1024,512]{1,0:T(8,128)(2,1)} %copy-done.1) | copy-start | bytes 3145732
  344.4 11.1 %collective-permute-start.8 = (bf16[1,1,256,512]{3,2,1,0:T(8,128)(2,1)S(1)}, bf16[1,1,256,512]{3,2,1,0:T(8,128)(2,1)S(1)}, u32[]{:S(2)}, u32[]{:S(2)}) collective-permute-start(bf16[1,1,256,512]{3,2,1,0:T(8,128)(2,1)S(1)} %fusion.29), channel_id=1, source_target_pairs={{0,8},{8,16},{16,24},{24,32},{32,40},{40,48},{48,56},{56,64},{64,7... | collective-permute-start | bytes 786440 | tf_op jit(solution)/shard_map/ppermute | solution.py:20
  345.4 10.1 %collective-permute-start.9 = (bf16[1,1,256,512]{3,2,1,0:T(8,128)(2,1)S(1)}, bf16[1,1,256,512]{3,2,1,0:T(8,128)(2,1)S(1)}, u32[]{:S(2)}, u32[]{:S(2)}) collective-permute-start(bf16[1,1,256,512]{3,2,1,0:T(8,128)(2,1)S(1)} %fusion.29), channel_id=1, source_target_pairs={{8,0},{16,8},{24,16},{32,24},{40,32},{48,40},{56,48},{64,56},{72,6... | collective-permute-start | bytes 786440 | tf_op jit(solution)/shard_map/ppermute | solution.py:22
  355.6 12.0 %collective-permute-start.10 = (bf16[3,1,256,512]{3,2,1,0:T(8,128)(2,1)S(1)}, bf16[3,1,256,512]{3,2,1,0:T(8,128)(2,1)S(1)}, u32[]{:S(2)}, u32[]{:S(2)}) collective-permute-start(bf16[3,1,256,512]{3,2,1,0:T(8,128)(2,1)S(1)} %pad_maximum_fusion.5), channel_id=1, source_target_pairs={{0,1},{1,2},{2,3},{3,4},{4,5},{5,6},{6,7},{7,0},{8,9},{9,10},{10,1... | collective-permute-start | bytes 2359304 | tf_op jit(solution)/shard_map/ppermute | solution.py:20
  358.6 12.6 %collective-permute-start.11 = (bf16[3,1,256,512]{3,2,1,0:T(8,128)(2,1)S(1)}, bf16[3,1,256,512]{3,2,1,0:T(8,128)(2,1)S(1)}, u32[]{:S(2)}, u32[]{:S(2)}) collective-permute-start(bf16[3,1,256,512]{3,2,1,0:T(8,128)(2,1)S(1)} %pad_maximum_fusion.5), channel_id=1, source_target_pairs={{1,0},{2,1},{3,2},{4,3},{5,4},{6,5},{7,6},{0,7},{9,8},{10,9},{11,1... | collective-permute-start | bytes 2359304 | tf_op jit(solution)/shard_map/ppermute | solution.py:22
  410.0 2.2 copy-start.5
Sparse Core Ops, SparseCore 0:
  246.3 63.8 all-gather.1
where the time goes:
time: 425 us; the launch traced here: 422 us
  matrix products  126 us (30%)
  local copies, waits for them, and re-layouts  117 us (28%)
  other arithmetic  82.3 us (19%)
  waiting for transfers between devices  48.7 us (11%)
  starting transfers between devices  21.4 us (5%)
  between operations  13.8 us (3%)
  loops' own time  12.4 us (3%)
    dot_general x33, matrix products, project(): return jnp.dot(values, weight, preferred_element_type=jnp.float32)  90.8 us
    gather x16, local copies, waits for them, and re-layouts, own_step(): send_rows = jnp.take(send_table, sender, axis=0)  54.7 us
    dot_general x16, matrix products, one_hot_sum(): jnp.dot(matches.astype(jnp.bfloat16), message, preferred_element_type=jnp...  35.7 us
    reduce_sum x22, other arithmetic, layer_norm(): spread = jnp.mean(centred * centred, axis=-1, keepdims=True)  28.4 us
    all_gather x1, waiting for transfers between devices, shards(): lax.all_gather(proc_send[node_count - COARSE_DEV:], ('band', 'patch'), ax...  28.1 us
    and x16, other arithmetic, own_step(): recv_rows = jnp.take(mesh_recv, receiver, axis=0)  21.8 us
    gather x1, local copies, waits for them, and re-layouts, shards(): jnp.take(dec_source, dec_senders, axis=0).astype(jnp.float32)  15.3 us
    ppermute x6, waiting for transfers between devices, padded_2(): lax.ppermute(tail, axis, [(i, (i + 1) % count) for i in range(count)])  14.6 us
  transfers between devices with their start and end apart: 13, of which 7 were waited for; matrix products, arithmetic and copies ran while one was open for 10% of the time, Pallas kernels for 0%

commit v1 on v0

v1 whole, which is shorter than its diff:
```python
import jax
import jax.numpy as jnp
from jax import lax
from jax.experimental import pallas as pl
from jax.experimental.pallas import tpu as pltpu
from jax.sharding import PartitionSpec as P

D = 512
AXES = ("band", "patch")
BANDS, PATCHES = 16, 8
EDGE_BLOCK = 256
epsilon = 1e-05
F32, BF16 = jnp.float32, jnp.bfloat16


def split(device):
    band, patch = divmod(device, PATCHES)
    return band // 4, band % 4, patch // 2, patch % 2


def torus(dy=0, dz=0, dx=0, dc=0):
    pairs = []
    for device in range(BANDS * PATCHES):
        y, z, x, c = split(device)
        band = (y + dy) % 4 * 4 + (z + dz) % 4
        patch = (x + dx) % 4 * 2 + (c + dc) % 2
        pairs.append((device, band * PATCHES + patch))
    return pairs


def plane(db, dp):
    return [
        (b * PATCHES + p, (b + db) % BANDS * PATCHES + (p + dp) % PATCHES)
        for b in range(BANDS)
        for p in range(PATCHES)
    ]


def send(values, pairs):
    return lax.ppermute(values, AXES, pairs)


def dot(a, b):
    return jnp.dot(a, b, preferred_element_type=F32)


def silu(v):
    half = 0.5 * v
    return half + half * jnp.tanh(half)


def layer_norm(v):
    centred = v - jnp.mean(v, axis=-1, keepdims=True)
    spread = jnp.mean(centred * centred, axis=-1, keepdims=True)
    return centred * lax.rsqrt(spread + epsilon)


def column(row):
    return jnp.transpose(jnp.broadcast_to(row, (8, row.shape[1])))[:, :1]


def pick_rows(row, count):
    col = column(row)
    lanes = lax.broadcasted_iota(jnp.int32, (row.shape[1], count), 1)
    return jnp.where(lanes == col, 1.0, 0.0).astype(BF16)


def add_rows(row, count):
    nodes = lax.broadcasted_iota(jnp.int32, (count, row.shape[1]), 0)
    return jnp.where(nodes == row, 1.0, 0.0).astype(BF16)


def weight(k):
    return pl.BlockSpec((None, D, D), lambda i: (k, 0, 0))


def whole(shape):
    return pl.BlockSpec(shape, lambda i: (0,) * len(shape))


def params(mb):
    return pltpu.CompilerParams(
        dimension_semantics=("arbitrary",), vmem_limit_bytes=mb << 20
    )


def cost(rows, nbytes):
    return pl.CostEstimate(flops=2 * rows * D * D, bytes_accessed=nbytes, transcendentals=0)


def grid_body(x_ref, w0, w7, w8, d1, sent, nxt, recv):
    x = x_ref[...]
    sent[...] = dot(x, w0[...]).astype(BF16)
    hidden = silu(dot(x, w7[...])).astype(BF16)
    y = (x.astype(F32) + layer_norm(dot(hidden, w8[...]))).astype(BF16)
    nxt[...] = y
    recv[...] = dot(y, d1[...]).astype(BF16)


def grid_kernel(grid_flat, enc_w, dec_w):
    blk = pl.BlockSpec((256, D), lambda i: (i, 0))
    return pl.pallas_call(
        grid_body,
        grid=(4,),
        in_specs=[blk, weight(0), weight(7), weight(8), weight(1)],
        out_specs=[blk] * 3,
        out_shape=[jax.ShapeDtypeStruct((1024, D), BF16)] * 3,
        compiler_params=params(24),
        cost_estimate=cost(4096, 6 << 20),
        name="grid_cells",
    )(grid_flat, enc_w, enc_w, enc_w, dec_w)


def enc_body(
    live, feat, snd, rcv, own, top, bottom, side, mesh_ref,
    w0, w1, w2, w3, w4, w5, w6, p0, p1,
    nxt, psend, precv, table, total,
):
    step = pl.program_id(0)

    @pl.when(step == 0)
    def _():
        table[0:512] = dot(top[...], w0[...]).astype(BF16)
        table[512:1536] = own[...]
        table[1536:2048] = dot(bottom[...], w0[...]).astype(BF16)
        table[2048:2080] = dot(side[...], w0[...]).astype(BF16)
        table[2080:2176] = jnp.zeros((96, D), BF16)
        table[2176:2432] = dot(mesh_ref[...], w1[...]).astype(BF16)
        total[...] = jnp.zeros_like(total)

    receiver = rcv[...]
    ones = jnp.concatenate([pick_rows(snd[...], 2176), pick_rows(receiver, 256)], axis=1)
    before = dot(feat[...], w2[...]) + dot(ones, table[...])
    hidden = silu(before).astype(BF16)
    message = layer_norm(dot(hidden, w3[...])).astype(BF16)
    edge = step * EDGE_BLOCK + lax.broadcasted_iota(jnp.int32, (1, EDGE_BLOCK), 1)
    target = jnp.where(edge < live[0] * 128, receiver, -1)
    total[...] += dot(add_rows(target, 256), message)

    @pl.when(step == pl.num_programs(0) - 1)
    def _():
        m = mesh_ref[...]
        hid = silu(dot(m, w4[...]) + dot(total[...].astype(BF16), w5[...])).astype(BF16)
        new = (m.astype(F32) + layer_norm(dot(hid, w6[...]))).astype(BF16)
        nxt[...] = new
        psend[...] = dot(new, p0[...]).astype(BF16)
        precv[...] = dot(new, p1[...]).astype(BF16)


def edge_rows():
    return pl.BlockSpec((None, 1, EDGE_BLOCK), lambda i: (i, 0, 0))


def enc_kernel(live, feats, senders, receivers, own, top, bottom, side, mesh_flat, enc_w, proc_w):
    steps = feats.shape[0] // EDGE_BLOCK
    node = whole((256, D))
    return pl.pallas_call(
        enc_body,
        grid=(steps,),
        in_specs=[
            pl.BlockSpec(memory_space=pltpu.SMEM),
            pl.BlockSpec((EDGE_BLOCK, D), lambda i: (i, 0)),
            edge_rows(),
            edge_rows(),
            whole((1024, D)),
            whole((512, D)),
            whole((512, D)),
            whole((32, D)),
            node,
        ]
        + [weight(k) for k in range(7)]
        + [weight(0), weight(1)],
        out_specs=[node] * 3,
        out_shape=[jax.ShapeDtypeStruct((256, D), BF16)] * 3,
        scratch_shapes=[pltpu.VMEM((2432, D), BF16), pltpu.VMEM((256, D), F32)],
        compiler_params=params(40),
        cost_estimate=cost(16000, 10 << 20),
        name="encoder_edges",
    )(
        live, feats, senders.reshape(steps, 1, -1), receivers.reshape(steps, 1, -1),
        own, top, bottom, side, mesh_flat, *[enc_w] * 7, proc_w, proc_w,
    )


def proc_body(
    feat, snd, rcv, mine, theirs, near, recv, mesh_ref,
    w2, w3, w4, w5, w6, d0,
    dsend, table, total,
):
    step = pl.program_id(0)

    @pl.when(step == 0)
    def _():
        table[0:1024] = mine[...]
        table[1024:2048] = theirs[...]
        table[2048:2816] = near[...]
        table[2816:3072] = recv[...]
        total[...] = jnp.zeros_like(total)

    receiver = rcv[...]
    ones = jnp.concatenate([pick_rows(snd[...], 2816), pick_rows(receiver, 256)], axis=1)
    before = dot(feat[...], w2[...]) + dot(ones, table[...])
    hidden = silu(before).astype(BF16)
    message = layer_norm(dot(hidden, w3[...])).astype(BF16)
    total[...] += dot(add_rows(receiver, 256), message)

    @pl.when(step == pl.num_programs(0) - 1)
    def _():
        m = mesh_ref[...]
        hid = silu(dot(m, w4[...]) + dot(total[...].astype(BF16), w5[...])).astype(BF16)
        new = (m.astype(F32) + layer_norm(dot(hid, w6[...]))).astype(BF16)
        dsend[...] = dot(new, d0[...]).astype(BF16)


def proc_kernel(feats, senders, receivers, mine, theirs, near, recv, mesh_next, proc_w, dec_w):
    steps = feats.shape[0] // EDGE_BLOCK
    node = whole((256, D))

    return pl.pallas_call(
        proc_body,
        grid=(steps,),
        in_specs=[
            pl.BlockSpec((EDGE_BLOCK, D), lambda i: (i, 0)),
            edge_rows(),
            edge_rows(),
            whole((1024, D)),
            whole((1024, D)),
            whole((768, D)),
            node,
            node,
        ]
        + [weight(k) for k in range(2, 7)]
        + [weight(0)],
        out_specs=node,
        out_shape=jax.ShapeDtypeStruct((256, D), BF16),
        scratch_shapes=[pltpu.VMEM((3072, D), BF16), pltpu.VMEM((256, D), F32)],
        compiler_params=params(40),
        cost_estimate=cost(19000, 10 << 20),
        name="mesh_edges",
    )(
        feats, senders.reshape(steps, 1, -1), receivers.reshape(steps, 1, -1),
        mine, theirs, near, recv, mesh_next, *[proc_w] * 5, dec_w,
    )


def dec_body(feat, snd, near, recv, cells, w2, w3, w4, w5, w6, out):
    r = recv[...].astype(F32)
    summed = None
    for k in range(3):
        before = dot(feat[k], w2[...]) + dot(pick_rows(snd[k], 768), near[...]) + r
        hidden = silu(before).astype(BF16)
        message = layer_norm(dot(hidden, w3[...])).astype(BF16).astype(F32)
        summed = message if summed is None else summed + message
    g = cells[...]
    hid = silu(dot(g, w4[...]) + dot(summed.astype(BF16), w5[...])).astype(BF16)
    out[...] = (g.astype(F32) + layer_norm(dot(hid, w6[...]))).astype(BF16)


def dec_kernel(feats, senders, near, recv, grid_next, dec_w):
    lat, lon = senders.shape[1:]
    blk = pl.BlockSpec((lon, D), lambda i: (i, 0))
    return pl.pallas_call(
        dec_body,
        grid=(lat,),
        in_specs=[
            pl.BlockSpec((3, None, lon, D), lambda i: (0, i, 0, 0)),
            pl.BlockSpec((3, None, 1, lon), lambda i: (0, i, 0, 0)),
            whole((768, D)),
            blk,
            blk,
        ]
        + [weight(k) for k in range(2, 7)],
        out_specs=blk,
        out_shape=jax.ShapeDtypeStruct((lat * lon, D), BF16),
        compiler_params=params(40),
        cost_estimate=cost(15000, 9 << 20),
        name="decoder_edges",
    )(feats, senders.reshape(3, lat, 1, lon), near, recv, grid_next, *[dec_w] * 5)


def near_rows(own):
    rim = own[:64]
    above, below = send(rim, plane(1, 0)), send(rim, plane(-1, 0))
    col = jnp.concatenate([above, rim, below], axis=0)
    left, right = send(col, plane(0, 1)), send(col, plane(0, -1))
    return jnp.concatenate([above, own, below, left, right], axis=0)


def near_index(sender):
    q, r = sender // 256, sender % 256
    row, col = q // 3, q % 3
    middle = jnp.where(row == 0, 0, jnp.where(row == 1, 64, 320))
    aside = jnp.where(col == 0, 384, 576) + row * 64
    return jnp.where(col == 1, middle, aside) + r


def coarse_rows(rows):
    for axis in ("dx", "dy"):
        rows = jnp.concatenate(
            [rows] + [send(rows, torus(**{axis: k})) for k in (1, 2, 3)], axis=0
        )
    mine = jnp.concatenate([rows] + [send(rows, torus(dz=k)) for k in (1, 2, 3)], axis=0)
    return mine, send(mine, torus(dc=1))


def coarse_index(c):
    band, patch = lax.axis_index("band"), lax.axis_index("patch")
    device, row = c // 16, c % 16
    b, p = device // PATCHES, device % PATCHES
    ky = (band // 4 - b // 4) % 4
    kz = (band % 4 - b % 4) % 4
    kx = (patch // 2 - p // 2) % 4
    kc = (patch % 2 - p % 2) % 2
    return kc * 1024 + kz * 256 + ky * 64 + kx * 16 + row


def shards(
    grid_state,
    mesh_state,
    g2m_features,
    g2m_sender,
    g2m_receiver,
    g2m_blocks,
    proc_features,
    proc_sender,
    proc_receiver,
    dec_features,
    dec_sender,
    enc_weights,
    proc_weights,
    dec_weights,
):
    cells = grid_state.reshape(1024, D)
    nodes = mesh_state.reshape(256, D)
    top = send(grid_state[2:4], plane(1, 0))
    bottom = send(grid_state[0:2], plane(-1, 0))
    west = send(grid_state[:, 254:256], plane(0, 1))
    east = send(grid_state[:, 0:2], plane(0, -1))
    flank = jnp.concatenate([west, east], axis=1)
    side = jnp.concatenate(
        [send(flank[2:4], plane(1, 0)), flank, send(flank[0:2], plane(-1, 0))], axis=0
    ).reshape(32, D)
    s = g2m_sender.reshape(-1)
    i, j = s // 260, s % 260
    inner = (j >= 2) & (j < 258)
    enc_sender = jnp.where(
        inner, i * 256 + j - 2, 2048 + i * 4 + jnp.where(j < 2, j, j - 256)
    )
    s = proc_sender.reshape(-1)
    mesh_sender = jnp.where(
        s < 2304, 2048 + near_index(jnp.minimum(s, 2303)), coarse_index(jnp.maximum(s - 2304, 0))
    )
    grid_sender = near_index(dec_sender)
    live = g2m_blocks[lax.axis_index("band"), lax.axis_index("patch")].reshape(1)

    grid_send, grid_next, dec_recv = grid_kernel(cells, enc_weights, dec_weights)
    mesh_next, proc_send, proc_recv = enc_kernel(
        live, g2m_features.reshape(-1, D), enc_sender, g2m_receiver.reshape(-1),
        grid_send, top.reshape(512, D), bottom.reshape(512, D), side, nodes,
        enc_weights, proc_weights,
    )
    mine, theirs = coarse_rows(proc_send[240:256])
    dec_send = proc_kernel(
        proc_features.reshape(-1, D), mesh_sender, proc_receiver.reshape(-1),
        mine, theirs, near_rows(proc_send), proc_recv, mesh_next, proc_weights, dec_weights,
    )
    out = dec_kernel(
        dec_features, grid_sender, near_rows(dec_send), dec_recv, grid_next, dec_weights
    )
    return out.reshape(grid_state.shape)


def solution(mesh):
    placed = (
        P("band", "patch", None),
        P("band", "patch", None, None),
        P("band", "patch", None, None),
        P("band", "patch", None),
        P("band", "patch", None),
        P(),
        P("band", "patch", None, None),
        P("band", "patch", None),
        P("band", "patch", None),
        P(None, "band", "patch", None),
        P(None, "band", "patch"),
        P(),
        P(),
        P(),
    )
    return jax.shard_map(
        shards, mesh=mesh, in_specs=placed, out_specs=P("band", "patch", None), check_vma=False
    )
```

time: 425 us -> 151 us (0.36)
  matrix products: 126 us -> 0 us
  local copies, waits for them, and re-layouts: 117 us -> 23.5 us
  other arithmetic: 82.3 us -> 2.18 us
  Pallas kernels: 0 us -> 55.3 us
  waiting for transfers between devices: 48.7 us -> 29.8 us
  starting transfers between devices: 21.4 us -> 38.5 us
  between operations: 13.8 us -> 0.49 us
  loops' own time: 12.4 us -> 0 us
    dot_general x49 -> x0, matrix products: 126 us -> none  [the longest x33 90.8 us: project(): return jnp.dot(values, weight, preferred_element_type=jnp.float32)]
    gather x35 -> x0, local copies, waits for them, and re-layouts: 105 us -> none  [the longest x16 54.7 us: own_step(): send_rows = jnp.take(send_table, sender, axis=0)]
    pallas_call x0 -> x4, Pallas kernels: none -> 55.3 us  [the longest x1 18.7 us: enc_kernel(): pl.pallas_call(enc_body, grid=(steps,), in_specs=[pl.BlockSpec(memory_spa...]
    reduce_sum x23 -> x0, other arithmetic: 32.1 us -> none  [the longest x22 28.4 us: layer_norm(): spread = jnp.mean(centred * centred, axis=-1, keepdims=True)]
    all_gather x1 -> x0, waiting for transfers between devices: 28.1 us -> none  [shards(): lax.all_gather(proc_send[node_count - COARSE_DEV:], ('band', 'patch'), ax...]
    and x18 -> x0, other arithmetic: 21.9 us -> none  [the longest x16 21.8 us: own_step(): recv_rows = jnp.take(mesh_recv, receiver, axis=0)]
    unnamed x39 -> x62, local copies, waits for them, and re-layouts: 0.85 us -> 19.1 us
    ppermute x12 -> x24, starting transfers between devices: 21.4 us -> 38.5 us  [send(): return lax.ppermute(values, AXES, pairs)]
  transfers between devices with their start and end apart: 13 -> 24, of which waited for: 7 -> 12; matrix products, arithmetic and copies ran while one was open for 10% -> 4% of each run, Pallas kernels for 0% -> 3%
where the time goes in v1:
time: 151 us; the launch traced here: 150 us
  Pallas kernels  55.3 us (37%)
  starting transfers between devices  38.5 us (25%)
  waiting for transfers between devices  29.8 us (20%)
  local copies, waits for them, and re-layouts  23.5 us (16%)
  other arithmetic  2.18 us (1%)
    ppermute x24, starting transfers between devices, send(): return lax.ppermute(values, AXES, pairs)  38.5 us
    ppermute x24, waiting for transfers between devices, send(): return lax.ppermute(values, AXES, pairs)  29.8 us
    unnamed x62, local copies, waits for them, and re-layouts  19.1 us
    pallas_call x1, Pallas kernels, enc_kernel(): pl.pallas_call(enc_body, grid=(steps,), in_specs=[pl.BlockSpec(memory_spa...  18.7 us
    pallas_call x1, Pallas kernels, proc_kernel(): pl.pallas_call(proc_body, grid=(steps,), in_specs=[pl.BlockSpec((EDGE_BLO...  18.3 us
    pallas_call x1, Pallas kernels, dec_kernel(): pl.pallas_call(dec_body, grid=(lat,), in_specs=[pl.BlockSpec((3, None, lo...  13.7 us
    pallas_call x1, Pallas kernels, grid_kernel(): pl.pallas_call(grid_body, grid=(4,), in_specs=[blk, weight(0), weight(7),...  4.6 us
  transfers between devices with their start and end apart: 24, of which 12 were waited for; matrix products, arithmetic and copies ran while one was open for 4% of the time, Pallas kernels for 3%

profile of v1, /device:TPU:7, one launch (start us, length us, event | category | flops | bytes accessed | tf_op | source)
XLA Modules:
  0.0 149.8 jit_solution(5579498457204587580)
XLA Ops:
  0.0 0.8 fusion.22
  0.8 0.7 collective-permute-start.2
  1.5 2.3 %fusion.23 = (bf16[2,256,512]{2,1,0:T(8,128)(2,1)}, bf16[2,256,512]{2,1,0:T(8,128)(2,1)}) fusion(bf16[4,256,512]{2,1,0:T(8,128)(2,1)} %param.14), kind=kLoop, calls=%fused_computation.120 | loop fusion | bytes 2097152 | tf_op jit(solution)/shard_map/slice | solution.py:336
  3.8 1.7 %collective-permute-start = (bf16[2,256,512]{2,1,0:T(8,128)(2,1)}, bf16[2,256,512]{2,1,0:T(8,128)(2,1)}, u32[]{:S(2)}, u32[]{:S(2)}) collective-permute-start(bf16[2,256,512]{2,1,0:T(8,128)(2,1)} %get-tuple-element.20), channel_id=1, source_target_pairs={{0,8},{1,9},{2,10},{3,11},{4,12},{5,13},{6,14},{7,15},{8,16},{9,17... | collective-permute-start | bytes 1572872 | tf_op jit(solution)/shard_map/ppermute | solution.py:40
  5.5 4.6 %collective-permute-start.1 = (bf16[2,256,512]{2,1,0:T(8,128)(2,1)}, bf16[2,256,512]{2,1,0:T(8,128)(2,1)}, u32[]{:S(2)}, u32[]{:S(2)}) collective-permute-start(bf16[2,256,512]{2,1,0:T(8,128)(2,1)} %get-tuple-element.19), channel_id=1, source_target_pairs={{0,120},{1,121},{2,122},{3,123},{4,124},{5,125},{6,126},{7,127},{8... | collective-permute-start | bytes 1572872 | tf_op jit(solution)/shard_map/ppermute | solution.py:40
  10.0 0.7 broadcast_divide_fusion
  10.8 0.7 sign_compare_fusion.2
  11.7 4.8 %collective-permute-start.5 = (bf16[2,4,512]{2,1,0:T(4,128)(2,1)S(1)}, bf16[2,4,512]{2,1,0:T(4,128)(2,1)S(1)}, u32[]{:S(2)}, u32[]{:S(2)}) collective-permute-start(bf16[2,4,512]{2,1,0:T(4,128)(2,1)S(1)} %get-tuple-element.37), channel_id=1, source_target_pairs={{0,120},{1,121},{2,122},{3,123},{4,124},{5,125},{6,126},{7,127},{8... | collective-permute-start | bytes 24584 | tf_op jit(solution)/shard_map/ppermute | solution.py:40
  16.5 2.3 %copy-done = bf16[9,512,512]{2,1,0:T(8,128)(2,1)S(1)} copy-done((bf16[9,512,512]{2,1,0:T(8,128)(2,1)S(1)}, bf16[9,512,512]{2,1,0:T(8,128)(2,1)}, u32[]{:S(2)}) %copy-start) | copy-done | bytes 4718616
  18.8 1.2 copy-done.4
  20.0 2.0 %copy-done.5 = bf16[7,512,512]{2,1,0:T(8,128)(2,1)S(1)} copy-done((bf16[7,512,512]{2,1,0:T(8,128)(2,1)S(1)}, bf16[7,512,512]{2,1,0:T(8,128)(2,1)}, u32[]{:S(2)}) %copy-start.5) | copy-done | bytes 3670040
  22.1 4.6 %grid_cells.1 = (bf16[1024,512]{1,0:T(8,128)(2,1)S(1)}, bf16[1024,512]{1,0:T(8,128)(2,1)S(1)}, bf16[1024,512]{1,0:T(8,128)(2,1)S(1)}) custom-call(bf16[1024,512]{1,0:T(8,128)(2,1)S(1)} %bitcast.18, bf16[9,512,512]{2,1,0:T(8,128)(2,1)S(1)} %copy-done, bf16[9,512,512]{2,1,0:T(8,128)(2,1)S(1)} %copy-done, bf16[9,512,512]{2,1,0:T(8,128)(2,1)S(1)} %copy-done, ...), custom_call_target="tpu_custom_call" | custom-call | flops 2147483648 | bytes 6291456 | tf_op jit(solution)/shard_map/grid_cells/pallas_call | solution.py:102
  26.7 1.0 copy-done.12
  27.7 1.0 copy-done.14
  28.7 1.3 dynamic_slice.3
  30.1 2.3 %copy-done.1 = bf16[9,512,512]{2,1,0:T(8,128)(2,1)S(1)} copy-done((bf16[9,512,512]{2,1,0:T(8,128)(2,1)S(1)}, bf16[9,512,512]{2,1,0:T(8,128)(2,1)}, u32[]{:S(2)}) %copy-start.1) | copy-done | bytes 4718616
  32.4 2.0 %copy-done.2 = bf16[7,512,512]{2,1,0:T(8,128)(2,1)S(1)} copy-done((bf16[7,512,512]{2,1,0:T(8,128)(2,1)S(1)}, bf16[7,512,512]{2,1,0:T(8,128)(2,1)}, u32[]{:S(2)}) %copy-start.2) | copy-done | bytes 3670040
  34.5 0.9 copy-done.8
  35.4 18.7 %encoder_edges.1 = (bf16[256,512]{1,0:T(8,128)(2,1)S(1)}, bf16[256,512]{1,0:T(8,128)(2,1)S(1)}, bf16[256,512]{1,0:T(8,128)(2,1)S(1)}) custom-call(s32[1]{0:T(128)} %bitcast.7.live, bf16[2048,512]{1,0:T(8,128)(2,1)S(1)} %bitcast.19, s32[8,1,256]{2,1,0:T(1,128)S(1)} %and_select_fusion.1.snd, s32[8,1,256]{2,1,0:T(1,128)S(1)} %bitcast.21, ...), custom_call_target="tpu_custom_call" | custom-call | flops 8388608000 | bytes 10485760 | tf_op jit(solution)/shard_map/encoder_edges/pallas_call | solution.py:157
  54.2 1.3 collective-permute-start.6
  55.5 1.8 %collective-permute-start.7 = (bf16[16,512]{1,0:T(8,128)(2,1)S(1)}, bf16[16,512]{1,0:T(8,128)(2,1)S(1)}, u32[]{:S(2)}, u32[]{:S(2)}) collective-permute-start(bf16[16,512]{1,0:T(8,128)(2,1)S(1)} %get-tuple-element.23), channel_id=1, source_target_pairs={{0,4},{1,5},{2,6},{3,7},{4,0},{5,1},{6,2},{7,3},{8,12},{9,13},{10,... | collective-permute-start | bytes 49160 | tf_op jit(solution)/shard_map/ppermute | solution.py:40
  57.3 2.2 %collective-permute-done.7 = bf16[16,512]{1,0:T(8,128)(2,1)S(1)} collective-permute-done((bf16[16,512]{1,0:T(8,128)(2,1)S(1)}, bf16[16,512]{1,0:T(8,128)(2,1)S(1)}, u32[]{:S(2)}, u32[]{:S(2)}) %collective-permute-start.7) | collective-permute-done | bytes 16416 | tf_op jit(solution)/shard_map/ppermute | solution.py:40
  59.6 1.6 %collective-permute-done.8 = bf16[16,512]{1,0:T(8,128)(2,1)S(1)} collective-permute-done((bf16[16,512]{1,0:T(8,128)(2,1)S(1)}, bf16[16,512]{1,0:T(8,128)(2,1)S(1)}, u32[]{:S(2)}, u32[]{:S(2)}) %collective-permute-start.8) | collective-permute-done | bytes 16416 | tf_op jit(solution)/shard_map/ppermute | solution.py:40
  61.1 0.4 collective-permute-start.10
  61.6 2.2 %collective-permute-start.11 = (bf16[64,512]{1,0:T(8,128)(2,1)S(1)}, bf16[64,512]{1,0:T(8,128)(2,1)S(1)}, u32[]{:S(2)}, u32[]{:S(2)}) collective-permute-start(bf16[64,512]{1,0:T(8,128)(2,1)S(1)} %pad_maximum_fusion.2), channel_id=1, source_target_pairs={{0,96},{1,97},{2,98},{3,99},{4,100},{5,101},{6,102},{7,103},{8,104... | collective-permute-start | bytes 196616 | tf_op jit(solution)/shard_map/ppermute | solution.py:40
  63.8 2.3 %collective-permute-done.9 = bf16[64,512]{1,0:T(8,128)(2,1)S(1)} collective-permute-done((bf16[64,512]{1,0:T(8,128)(2,1)S(1)}, bf16[64,512]{1,0:T(8,128)(2,1)S(1)}, u32[]{:S(2)}, u32[]{:S(2)}) %collective-permute-start.9) | collective-permute-done | bytes 65568 | tf_op jit(solution)/shard_map/ppermute | solution.py:40
  66.2 0.5 collective-permute-done.11
  67.0 2.5 %collective-permute-start.14 = (bf16[256,512]{1,0:T(8,128)(2,1)S(1)}, bf16[256,512]{1,0:T(8,128)(2,1)S(1)}, u32[]{:S(2)}, u32[]{:S(2)}) collective-permute-start(bf16[256,512]{1,0:T(8,128)(2,1)S(1)} %get-tuple-element.24), channel_id=1, source_target_pairs={{0,24},{1,25},{2,26},{3,27},{4,28},{5,29},{6,30},{7,31},{8,0},{9,1... | collective-permute-start | bytes 786440 | tf_op jit(solution)/shard_map/ppermute | solution.py:40
  69.5 7.0 %collective-permute-done.12 = bf16[256,512]{1,0:T(8,128)(2,1)S(1)} collective-permute-done((bf16[256,512]{1,0:T(8,128)(2,1)S(1)}, bf16[256,512]{1,0:T(8,128)(2,1)S(1)}, u32[]{:S(2)}, u32[]{:S(2)}) %collective-permute-start.12) | collective-permute-done | bytes 262176 | tf_op jit(solution)/shard_map/ppermute | solution.py:40
  76.6 0.4 collective-permute-done.14
  77.0 6.1 %collective-permute-start.15 = (bf16[1024,512]{1,0:T(8,128)(2,1)S(1)}, bf16[1024,512]{1,0:T(8,128)(2,1)}, u32[]{:S(2)}, u32[]{:S(2)}) collective-permute-start(bf16[1024,512]{1,0:T(8,128)(2,1)S(1)} %constant_dynamic-update-slice_fusion.7.mine), channel_id=1, source_target_pairs={{0,1},{1,0},{2,3},{3,2},{4,5},{5,4},{6,7},{7,6},{8,9},{9,8},{10,11... | collective-permute-start | bytes 3145736 | tf_op jit(solution)/shard_map/ppermute | solution.py:40
  83.3 4.8 %collective-permute-start.17 = (bf16[64,512]{1,0:T(8,128)(2,1)S(1)}, bf16[64,512]{1,0:T(8,128)(2,1)S(1)}, u32[]{:S(2)}, u32[]{:S(2)}) collective-permute-start(bf16[64,512]{1,0:T(8,128)(2,1)S(1)} %slice.34), channel_id=1, source_target_pairs={{0,120},{1,121},{2,122},{3,123},{4,124},{5,125},{6,126},{7,127},{8... | collective-permute-start | bytes 196616 | tf_op jit(solution)/shard_map/ppermute | solution.py:40
  88.1 0.5 fusion.5.snd
  88.6 1.8 %collective-permute-done.16 = bf16[64,512]{1,0:T(8,128)(2,1)S(1)} collective-permute-done((bf16[64,512]{1,0:T(8,128)(2,1)S(1)}, bf16[64,512]{1,0:T(8,128)(2,1)S(1)}, u32[]{:S(2)}, u32[]{:S(2)}) %collective-permute-start.16) | collective-permute-done | bytes 65568 | tf_op jit(solution)/shard_map/ppermute | solution.py:40
  90.3 1.0 collective-permute-start.18
  91.4 2.6 %collective-permute-done.18 = bf16[192,512]{1,0:T(8,128)(2,1)S(1)} collective-permute-done((bf16[192,512]{1,0:T(8,128)(2,1)S(1)}, bf16[192,512]{1,0:T(8,128)(2,1)S(1)}, u32[]{:S(2)}, u32[]{:S(2)}) %collective-permute-start.18) | collective-permute-done | bytes 196640 | tf_op jit(solution)/shard_map/ppermute | solution.py:40
  94.0 3.7 %collective-permute-done.19 = bf16[192,512]{1,0:T(8,128)(2,1)S(1)} collective-permute-done((bf16[192,512]{1,0:T(8,128)(2,1)S(1)}, bf16[192,512]{1,0:T(8,128)(2,1)S(1)}, u32[]{:S(2)}, u32[]{:S(2)}) %collective-permute-start.19) | collective-permute-done | bytes 196640 | tf_op jit(solution)/shard_map/ppermute | solution.py:40
  97.7 2.0 %copy-done.3 = bf16[7,512,512]{2,1,0:T(8,128)(2,1)S(1)} copy-done((bf16[7,512,512]{2,1,0:T(8,128)(2,1)S(1)}, bf16[7,512,512]{2,1,0:T(8,128)(2,1)}, u32[]{:S(2)}) %copy-start.3) | copy-done | bytes 3670040
  99.8 2.0 %copy-done.6 = bf16[7,512,512]{2,1,0:T(8,128)(2,1)S(1)} copy-done((bf16[7,512,512]{2,1,0:T(8,128)(2,1)S(1)}, bf16[7,512,512]{2,1,0:T(8,128)(2,1)}, u32[]{:S(2)}) %copy-start.6) | copy-done | bytes 3670040
  101.8 0.9 copy-done.17
  102.7 0.9 copy-done.19
  103.7 18.3 %mesh_edges.1 = bf16[256,512]{1,0:T(8,128)(2,1)S(1)} custom-call(bf16[2048,512]{1,0:T(8,128)(2,1)S(1)} %bitcast.22, s32[8,1,256]{2,1,0:T(1,128)S(1)} %fusion.5.snd, s32[8,1,256]{2,1,0:T(1,128)S(1)} %bitcast.23, bf16[1024,512]{1,0:T(8,128)(2,1)S(1)} %constant_dynamic-update-slice_fusion.7.mine, bf16[1024,512]{1,0:T(8,128)(2,1)} %collective-permute-done.15.theirs, ...), custom_call_target="tpu_custom_call" | custom-call | flops 9961472000 | bytes 10485760 | tf_op jit(solution)/shard_map/mesh_edges/pallas_call | solution.py:219
  122.1 4.9 %collective-permute-start.21 = (bf16[64,512]{1,0:T(8,128)(2,1)S(1)}, bf16[64,512]{1,0:T(8,128)(2,1)S(1)}, u32[]{:S(2)}, u32[]{:S(2)}) collective-permute-start(bf16[64,512]{1,0:T(8,128)(2,1)S(1)} %slice.38), channel_id=1, source_target_pairs={{0,120},{1,121},{2,122},{3,123},{4,124},{5,125},{6,126},{7,127},{8... | collective-permute-start | bytes 196616 | tf_op jit(solution)/shard_map/ppermute | solution.py:40
  127.1 1.5 collective-permute-done.20
  128.6 1.1 collective-permute-start.22
  129.8 2.6 %collective-permute-done.22 = bf16[192,512]{1,0:T(8,128)(2,1)S(1)} collective-permute-done((bf16[192,512]{1,0:T(8,128)(2,1)S(1)}, bf16[192,512]{1,0:T(8,128)(2,1)S(1)}, u32[]{:S(2)}, u32[]{:S(2)}) %collective-permute-start.22) | collective-permute-done | bytes 196640 | tf_op jit(solution)/shard_map/ppermute | solution.py:40
  132.4 3.7 %collective-permute-done.23 = bf16[192,512]{1,0:T(8,128)(2,1)S(1)} collective-permute-done((bf16[192,512]{1,0:T(8,128)(2,1)S(1)}, bf16[192,512]{1,0:T(8,128)(2,1)S(1)}, u32[]{:S(2)}, u32[]{:S(2)}) %collective-permute-start.23) | collective-permute-done | bytes 196640 | tf_op jit(solution)/shard_map/ppermute | solution.py:40
  136.1 13.7 %decoder_edges.1 = bf16[1024,512]{1,0:T(8,128)(2,1)} custom-call(bf16[3,4,256,512]{3,2,1,0:T(8,128)(2,1)S(1)} %copy-done.10, s32[3,4,1,256]{3,2,1,0:T(1,128)S(1)} %reshape.715.snd, bf16[768,512]{1,0:T(8,128)(2,1)S(1)} %constant_dynamic-update-slice_fusion.22.near, bf16[1024,512]{1,0:T(8,128)(2,1)S(1)} %copy-done.15, bf16[1024,512]{1,0:T(8,128)(2,1)S(1)} %copy-done.13, ...), custom_call_target="tpu_custom_call" | custom-call | flops 7864320000 | bytes 9437184 | tf_op jit(solution)/shard_map/decoder_edges/pallas_call | solution.py:262
  (89 shorter events, 1.1 us)
Async XLA Ops:
  0.8 10.8 %collective-permute-start.2 = (bf16[4,2,512]{2,1,0:T(2,128)(2,1)S(1)}, bf16[4,2,512]{2,1,0:T(2,128)(2,1)S(1)}, u32[]{:S(2)}, u32[]{:S(2)}) collective-permute-start(bf16[4,2,512]{2,1,0:T(2,128)(2,1)S(1)} %get-tuple-element.17), channel_id=1, source_target_pairs={{0,1},{1,2},{2,3},{3,4},{4,5},{5,6},{6,7},{7,0},{8,9},{9,10},{10,1... | collective-permute-start | bytes 24584 | tf_op jit(solution)/shard_map/ppermute | solution.py:40
  1.5 10.1 %collective-permute-start.3 = (bf16[4,2,512]{2,1,0:T(2,128)(2,1)S(1)}, bf16[4,2,512]{2,1,0:T(2,128)(2,1)S(1)}, u32[]{:S(2)}, u32[]{:S(2)}) collective-permute-start(bf16[4,2,512]{2,1,0:T(2,128)(2,1)S(1)} %get-tuple-element.18), channel_id=1, source_target_pairs={{0,7},{1,0},{2,1},{3,2},{4,3},{5,4},{6,5},{7,6},{8,15},{9,8},{10,9... | collective-permute-start | bytes 24584 | tf_op jit(solution)/shard_map/ppermute | solution.py:40
  3.8 26.3 %collective-permute-start = (bf16[2,256,512]{2,1,0:T(8,128)(2,1)}, bf16[2,256,512]{2,1,0:T(8,128)(2,1)}, u32[]{:S(2)}, u32[]{:S(2)}) collective-permute-start(bf16[2,256,512]{2,1,0:T(8,128)(2,1)} %get-tuple-element.20), channel_id=1, source_target_pairs={{0,8},{1,9},{2,10},{3,11},{4,12},{5,13},{6,14},{7,15},{8,16},{9,17... | collective-permute-start | bytes 1572872 | tf_op jit(solution)/shard_map/ppermute | solution.py:40
  5.5 24.6 %collective-permute-start.1 = (bf16[2,256,512]{2,1,0:T(8,128)(2,1)}, bf16[2,256,512]{2,1,0:T(8,128)(2,1)}, u32[]{:S(2)}, u32[]{:S(2)}) collective-permute-start(bf16[2,256,512]{2,1,0:T(8,128)(2,1)} %get-tuple-element.19), channel_id=1, source_target_pairs={{0,120},{1,121},{2,122},{3,123},{4,124},{5,125},{6,126},{7,127},{8... | collective-permute-start | bytes 1572872 | tf_op jit(solution)/shard_map/ppermute | solution.py:40
  11.6 18.4 %collective-permute-start.4 = (bf16[2,4,512]{2,1,0:T(4,128)(2,1)S(1)}, bf16[2,4,512]{2,1,0:T(4,128)(2,1)S(1)}, u32[]{:S(2)}, u32[]{:S(2)}) collective-permute-start(bf16[2,4,512]{2,1,0:T(4,128)(2,1)S(1)} %get-tuple-element.36), channel_id=1, source_target_pairs={{0,8},{1,9},{2,10},{3,11},{4,12},{5,13},{6,14},{7,15},{8,16},{9,17... | collective-permute-start | bytes 24584 | tf_op jit(solution)/shard_map/ppermute | solution.py:40
  11.7 18.3 %collective-permute-start.5 = (bf16[2,4,512]{2,1,0:T(4,128)(2,1)S(1)}, bf16[2,4,512]{2,1,0:T(4,128)(2,1)S(1)}, u32[]{:S(2)}, u32[]{:S(2)}) collective-permute-start(bf16[2,4,512]{2,1,0:T(4,128)(2,1)S(1)} %get-tuple-element.37), channel_id=1, source_target_pairs={{0,120},{1,121},{2,122},{3,123},{4,124},{5,125},{6,126},{7,127},{8... | collective-permute-start | bytes 24584 | tf_op jit(solution)/shard_map/ppermute | solution.py:40
  16.5 2.3 %copy-start = (bf16[9,512,512]{2,1,0:T(8,128)(2,1)S(1)}, bf16[9,512,512]{2,1,0:T(8,128)(2,1)}, u32[]{:S(2)}) copy-start(bf16[9,512,512]{2,1,0:T(8,128)(2,1)} %w6.3) | copy-start | bytes 14155780
  18.8 1.2 copy-start.4
  20.0 2.0 %copy-start.5 = (bf16[7,512,512]{2,1,0:T(8,128)(2,1)S(1)}, bf16[7,512,512]{2,1,0:T(8,128)(2,1)}, u32[]{:S(2)}) copy-start(bf16[7,512,512]{2,1,0:T(8,128)(2,1)} %w6.5) | copy-start | bytes 11010052
  22.1 8.0 %copy-start.7 = (bf16[1,1,2048,512]{3,2,1,0:T(8,128)(2,1)S(1)}, bf16[1,1,2048,512]{3,2,1,0:T(8,128)(2,1)}, u32[]{:S(2)}) copy-start(bf16[1,1,2048,512]{3,2,1,0:T(8,128)(2,1)} %param.16) | copy-start | bytes 6291460
  22.1 8.0 %copy-start.9 = (s32[1,1,2048]{2,1,0:T(1,128)S(1)}, s32[1,1,2048]{2,1,0:T(1,128)}, u32[]{:S(2)}) copy-start(s32[1,1,2048]{2,1,0:T(1,128)} %param.18) | copy-start | bytes 24580
  26.7 1.0 copy-start.12
  27.7 1.0 copy-start.14
  30.1 2.3 %copy-start.1 = (bf16[9,512,512]{2,1,0:T(8,128)(2,1)S(1)}, bf16[9,512,512]{2,1,0:T(8,128)(2,1)}, u32[]{:S(2)}) copy-start(bf16[9,512,512]{2,1,0:T(8,128)(2,1)} %w6.3) | copy-start | bytes 14155780
  32.4 2.0 %copy-start.2 = (bf16[7,512,512]{2,1,0:T(8,128)(2,1)S(1)}, bf16[7,512,512]{2,1,0:T(8,128)(2,1)}, u32[]{:S(2)}) copy-start(bf16[7,512,512]{2,1,0:T(8,128)(2,1)} %w6.4) | copy-start | bytes 11010052
  34.5 0.9 copy-start.8
  35.4 34.1 %copy-start.21 = (s32[1,1,2048]{2,1,0:T(1,128)S(1)}, s32[1,1,2048]{2,1,0:T(1,128)}, u32[]{:S(2)}) copy-start(s32[1,1,2048]{2,1,0:T(1,128)} %param.21) | copy-start | bytes 24580
  54.1 22.9 %copy-start.16 = (bf16[256,512]{1,0:T(8,128)(2,1)}, bf16[256,512]{1,0:T(8,128)(2,1)S(1)}, u32[]{:S(2)}) copy-start(bf16[256,512]{1,0:T(8,128)(2,1)S(1)} %get-tuple-element.14.mesh_ref) | copy-start | bytes 786436
  54.1 29.0 %copy-start.18 = (bf16[256,512]{1,0:T(8,128)(2,1)}, bf16[256,512]{1,0:T(8,128)(2,1)S(1)}, u32[]{:S(2)}) copy-start(bf16[256,512]{1,0:T(8,128)(2,1)S(1)} %get-tuple-element.13.recv) | copy-start | bytes 786436
  54.2 43.5 %copy-start.11 = (bf16[1,1,2048,512]{3,2,1,0:T(8,128)(2,1)S(1)}, bf16[1,1,2048,512]{3,2,1,0:T(8,128)(2,1)}, u32[]{:S(2)}) copy-start(bf16[1,1,2048,512]{3,2,1,0:T(8,128)(2,1)} %param.20) | copy-start | bytes 6291460
  54.2 43.5 %copy-start.20 = (s32[1,1,2048]{2,1,0:T(1,128)S(1)}, s32[1,1,2048]{2,1,0:T(1,128)}, u32[]{:S(2)}) copy-start(s32[1,1,2048]{2,1,0:T(1,128)} %param.22) | copy-start | bytes 24580
  54.2 3.1 %collective-permute-start.6 = (bf16[16,512]{1,0:T(8,128)(2,1)S(1)}, bf16[16,512]{1,0:T(8,128)(2,1)S(1)}, u32[]{:S(2)}, u32[]{:S(2)}) collective-permute-start(bf16[16,512]{1,0:T(8,128)(2,1)S(1)} %get-tuple-element.23), channel_id=1, source_target_pairs={{0,2},{1,3},{2,4},{3,5},{4,6},{5,7},{6,0},{7,1},{8,10},{9,11},{10,... | collective-permute-start | bytes 49160 | tf_op jit(solution)/shard_map/ppermute | solution.py:40
  55.5 4.1 %collective-permute-start.7 = (bf16[16,512]{1,0:T(8,128)(2,1)S(1)}, bf16[16,512]{1,0:T(8,128)(2,1)S(1)}, u32[]{:S(2)}, u32[]{:S(2)}) collective-permute-start(bf16[16,512]{1,0:T(8,128)(2,1)S(1)} %get-tuple-element.23), channel_id=1, source_target_pairs={{0,4},{1,5},{2,6},{3,7},{4,0},{5,1},{6,2},{7,3},{8,12},{9,13},{10,... | collective-permute-start | bytes 49160 | tf_op jit(solution)/shard_map/ppermute | solution.py:40
  57.3 3.8 %collective-permute-start.8 = (bf16[16,512]{1,0:T(8,128)(2,1)S(1)}, bf16[16,512]{1,0:T(8,128)(2,1)S(1)}, u32[]{:S(2)}, u32[]{:S(2)}) collective-permute-start(bf16[16,512]{1,0:T(8,128)(2,1)S(1)} %get-tuple-element.23), channel_id=1, source_target_pairs={{0,6},{1,7},{2,0},{3,1},{4,2},{5,3},{6,4},{7,5},{8,14},{9,15},{10,... | collective-permute-start | bytes 49160 | tf_op jit(solution)/shard_map/ppermute | solution.py:40
  61.1 5.0 %collective-permute-start.9 = (bf16[64,512]{1,0:T(8,128)(2,1)S(1)}, bf16[64,512]{1,0:T(8,128)(2,1)S(1)}, u32[]{:S(2)}, u32[]{:S(2)}) collective-permute-start(bf16[64,512]{1,0:T(8,128)(2,1)S(1)} %pad_maximum_fusion.2), channel_id=1, source_target_pairs={{0,32},{1,33},{2,34},{3,35},{4,36},{5,37},{6,38},{7,39},{8,40},{9,... | collective-permute-start | bytes 196616 | tf_op jit(solution)/shard_map/ppermute | solution.py:40
  61.1 5.0 %collective-permute-start.10 = (bf16[64,512]{1,0:T(8,128)(2,1)S(1)}, bf16[64,512]{1,0:T(8,128)(2,1)S(1)}, u32[]{:S(2)}, u32[]{:S(2)}) collective-permute-start(bf16[64,512]{1,0:T(8,128)(2,1)S(1)} %pad_maximum_fusion.2), channel_id=1, source_target_pairs={{0,64},{1,65},{2,66},{3,67},{4,68},{5,69},{6,70},{7,71},{8,72},{9,... | collective-permute-start | bytes 196616 | tf_op jit(solution)/shard_map/ppermute | solution.py:40
  61.6 5.2 %collective-permute-start.11 = (bf16[64,512]{1,0:T(8,128)(2,1)S(1)}, bf16[64,512]{1,0:T(8,128)(2,1)S(1)}, u32[]{:S(2)}, u32[]{:S(2)}) collective-permute-start(bf16[64,512]{1,0:T(8,128)(2,1)S(1)} %pad_maximum_fusion.2), channel_id=1, source_target_pairs={{0,96},{1,97},{2,98},{3,99},{4,100},{5,101},{6,102},{7,103},{8,104... | collective-permute-start | bytes 196616 | tf_op jit(solution)/shard_map/ppermute | solution.py:40
  66.7 9.8 %collective-permute-start.12 = (bf16[256,512]{1,0:T(8,128)(2,1)S(1)}, bf16[256,512]{1,0:T(8,128)(2,1)S(1)}, u32[]{:S(2)}, u32[]{:S(2)}) collective-permute-start(bf16[256,512]{1,0:T(8,128)(2,1)S(1)} %get-tuple-element.24), channel_id=1, source_target_pairs={{0,8},{1,9},{2,10},{3,11},{4,12},{5,13},{6,14},{7,15},{8,16},{9,17... | collective-permute-start | bytes 786440 | tf_op jit(solution)/shard_map/ppermute | solution.py:40
  66.8 9.7 %collective-permute-start.13 = (bf16[256,512]{1,0:T(8,128)(2,1)S(1)}, bf16[256,512]{1,0:T(8,128)(2,1)S(1)}, u32[]{:S(2)}, u32[]{:S(2)}) collective-permute-start(bf16[256,512]{1,0:T(8,128)(2,1)S(1)} %get-tuple-element.24), channel_id=1, source_target_pairs={{0,16},{1,17},{2,18},{3,19},{4,20},{5,21},{6,22},{7,23},{8,24},{9,... | collective-permute-start | bytes 786440 | tf_op jit(solution)/shard_map/ppermute | solution.py:40
  67.0 10.0 %collective-permute-start.14 = (bf16[256,512]{1,0:T(8,128)(2,1)S(1)}, bf16[256,512]{1,0:T(8,128)(2,1)S(1)}, u32[]{:S(2)}, u32[]{:S(2)}) collective-permute-start(bf16[256,512]{1,0:T(8,128)(2,1)S(1)} %get-tuple-element.24), channel_id=1, source_target_pairs={{0,24},{1,25},{2,26},{3,27},{4,28},{5,29},{6,30},{7,31},{8,0},{9,1... | collective-permute-start | bytes 786440 | tf_op jit(solution)/shard_map/ppermute | solution.py:40
  77.0 20.7 %collective-permute-start.15 = (bf16[1024,512]{1,0:T(8,128)(2,1)S(1)}, bf16[1024,512]{1,0:T(8,128)(2,1)}, u32[]{:S(2)}, u32[]{:S(2)}) collective-permute-start(bf16[1024,512]{1,0:T(8,128)(2,1)S(1)} %constant_dynamic-update-slice_fusion.7.mine), channel_id=1, source_target_pairs={{0,1},{1,0},{2,3},{3,2},{4,5},{5,4},{6,7},{7,6},{8,9},{9,8},{10,11... | collective-permute-start | bytes 3145736 | tf_op jit(solution)/shard_map/ppermute | solution.py:40
  83.2 7.1 %collective-permute-start.16 = (bf16[64,512]{1,0:T(8,128)(2,1)S(1)}, bf16[64,512]{1,0:T(8,128)(2,1)S(1)}, u32[]{:S(2)}, u32[]{:S(2)}) collective-permute-start(bf16[64,512]{1,0:T(8,128)(2,1)S(1)} %slice.34), channel_id=1, source_target_pairs={{0,8},{1,9},{2,10},{3,11},{4,12},{5,13},{6,14},{7,15},{8,16},{9,17... | collective-permute-start | bytes 196616 | tf_op jit(solution)/shard_map/ppermute | solution.py:40
  83.3 7.0 %collective-permute-start.17 = (bf16[64,512]{1,0:T(8,128)(2,1)S(1)}, bf16[64,512]{1,0:T(8,128)(2,1)S(1)}, u32[]{:S(2)}, u32[]{:S(2)}) collective-permute-start(bf16[64,512]{1,0:T(8,128)(2,1)S(1)} %slice.34), channel_id=1, source_target_pairs={{0,120},{1,121},{2,122},{3,123},{4,124},{5,125},{6,126},{7,127},{8... | collective-permute-start | bytes 196616 | tf_op jit(solution)/shard_map/ppermute | solution.py:40
  90.3 3.6 %collective-permute-start.18 = (bf16[192,512]{1,0:T(8,128)(2,1)S(1)}, bf16[192,512]{1,0:T(8,128)(2,1)S(1)}, u32[]{:S(2)}, u32[]{:S(2)}) collective-permute-start(bf16[192,512]{1,0:T(8,128)(2,1)S(1)} %pad_maximum_fusion), channel_id=1, source_target_pairs={{0,1},{1,2},{2,3},{3,4},{4,5},{5,6},{6,7},{7,0},{8,9},{9,10},{10,1... | collective-permute-start | bytes 589832 | tf_op jit(solution)/shard_map/ppermute | solution.py:40
  91.4 6.3 %collective-permute-start.19 = (bf16[192,512]{1,0:T(8,128)(2,1)S(1)}, bf16[192,512]{1,0:T(8,128)(2,1)S(1)}, u32[]{:S(2)}, u32[]{:S(2)}) collective-permute-start(bf16[192,512]{1,0:T(8,128)(2,1)S(1)} %pad_maximum_fusion), channel_id=1, source_target_pairs={{0,7},{1,0},{2,1},{3,2},{4,3},{5,4},{6,5},{7,6},{8,15},{9,8},{10,9... | collective-permute-start | bytes 589832 | tf_op jit(solution)/shard_map/ppermute | solution.py:40
  97.7 2.0 %copy-start.3 = (bf16[7,512,512]{2,1,0:T(8,128)(2,1)S(1)}, bf16[7,512,512]{2,1,0:T(8,128)(2,1)}, u32[]{:S(2)}) copy-start(bf16[7,512,512]{2,1,0:T(8,128)(2,1)} %w6.4) | copy-start | bytes 11010052
  99.7 2.0 %copy-start.6 = (bf16[7,512,512]{2,1,0:T(8,128)(2,1)S(1)}, bf16[7,512,512]{2,1,0:T(8,128)(2,1)}, u32[]{:S(2)}) copy-start(bf16[7,512,512]{2,1,0:T(8,128)(2,1)} %w6.5) | copy-start | bytes 11010052
  101.8 0.9 copy-start.17
  102.7 0.9 copy-start.19
  103.7 23.4 %copy-start.22 = (s32[3,4,256]{2,1,0:T(4,128)S(1)}, s32[3,4,256]{2,1,0:T(4,128)}, u32[]{:S(2)}) copy-start(s32[3,4,256]{2,1,0:T(4,128)} %param.24) | copy-start | bytes 36868
  103.7 32.4 %copy-start.10 = (bf16[3,4,256,512]{3,2,1,0:T(8,128)(2,1)S(1)}, bf16[3,4,256,512]{3,2,1,0:T(8,128)(2,1)}, u32[]{:S(2)}) copy-start(bf16[3,4,256,512]{3,2,1,0:T(8,128)(2,1)} %feat.1) | copy-start | bytes 9437188
  103.7 32.4 %copy-start.13 = (bf16[1024,512]{1,0:T(8,128)(2,1)S(1)}, bf16[1024,512]{1,0:T(8,128)(2,1)}, u32[]{:S(2)}) copy-start(bf16[1024,512]{1,0:T(8,128)(2,1)} %copy-done.12) | copy-start | bytes 3145732
  103.7 32.4 %copy-start.15 = (bf16[1024,512]{1,0:T(8,128)(2,1)S(1)}, bf16[1024,512]{1,0:T(8,128)(2,1)}, u32[]{:S(2)}) copy-start(bf16[1024,512]{1,0:T(8,128)(2,1)} %copy-done.14) | copy-start | bytes 3145732
  122.0 6.6 %collective-permute-start.20 = (bf16[64,512]{1,0:T(8,128)(2,1)S(1)}, bf16[64,512]{1,0:T(8,128)(2,1)S(1)}, u32[]{:S(2)}, u32[]{:S(2)}) collective-permute-start(bf16[64,512]{1,0:T(8,128)(2,1)S(1)} %slice.38), channel_id=1, source_target_pairs={{0,8},{1,9},{2,10},{3,11},{4,12},{5,13},{6,14},{7,15},{8,16},{9,17... | collective-permute-start | bytes 196616 | tf_op jit(solution)/shard_map/ppermute | solution.py:40
  122.1 6.5 %collective-permute-start.21 = (bf16[64,512]{1,0:T(8,128)(2,1)S(1)}, bf16[64,512]{1,0:T(8,128)(2,1)S(1)}, u32[]{:S(2)}, u32[]{:S(2)}) collective-permute-start(bf16[64,512]{1,0:T(8,128)(2,1)S(1)} %slice.38), channel_id=1, source_target_pairs={{0,120},{1,121},{2,122},{3,123},{4,124},{5,125},{6,126},{7,127},{8... | collective-permute-start | bytes 196616 | tf_op jit(solution)/shard_map/ppermute | solution.py:40
  128.6 3.7 %collective-permute-start.22 = (bf16[192,512]{1,0:T(8,128)(2,1)S(1)}, bf16[192,512]{1,0:T(8,128)(2,1)S(1)}, u32[]{:S(2)}, u32[]{:S(2)}) collective-permute-start(bf16[192,512]{1,0:T(8,128)(2,1)S(1)} %pad_maximum_fusion.1), channel_id=1, source_target_pairs={{0,1},{1,2},{2,3},{3,4},{4,5},{5,6},{6,7},{7,0},{8,9},{9,10},{10,1... | collective-permute-start | bytes 589832 | tf_op jit(solution)/shard_map/ppermute | solution.py:40
  129.8 6.3 %collective-permute-start.23 = (bf16[192,512]{1,0:T(8,128)(2,1)S(1)}, bf16[192,512]{1,0:T(8,128)(2,1)S(1)}, u32[]{:S(2)}, u32[]{:S(2)}) collective-permute-start(bf16[192,512]{1,0:T(8,128)(2,1)S(1)} %pad_maximum_fusion.1), channel_id=1, source_target_pairs={{0,7},{1,0},{2,1},{3,2},{4,3},{5,4},{6,5},{7,6},{8,15},{9,8},{10,9... | collective-permute-start | bytes 589832 | tf_op jit(solution)/shard_map/ppermute | solution.py:40

commit v2 on v1

v2 whole, which is shorter than its diff:
```python
import jax
import jax.numpy as jnp
from jax import lax
from jax.experimental import pallas as pl
from jax.experimental.pallas import tpu as pltpu
from jax.sharding import PartitionSpec as P

D = 512
AXES = ("band", "patch")
BANDS, PATCHES = 16, 8
EDGE_BLOCK = 1024
epsilon = 1e-05
F32, BF16 = jnp.float32, jnp.bfloat16


def split(device):
    band, patch = device // PATCHES, device % PATCHES
    return band // 4, band % 4, patch // 2, patch % 2


def torus(dy=0, dz=0, dx=0, dc=0):
    pairs = []
    for device in range(BANDS * PATCHES):
        y, z, x, c = split(device)
        band = (y + dy) % 4 * 4 + (z + dz) % 4
        patch = (x + dx) % 4 * 2 + (c + dc) % 2
        pairs.append((device, band * PATCHES + patch))
    return pairs


def plane(db, dp):
    return [
        (b * PATCHES + p, (b + db) % BANDS * PATCHES + (p + dp) % PATCHES)
        for b in range(BANDS)
        for p in range(PATCHES)
    ]


def send(values, pairs):
    return lax.ppermute(values, AXES, pairs)


def dot(a, b):
    return jnp.dot(a, b, preferred_element_type=F32)


def silu(v):
    half = 0.5 * v
    return half + half * jnp.tanh(half)


def layer_norm(v):
    centred = v - jnp.mean(v, axis=-1, keepdims=True)
    spread = jnp.mean(centred * centred, axis=-1, keepdims=True)
    return centred * lax.rsqrt(spread + epsilon)


def column(row):
    return jnp.transpose(jnp.broadcast_to(row, (8, row.shape[1])))[:, :1]


def pick_rows(row, count):
    col = column(row)
    lanes = lax.broadcasted_iota(jnp.int32, (row.shape[1], count), 1)
    return jnp.where(lanes == col, 1.0, 0.0).astype(BF16)


def add_rows(row, count):
    nodes = lax.broadcasted_iota(jnp.int32, (count, row.shape[1]), 0)
    return jnp.where(nodes == row, 1.0, 0.0).astype(BF16)


def weight(k):
    return pl.BlockSpec((None, D, D), lambda i: (k, 0, 0))


class Fetched:
    def __init__(self, source, target, sem):
        self.copy, self.target, self.ready = pltpu.make_async_copy(source, target, sem), target, False
        self.copy.start()

    def __call__(self):
        if not self.ready:
            self.copy.wait()
            self.ready = True
        return self.target


def whole(shape):
    return pl.BlockSpec(shape, lambda i: (0,) * len(shape))


def params(mb):
    return pltpu.CompilerParams(
        dimension_semantics=("arbitrary",), vmem_limit_bytes=mb << 20
    )


def cost(rows, nbytes):
    return pl.CostEstimate(flops=2 * rows * D * D, bytes_accessed=nbytes, transcendentals=0)


def grid_body(x_ref, w0, w7, w8, sent, nxt):
    x = x_ref[...]
    sent[...] = dot(x, w0[...]).astype(BF16)
    hidden = silu(dot(x, w7[...])).astype(BF16)
    nxt[...] = (x.astype(F32) + layer_norm(dot(hidden, w8[...]))).astype(BF16)


def grid_kernel(grid_flat, enc_w):
    blk = pl.BlockSpec((512, D), lambda i: (i, 0))
    return pl.pallas_call(
        grid_body,
        grid=(2,),
        in_specs=[blk, weight(0), weight(7), weight(8)],
        out_specs=[blk] * 2,
        out_shape=[jax.ShapeDtypeStruct((1024, D), BF16)] * 2,
        compiler_params=params(60),
        cost_estimate=cost(5000, 5 << 20),
        name="grid_cells",
    )(grid_flat, *[enc_w] * 3)


def lead_body(feat, cells, d1, w2, w4, before, self_part):
    g = cells[...]
    recv = dot(g, d1[...]).astype(BF16).astype(F32)
    self_part[...] = dot(g, w4[...])
    for k in range(3):
        before[k] = (dot(feat[k], w2[...]) + recv).astype(before.dtype)


def lead_kernel(feats, grid_next, dec_w):
    lat, lon = feats.shape[1:3]
    blk = pl.BlockSpec((lon, D), lambda i: (i, 0))
    edges = pl.BlockSpec((3, None, lon, D), lambda i: (0, i, 0, 0))
    return pl.pallas_call(
        lead_body,
        grid=(lat,),
        in_specs=[edges, blk, weight(1), weight(2), weight(4)],
        out_specs=[edges, blk],
        out_shape=[
            jax.ShapeDtypeStruct(feats.shape, BF16),
            jax.ShapeDtypeStruct(grid_next.shape, F32),
        ],
        compiler_params=params(60),
        cost_estimate=cost(8000, 10 << 20),
        name="decoder_lead",
    )(feats, grid_next, *[dec_w] * 3)


def edge_sum(before, hidden_weight, target):
    hidden = silu(before).astype(BF16)
    message = layer_norm(dot(hidden, hidden_weight)).astype(BF16)
    return dot(add_rows(target, 256), message)


def node_update(m, total, w4, w5, w6):
    hid = silu(dot(m, w4()[...]) + dot(total.astype(BF16), w5()[...])).astype(BF16)
    return (m.astype(F32) + layer_norm(dot(hid, w6()[...]))).astype(BF16)


def enc_body(
    live, snd, rcv, feat, own, top, bottom, side, mesh_ref, enc_w, proc_w,
    nxt, psend, precv,
    table, feat_v, rim_v, side_v, mesh_v, weights, sems,
):
    count = iter(range(sems.shape[0]))

    def fetch(source, target):
        return Fetched(source, target, sems.at[next(count)])

    steps = feat.shape[0] // EDGE_BLOCK
    w0 = fetch(enc_w.at[0], weights.at[0])
    rims = [fetch(top, rim_v.at[0]), fetch(bottom, rim_v.at[1])]
    sides = fetch(side, side_v)
    mesh = fetch(mesh_ref, mesh_v)
    w1 = fetch(enc_w.at[1], weights.at[1])
    mine = fetch(own, table.at[pl.ds(512, 1024)])
    w2, w3 = (fetch(enc_w.at[k], weights.at[k]) for k in (2, 3))
    feats = []
    for k in range(steps):
        rows = pl.ds(k * EDGE_BLOCK, EDGE_BLOCK)
        feats.append(fetch(feat.at[rows], feat_v.at[rows]))
    w4, w5, w6 = (fetch(enc_w.at[k], weights.at[k]) for k in (4, 5, 6))
    p0, p1 = (fetch(proc_w.at[k], weights.at[7 + k]) for k in (0, 1))

    table[2080:2176] = jnp.zeros((96, D), BF16)
    table[0:512] = dot(rims[0]()[...], w0()[...]).astype(BF16)
    table[1536:2048] = dot(rims[1]()[...], w0()[...]).astype(BF16)
    table[2048:2080] = dot(sides()[...], w0()[...]).astype(BF16)
    table[2176:2432] = dot(mesh()[...], w1()[...]).astype(BF16)
    mine()
    for ready in (w2, w3, *feats):
        ready()
    alive = live[lax.axis_index("band"), lax.axis_index("patch")] * 128

    def edges(k, total):
        receiver = rcv[k]
        ones = jnp.concatenate([pick_rows(snd[k], 2176), pick_rows(receiver, 256)], axis=1)
        x = feat_v[pl.ds(pl.multiple_of(k * EDGE_BLOCK, EDGE_BLOCK), EDGE_BLOCK)]
        before = dot(x, w2()[...]) + dot(ones, table[...])
        edge = k * EDGE_BLOCK + lax.broadcasted_iota(jnp.int32, (1, EDGE_BLOCK), 1)
        return total + edge_sum(before, w3()[...], jnp.where(edge < alive, receiver, -1))

    total = lax.fori_loop(0, steps, edges, jnp.zeros((256, D), F32))
    new = node_update(mesh()[...], total, w4, w5, w6)
    psend[...] = dot(new, p0()[...]).astype(BF16)
    nxt[...] = new
    precv[...] = dot(new, p1()[...]).astype(BF16)


SMEM = pl.BlockSpec(memory_space=pltpu.SMEM)
VMEM = pl.BlockSpec(memory_space=pltpu.VMEM)
HBM = pl.BlockSpec(memory_space=pl.ANY)


def edge_rows(index):
    return index.reshape(-1, 1, EDGE_BLOCK)


def enc_kernel(live, feats, senders, receivers, own, top, bottom, side, mesh_flat, enc_w, proc_w):
    return pl.pallas_call(
        enc_body,
        in_specs=[SMEM, VMEM, VMEM] + [HBM] * 8,
        out_specs=[VMEM] * 3,
        out_shape=[jax.ShapeDtypeStruct((256, D), BF16)] * 3,
        scratch_shapes=[
            pltpu.VMEM((2432, D), BF16),
            pltpu.VMEM(feats.shape, BF16),
            pltpu.VMEM((2, 512, D), BF16),
            pltpu.VMEM((32, D), BF16),
            pltpu.VMEM((256, D), BF16),
            pltpu.VMEM((9, D, D), BF16),
            pltpu.SemaphoreType.DMA((15 + feats.shape[0] // EDGE_BLOCK,)),
        ],
        compiler_params=pltpu.CompilerParams(vmem_limit_bytes=60 << 20),
        cost_estimate=cost(25000, 10 << 20),
        name="encoder_edges",
    )(
        live, edge_rows(senders), edge_rows(receivers),
        feats, own, top, bottom, side, mesh_flat, enc_w, proc_w,
    )


COARSE = ((0, 256), (256, 256), (512, 256), (768, 128), (896, 128))
NEAR = ((2048, 64), (2112, 256), (2368, 64), (2432, 192), (2624, 192))


def proc_body(*refs):
    snd, rcv, feat = refs[:3]
    pieces, (recv, mesh_ref, proc_w, dec_w) = refs[3:18], refs[18:22]
    dsend, table, feat_v, mesh_v, weights, sems = refs[22:]
    count = iter(range(sems.shape[0]))

    def fetch(source, target):
        return Fetched(source, target, sems.at[next(count)])

    places = COARSE + tuple((at + 1024, rows) for at, rows in COARSE) + NEAR
    first = [fetch(recv, table.at[pl.ds(2816, 256)])]
    for piece, (at, rows) in zip(pieces, places):
        first.append(fetch(piece.at[pl.ds(0, rows)], table.at[pl.ds(at, rows)]))
    first += [fetch(proc_w.at[k], weights.at[k - 2]) for k in (2, 3)]
    first.append(fetch(feat, feat_v))
    mesh = fetch(mesh_ref, mesh_v)
    w4, w5, w6 = (fetch(proc_w.at[k], weights.at[k - 2]) for k in (4, 5, 6))
    d0 = fetch(dec_w.at[0], weights.at[5])
    for ready in first:
        ready()

    def edges(k, total):
        receiver = rcv[k]
        ones = jnp.concatenate([pick_rows(snd[k], 2816), pick_rows(receiver, 256)], axis=1)
        x = feat_v[pl.ds(pl.multiple_of(k * EDGE_BLOCK, EDGE_BLOCK), EDGE_BLOCK)]
        before = dot(x, weights[0]) + dot(ones, table[...])
        return total + edge_sum(before, weights[1], receiver)

    total = lax.fori_loop(0, snd.shape[0], edges, jnp.zeros((256, D), F32))
    new = node_update(mesh()[...], total, w4, w5, w6)
    dsend[...] = dot(new, d0()[...]).astype(BF16)


def proc_kernel(feats, senders, receivers, pieces, recv, mesh_next, proc_w, dec_w):
    return pl.pallas_call(
        proc_body,
        in_specs=[VMEM, VMEM] + [HBM] * 20,
        out_specs=VMEM,
        out_shape=jax.ShapeDtypeStruct((256, D), BF16),
        scratch_shapes=[
            pltpu.VMEM((3072, D), BF16),
            pltpu.VMEM(feats.shape, BF16),
            pltpu.VMEM((256, D), BF16),
            pltpu.VMEM((6, D, D), BF16),
            pltpu.SemaphoreType.DMA((24,)),
        ],
        compiler_params=pltpu.CompilerParams(vmem_limit_bytes=60 << 20),
        cost_estimate=cost(25000, 10 << 20),
        name="mesh_edges",
    )(
        edge_rows(senders), edge_rows(receivers), feats, *pieces, recv, mesh_next, proc_w, dec_w,
    )


def dec_body(snd, lead, above, own, below, beside, across, cells, self_part, w3, w5, w6, out, near):
    @pl.when(pl.program_id(0) == 0)
    def _():
        near[0:64] = above[...]
        near[64:320] = own[...]
        near[320:384] = below[...]
        near[384:576] = beside[...]
        near[576:768] = across[...]

    n = cells.shape[0]
    ones = jnp.concatenate([pick_rows(snd[k], 768) for k in range(3)], axis=0)
    before = lead[...].astype(F32).reshape(3 * n, D) + dot(ones, near[...])
    hidden = silu(before).astype(BF16)
    message = layer_norm(dot(hidden, w3[...])).astype(BF16).astype(F32).reshape(3, n, D)
    summed = message[0] + message[1] + message[2]
    hid = silu(self_part[...] + dot(summed.astype(BF16), w5[...])).astype(BF16)
    out[...] = (cells[...].astype(F32) + layer_norm(dot(hid, w6[...]))).astype(BF16)


def dec_kernel(lead, senders, near, grid_next, self_part, dec_w):
    lat, lon = senders.shape[1:]
    blk = pl.BlockSpec((lon, D), lambda i: (i, 0))
    return pl.pallas_call(
        dec_body,
        grid=(lat,),
        in_specs=[
            pl.BlockSpec((3, None, 1, lon), lambda i: (0, i, 0, 0)),
            pl.BlockSpec((3, None, lon, D), lambda i: (0, i, 0, 0)),
        ]
        + [whole(rows.shape) for rows in near]
        + [blk, blk, weight(3), weight(5), weight(6)],
        out_specs=blk,
        out_shape=jax.ShapeDtypeStruct((lat * lon, D), BF16),
        scratch_shapes=[pltpu.VMEM((768, D), BF16)],
        compiler_params=params(60),
        cost_estimate=cost(15000, 9 << 20),
        name="decoder_edges",
    )(senders.reshape(3, lat, 1, lon), lead, *near, grid_next, self_part, *[dec_w] * 3)


SWAP = [(d, d ^ 1) for d in range(BANDS * PATCHES)]
CROSS = [
    (d, d // PATCHES * PATCHES + (d % PATCHES + (1 if d % 2 else -1)) % PATCHES)
    for d in range(BANDS * PATCHES)
]


def on_chip(col):
    return (col == 2) == (lax.axis_index("patch") % 2 == 0)


def near_index(sender):
    q, r = sender // 256, sender % 256
    row, col = q // 3, q % 3
    middle = jnp.where(row == 0, 0, jnp.where(row == 1, 64, 320))
    return jnp.where(col == 1, middle, jnp.where(on_chip(col), 384, 576) + row * 64) + r


def mesh_index(sender):
    device, node = jnp.maximum(sender - 2304, 0) // 16, sender % 16
    y, z, x, c = split(device)
    my_y, my_z, my_x, my_c = split(lax.axis_index("band") * PATCHES + lax.axis_index("patch"))
    kx, kz, kc = (my_x - x) % 4, (my_z - z) % 4, (my_c - c) % 2
    turn = jnp.where((kz == 1) & (my_z == 0), -1, 0) + jnp.where((kz == 3) & (my_z == 3), 1, 0)
    ky = (my_y - y + turn) % 4
    ky, kz = (jnp.where(k < 2, k, 5 - k) for k in (ky, kz))
    far = kc * 1024 + ky * 256 + kx * 64 + kz * 16 + node
    return jnp.where(sender < 2304, 2048 + near_index(jnp.minimum(sender, 2303)), far)


def mesh_rows(own, lead):
    rim, rows = own[:64], own[240:256]
    both = jnp.concatenate([rim, rows], axis=0)
    above, below = send(both, plane(1, 0)), send(both, plane(-1, 0))
    rows = jnp.concatenate([rows, above[64:], below[64:], send(rows, torus(dz=2))], axis=0)
    here = jnp.concatenate([rows] + [send(rows, torus(dx=k)) for k in (1, 2, 3)], axis=0)
    col = jnp.concatenate([above[:64], rim, below[:64]], axis=0)
    beside, across = send(col, SWAP), send(col, CROSS)
    here, given = lax.optimization_barrier((here, lead[0]))
    lead = lead[1](given)
    ahead, behind = send(here, torus(dy=1)), send(here, torus(dy=-1))
    ahead, behind, lead = lax.optimization_barrier((ahead, behind, lead))
    far = send(ahead[:128], torus(dy=1)), send(behind[128:], torus(dy=-1))
    coarse = [here, ahead, behind, *far]
    return coarse + [send(v, SWAP) for v in coarse] + [above, own, below, beside, across], lead


def near_rows(own):
    rim = own[:64]
    above, below = send(rim, plane(1, 0)), send(rim, plane(-1, 0))
    col = jnp.concatenate([above, rim, below], axis=0)
    return above, own, below, send(col, SWAP), send(col, CROSS)


def shards(
    grid_state,
    mesh_state,
    g2m_features,
    g2m_sender,
    g2m_receiver,
    g2m_blocks,
    proc_features,
    proc_sender,
    proc_receiver,
    dec_features,
    dec_sender,
    enc_weights,
    proc_weights,
    dec_weights,
):
    cells = grid_state.reshape(1024, D)
    nodes = mesh_state.reshape(256, D)
    top = send(grid_state[2:4], plane(1, 0))
    bottom = send(grid_state[0:2], plane(-1, 0))
    first = jnp.concatenate([top[:, :2], grid_state[:, :2], bottom[:, :2]], axis=0)
    final = jnp.concatenate([top[:, 254:], grid_state[:, 254:], bottom[:, 254:]], axis=0)
    west, east = send(final, plane(0, 1)), send(first, plane(0, -1))
    side = jnp.concatenate([west, east], axis=1).reshape(32, D)
    s = g2m_sender.reshape(-1)
    i, j = s // 260, s % 260
    inner = (j >= 2) & (j < 258)
    enc_sender = jnp.where(
        inner, i * 256 + j - 2, 2048 + i * 4 + jnp.where(j < 2, j, j - 256)
    )
    proc_sender, proc_receiver = proc_sender.reshape(-1), proc_receiver.reshape(-1)

    grid_send, grid_next = grid_kernel(cells, enc_weights)
    mesh_next, proc_send, proc_recv = enc_kernel(
        g2m_blocks, g2m_features.reshape(-1, D), enc_sender, g2m_receiver.reshape(-1),
        grid_send, top.reshape(512, D), bottom.reshape(512, D), side, nodes,
        enc_weights, proc_weights,
    )
    pieces, (lead, self_part) = mesh_rows(
        proc_send, (grid_next, lambda g: lead_kernel(dec_features, g, dec_weights))
    )
    dec_send = proc_kernel(
        proc_features.reshape(-1, D), mesh_index(proc_sender), proc_receiver, pieces, proc_recv,
        mesh_next, proc_weights, dec_weights,
    )
    out = dec_kernel(
        lead, near_index(dec_sender), near_rows(dec_send), grid_next, self_part, dec_weights
    )
    return out.reshape(grid_state.shape)


def solution(mesh):
    placed = (
        P("band", "patch", None),
        P("band", "patch", None, None),
        P("band", "patch", None, None),
        P("band", "patch", None),
        P("band", "patch", None),
        P(),
        P("band", "patch", None, None),
        P("band", "patch", None),
        P("band", "patch", None),
        P(None, "band", "patch", None),
        P(None, "band", "patch"),
        P(),
        P(),
        P(),
    )
    return jax.shard_map(
        shards, mesh=mesh, in_specs=placed, out_specs=P("band", "patch", None), check_vma=False
    )
```

time: 151 us -> 128 us (0.85)
  local copies, waits for them, and re-layouts: 23.5 us -> 8.1 us
  waiting for transfers between devices: 29.8 us -> 19 us
  Pallas kernels: 55.3 us -> 59 us
    unnamed x62 -> x52, local copies, waits for them, and re-layouts: 19.1 us -> 2.27 us
    ppermute x24 -> x25, waiting for transfers between devices: 29.8 us -> 19 us  [send(): return lax.ppermute(values, AXES, pairs)]
    pallas_call x4 -> x5, Pallas kernels: 55.3 us -> 59 us  [the longest x1 17.2 us: proc_kernel(): pl.pallas_call(proc_body, in_specs=[VMEM, VMEM] + [HBM] * 20, out_specs=V...]
    slice x1 -> x15, local copies, waits for them, and re-layouts: 0.79 us -> 2.44 us  [the longest x2 1.57 us: mesh_rows(): rim, rows = (own[:64], own[240:256])]
    ppermute x24 -> x25, starting transfers between devices: 38.5 us -> 37.4 us  [send(): return lax.ppermute(values, AXES, pairs)]
  transfers between devices with their start and end apart: 24 -> 25, of which waited for: 12 -> 9; matrix products, arithmetic and copies ran while one was open for 4% -> 4% of each run, Pallas kernels for 3% -> 9%
where the time goes in v2:
time: 128 us; the launch traced here: 127 us
  Pallas kernels  59 us (46%)
  starting transfers between devices  37.4 us (29%)
  waiting for transfers between devices  19 us (15%)
  local copies, waits for them, and re-layouts  8.1 us (6%)
  other arithmetic  3.39 us (3%)
    ppermute x25, starting transfers between devices, send(): return lax.ppermute(values, AXES, pairs)  37.4 us
    ppermute x25, waiting for transfers between devices, send(): return lax.ppermute(values, AXES, pairs)  19 us
    pallas_call x1, Pallas kernels, proc_kernel(): pl.pallas_call(proc_body, in_specs=[VMEM, VMEM] + [HBM] * 20, out_specs=V...  17.2 us
    pallas_call x1, Pallas kernels, enc_kernel(): pl.pallas_call(enc_body, in_specs=[SMEM, VMEM, VMEM] + [HBM] * 8, out_spe...  16.5 us
    pallas_call x1, Pallas kernels, dec_kernel(): pl.pallas_call(dec_body, grid=(lat,), in_specs=[pl.BlockSpec((3, None, 1,...  13.3 us
    pallas_call x1, Pallas kernels, lead_kernel(): pl.pallas_call(lead_body, grid=(lat,), in_specs=[edges, blk, weight(1), w...  7.08 us
    pallas_call x1, Pallas kernels, grid_kernel(): pl.pallas_call(grid_body, grid=(2,), in_specs=[blk, weight(0), weight(7),...  4.92 us
  transfers between devices with their start and end apart: 25, of which 9 were waited for; matrix products, arithmetic and copies ran while one was open for 4% of the time, Pallas kernels for 9%

profile of v2, /device:TPU:7, one launch (start us, length us, event | category | flops | bytes accessed | tf_op | source)
XLA Modules:
  0.0 127.3 jit_solution(8383953947923142125)
XLA Ops:
  0.0 1.3 %fusion.24 = (bf16[2,256,512]{2,1,0:T(8,128)(2,1)S(1)}, bf16[2,256,512]{2,1,0:T(8,128)(2,1)S(1)}) fusion(bf16[4,256,512]{2,1,0:T(8,128)(2,1)} %param.14), kind=kLoop, calls=%fused_computation.103 | loop fusion | bytes 2097152 | tf_op jit(solution)/shard_map/slice | solution.py:416
  1.3 1.7 %collective-permute-start = (bf16[2,256,512]{2,1,0:T(8,128)(2,1)S(1)}, bf16[2,256,512]{2,1,0:T(8,128)(2,1)S(1)}, u32[]{:S(2)}, u32[]{:S(2)}) collective-permute-start(bf16[2,256,512]{2,1,0:T(8,128)(2,1)S(1)} %get-tuple-element.34), channel_id=1, source_target_pairs={{0,8},{1,9},{2,10},{3,11},{4,12},{5,13},{6,14},{7,15},{8,16},{9,17... | collective-permute-start | bytes 1572872 | tf_op jit(solution)/shard_map/ppermute | solution.py:40
  3.0 4.7 %collective-permute-start.1 = (bf16[2,256,512]{2,1,0:T(8,128)(2,1)S(1)}, bf16[2,256,512]{2,1,0:T(8,128)(2,1)S(1)}, u32[]{:S(2)}, u32[]{:S(2)}) collective-permute-start(bf16[2,256,512]{2,1,0:T(8,128)(2,1)S(1)} %get-tuple-element.33), channel_id=1, source_target_pairs={{0,120},{1,121},{2,122},{3,123},{4,124},{5,125},{6,126},{7,127},{8... | collective-permute-start | bytes 1572872 | tf_op jit(solution)/shard_map/ppermute | solution.py:40
  7.7 0.7 broadcast_divide_fusion
  8.4 0.7 sign_compare_fusion.2
  9.1 0.8 fusion.23
  9.9 4.9 %grid_cells.1 = (bf16[1024,512]{1,0:T(8,128)(2,1)}, bf16[1024,512]{1,0:T(8,128)(2,1)}) custom-call(bf16[1024,512]{1,0:T(8,128)(2,1)} %bitcast.13, bf16[9,512,512]{2,1,0:T(8,128)(2,1)} %enc_w.1, bf16[9,512,512]{2,1,0:T(8,128)(2,1)} %enc_w.1, bf16[9,512,512]{2,1,0:T(8,128)(2,1)} %enc_w.1), custom_call_target="tpu_custom_call" | custom-call | flops 2621440000 | bytes 5242880 | tf_op jit(solution)/shard_map/grid_cells/pallas_call | solution.py:112
  14.9 4.4 %collective-permute-done = bf16[2,256,512]{2,1,0:T(8,128)(2,1)S(1)} collective-permute-done((bf16[2,256,512]{2,1,0:T(8,128)(2,1)S(1)}, bf16[2,256,512]{2,1,0:T(8,128)(2,1)S(1)}, u32[]{:S(2)}, u32[]{:S(2)}) %collective-permute-start) | collective-permute-done | bytes 524320 | tf_op jit(solution)/shard_map/ppermute | solution.py:40
  19.3 1.3 %collective-permute-start.2 = (bf16[8,2,512]{2,0,1:T(8,128)(2,1)S(1)}, bf16[8,2,512]{2,0,1:T(8,128)(2,1)S(1)}, u32[]{:S(2)}, u32[]{:S(2)}) collective-permute-start(bf16[8,2,512]{2,0,1:T(8,128)(2,1)S(1)} %pad_maximum_fusion.5), channel_id=1, source_target_pairs={{0,1},{1,2},{2,3},{3,4},{4,5},{5,6},{6,7},{7,0},{8,9},{9,10},{10,1... | collective-permute-start | bytes 49160 | tf_op jit(solution)/shard_map/ppermute | solution.py:40
  20.7 0.7 and_select_fusion.19.snd
  21.4 0.7 copy.32.live
  22.0 3.0 %collective-permute-done.3 = bf16[8,2,512]{2,0,1:T(8,128)(2,1)S(1)} collective-permute-done((bf16[8,2,512]{2,0,1:T(8,128)(2,1)S(1)}, bf16[8,2,512]{2,0,1:T(8,128)(2,1)S(1)}, u32[]{:S(2)}, u32[]{:S(2)}) %collective-permute-start.3) | collective-permute-done | bytes 16416 | tf_op jit(solution)/shard_map/ppermute | solution.py:40
  25.1 0.6 reshape.789.side
  25.7 16.5 %encoder_edges.1 = (bf16[256,512]{1,0:T(8,128)(2,1)}, bf16[256,512]{1,0:T(8,128)(2,1)}, bf16[256,512]{1,0:T(8,128)(2,1)}) custom-call(s32[16,8]{1,0:T(8,128)} %copy.32.live, s32[2,1,1024]{2,1,0:T(1,128)} %and_select_fusion.19.snd, s32[2,1,1024]{2,1,0:T(1,128)} %bitcast.23, bf16[2048,512]{1,0:T(8,128)(2,1)} %bitcast.20, ...), custom_call_target="tpu_custom_call" | custom-call | flops 13107200000 | bytes 10485760 | tf_op jit(solution)/shard_map/encoder_edges/pallas_call | solution.py:222
  42.2 0.7 fusion.27
  43.0 0.8 slice.60
  43.9 4.9 %collective-permute-start.5 = (bf16[80,512]{1,0:T(8,128)(2,1)S(1)}, bf16[80,512]{1,0:T(8,128)(2,1)S(1)}, u32[]{:S(2)}, u32[]{:S(2)}) collective-permute-start(bf16[80,512]{1,0:T(8,128)(2,1)S(1)} %pad_maximum_fusion.2), channel_id=1, source_target_pairs={{0,120},{1,121},{2,122},{3,123},{4,124},{5,125},{6,126},{7,127},{8... | collective-permute-start | bytes 245768 | tf_op jit(solution)/shard_map/ppermute | solution.py:40
  48.8 1.8 %collective-permute-done.4.refs_13_ = bf16[80,512]{1,0:T(8,128)(2,1)S(1)} collective-permute-done((bf16[80,512]{1,0:T(8,128)(2,1)S(1)}, bf16[80,512]{1,0:T(8,128)(2,1)S(1)}, u32[]{:S(2)}, u32[]{:S(2)}) %collective-permute-start.4) | collective-permute-done | bytes 81952 | tf_op jit(solution)/shard_map/ppermute | solution.py:40
  50.6 2.3 %collective-permute-done.6 = bf16[16,512]{1,0:T(8,128)(2,1)S(1)} collective-permute-done((bf16[16,512]{1,0:T(8,128)(2,1)S(1)}, bf16[16,512]{1,0:T(8,128)(2,1)S(1)}, u32[]{:S(2)}, u32[]{:S(2)}) %collective-permute-start.6) | collective-permute-done | bytes 16416 | tf_op jit(solution)/shard_map/ppermute | solution.py:40
  52.9 2.2 %collective-permute-start.8 = (bf16[64,512]{1,0:T(8,128)(2,1)S(1)}, bf16[64,512]{1,0:T(8,128)(2,1)S(1)}, u32[]{:S(2)}, u32[]{:S(2)}) collective-permute-start(bf16[64,512]{1,0:T(8,128)(2,1)S(1)} %pad_maximum_fusion.3), channel_id=1, source_target_pairs={{0,4},{1,5},{2,6},{3,7},{4,0},{5,1},{6,2},{7,3},{8,12},{9,13},{10,... | collective-permute-start | bytes 196616 | tf_op jit(solution)/shard_map/ppermute | solution.py:40
  55.1 1.2 collective-permute-start.19
  56.3 2.9 %collective-permute-start.20 = (bf16[192,512]{1,0:T(8,128)(2,1)S(1)}, bf16[192,512]{1,0:T(8,128)(2,1)S(1)}, u32[]{:S(2)}, u32[]{:S(2)}) collective-permute-start(bf16[192,512]{1,0:T(8,128)(2,1)S(1)} %pad_maximum_fusion), channel_id=1, source_target_pairs={{0,7},{1,2},{2,1},{3,4},{4,3},{5,6},{6,5},{7,0},{8,15},{9,10},{10,... | collective-permute-start | bytes 589832 | tf_op jit(solution)/shard_map/ppermute | solution.py:40
  59.2 0.4 collective-permute-done.9
  59.8 2.7 %collective-permute-start.11 = (bf16[256,512]{1,0:T(8,128)(2,1)S(1)}, bf16[256,512]{1,0:T(8,128)(2,1)S(1)}, u32[]{:S(2)}, u32[]{:S(2)}) collective-permute-start(bf16[256,512]{1,0:T(8,128)(2,1)S(1)} %constant_dynamic-update-slice_fusion.refs_3_), channel_id=1, source_target_pairs={{0,96},{1,97},{2,98},{3,99},{4,100},{5,101},{6,102},{7,103},{8,104... | collective-permute-start | bytes 786440 | tf_op jit(solution)/shard_map/ppermute | solution.py:40
  62.4 7.1 %decoder_lead.1 = (bf16[3,4,256,512]{3,2,1,0:T(8,128)(2,1)}, f32[1024,512]{1,0:T(8,128)}) custom-call(bf16[3,4,256,512]{3,2,1,0:T(8,128)(2,1)} %feat.1, bf16[1024,512]{1,0:T(8,128)(2,1)} %get-tuple-element.22.cells, bf16[7,512,512]{2,1,0:T(8,128)(2,1)} %w6.1, bf16[7,512,512]{2,1,0:T(8,128)(2,1)} %w6.1, bf16[7,512,512]{2,1,0:T(8,128)(2,1)} %w6.1), custom_call_target="tpu_custom_call" | custom-call | flops 4194304000 | bytes 10485760 | tf_op jit(solution)/shard_map/decoder_lead/pallas_call | solution.py:136
  69.6 0.3 collective-permute-start.12
  69.8 2.7 %collective-permute-start.13 = (bf16[128,512]{1,0:T(8,128)(2,1)S(1)}, bf16[128,512]{1,0:T(8,128)(2,1)S(1)}, u32[]{:S(2)}, u32[]{:S(2)}) collective-permute-start(bf16[128,512]{1,0:T(8,128)(2,1)S(1)} %slice.64), channel_id=1, source_target_pairs={{0,96},{1,97},{2,98},{3,99},{4,100},{5,101},{6,102},{7,103},{8,104... | collective-permute-start | bytes 393224 | tf_op jit(solution)/shard_map/ppermute | solution.py:40
  72.6 3.1 %collective-permute-start.14 = (bf16[256,512]{1,0:T(8,128)(2,1)S(1)}, bf16[256,512]{1,0:T(8,128)(2,1)S(1)}, u32[]{:S(2)}, u32[]{:S(2)}) collective-permute-start(bf16[256,512]{1,0:T(8,128)(2,1)S(1)} %constant_dynamic-update-slice_fusion.refs_3_), channel_id=1, source_target_pairs={{0,1},{1,0},{2,3},{3,2},{4,5},{5,4},{6,7},{7,6},{8,9},{9,8},{10,11... | collective-permute-start | bytes 786440 | tf_op jit(solution)/shard_map/ppermute | solution.py:40
  75.7 0.1 collective-permute-start.15
  75.8 0.4 collective-permute-start.16
  76.2 2.3 %collective-permute-start.17 = (bf16[128,512]{1,0:T(8,128)(2,1)S(1)}, bf16[128,512]{1,0:T(8,128)(2,1)S(1)}, u32[]{:S(2)}, u32[]{:S(2)}) collective-permute-start(bf16[128,512]{1,0:T(8,128)(2,1)S(1)} %collective-permute-done.12.refs_6_), channel_id=1, source_target_pairs={{0,1},{1,0},{2,3},{3,2},{4,5},{5,4},{6,7},{7,6},{8,9},{9,8},{10,11... | collective-permute-start | bytes 393224 | tf_op jit(solution)/shard_map/ppermute | solution.py:40
  78.5 0.1 collective-permute-start.18
  78.6 1.1 compare_select_fusion.17.refs_0_
  79.8 0.1 collective-permute-done.18.refs_12_
  80.0 0.5 copy-done.12
  80.6 0.1 copy-done.13
  80.7 0.1 copy-done.14
  80.8 17.2 %mesh_edges.1.own = bf16[256,512]{1,0:T(8,128)(2,1)} custom-call(s32[2,1,1024]{2,1,0:T(1,128)} %compare_select_fusion.17.refs_0_, s32[2,1,1024]{2,1,0:T(1,128)} %bitcast.24, bf16[2048,512]{1,0:T(8,128)(2,1)} %bitcast.21, bf16[256,512]{1,0:T(8,128)(2,1)} %copy-done.9, bf16[256,512]{1,0:T(8,128)(2,1)} %copy-done.2, bf16[256,512]{1,0:T(8,128)(2,1)} %copy-done.3, ...), custom_call_target="tpu_custom_call" | custom-call | flops 13107200000 | bytes 10485760 | tf_op jit(solution)/shard_map/mesh_edges/pallas_call | solution.py:283
  98.1 0.8 slice.76
  98.9 4.8 %collective-permute-start.22 = (bf16[64,512]{1,0:T(8,128)(2,1)S(1)}, bf16[64,512]{1,0:T(8,128)(2,1)S(1)}, u32[]{:S(2)}, u32[]{:S(2)}) collective-permute-start(bf16[64,512]{1,0:T(8,128)(2,1)S(1)} %slice.76), channel_id=1, source_target_pairs={{0,120},{1,121},{2,122},{3,123},{4,124},{5,125},{6,126},{7,127},{8... | collective-permute-start | bytes 196616 | tf_op jit(solution)/shard_map/ppermute | solution.py:40
  103.7 1.6 %collective-permute-done.21.above = bf16[64,512]{1,0:T(8,128)(2,1)S(1)} collective-permute-done((bf16[64,512]{1,0:T(8,128)(2,1)S(1)}, bf16[64,512]{1,0:T(8,128)(2,1)S(1)}, u32[]{:S(2)}, u32[]{:S(2)}) %collective-permute-start.21) | collective-permute-done | bytes 65568 | tf_op jit(solution)/shard_map/ppermute | solution.py:40
  105.4 1.6 %collective-permute-start.23 = (bf16[192,512]{1,0:T(8,128)(2,1)S(1)}, bf16[192,512]{1,0:T(8,128)(2,1)S(1)}, u32[]{:S(2)}, u32[]{:S(2)}) collective-permute-start(bf16[192,512]{1,0:T(8,128)(2,1)S(1)} %pad_maximum_fusion.1), channel_id=1, source_target_pairs={{0,1},{1,0},{2,3},{3,2},{4,5},{5,4},{6,7},{7,6},{8,9},{9,8},{10,11... | collective-permute-start | bytes 589832 | tf_op jit(solution)/shard_map/ppermute | solution.py:40
  107.0 0.3 collective-permute-start.24
  107.3 0.6 reshape.784.snd
  107.9 0.1 collective-permute-done.23.beside
  108.1 5.2 %collective-permute-done.24.across = bf16[192,512]{1,0:T(8,128)(2,1)S(1)} collective-permute-done((bf16[192,512]{1,0:T(8,128)(2,1)S(1)}, bf16[192,512]{1,0:T(8,128)(2,1)S(1)}, u32[]{:S(2)}, u32[]{:S(2)}) %collective-permute-start.24) | collective-permute-done | bytes 196640 | tf_op jit(solution)/shard_map/ppermute | solution.py:40
  113.3 0.7 copy-done.18
  114.0 13.3 %decoder_edges.1 = bf16[1024,512]{1,0:T(8,128)(2,1)} custom-call(s32[3,4,1,256]{3,2,1,0:T(1,128)} %reshape.784.snd, bf16[3,4,256,512]{3,2,1,0:T(8,128)(2,1)} %get-tuple-element.25.lead, bf16[64,512]{1,0:T(8,128)(2,1)} %copy-done.4, bf16[256,512]{1,0:T(8,128)(2,1)} %mesh_edges.1.own, bf16[64,512]{1,0:T(8,128)(2,1)} %copy-done.5, bf16[192,512]{1,0:T(8,128)(2,1)} %copy-done.17, ...), custom_call_target="tpu_custom_call" | custom-call | flops 7864320000 | bytes 9437184 | tf_op jit(solution)/shard_map/decoder_edges/pallas_call | solution.py:325
  (92 shorter events, 0.7 us)
Async XLA Ops:
  1.3 17.9 %collective-permute-start = (bf16[2,256,512]{2,1,0:T(8,128)(2,1)S(1)}, bf16[2,256,512]{2,1,0:T(8,128)(2,1)S(1)}, u32[]{:S(2)}, u32[]{:S(2)}) collective-permute-start(bf16[2,256,512]{2,1,0:T(8,128)(2,1)S(1)} %get-tuple-element.34), channel_id=1, source_target_pairs={{0,8},{1,9},{2,10},{3,11},{4,12},{5,13},{6,14},{7,15},{8,16},{9,17... | collective-permute-start | bytes 1572872 | tf_op jit(solution)/shard_map/ppermute | solution.py:40
  3.0 16.3 %collective-permute-start.1 = (bf16[2,256,512]{2,1,0:T(8,128)(2,1)S(1)}, bf16[2,256,512]{2,1,0:T(8,128)(2,1)S(1)}, u32[]{:S(2)}, u32[]{:S(2)}) collective-permute-start(bf16[2,256,512]{2,1,0:T(8,128)(2,1)S(1)} %get-tuple-element.33), channel_id=1, source_target_pairs={{0,120},{1,121},{2,122},{3,123},{4,124},{5,125},{6,126},{7,127},{8... | collective-permute-start | bytes 1572872 | tf_op jit(solution)/shard_map/ppermute | solution.py:40
  9.9 11.4 %copy-start.8 = (s32[16,8]{0,1:T(8,128)S(1)}, s32[16,8]{0,1:T(8,128)}, u32[]{:S(2)}) copy-start(s32[16,8]{0,1:T(8,128)} %param.19) | copy-start | bytes 1540
  19.2 6.5 %copy-start.10 = (bf16[2,256,512]{2,1,0:T(8,128)(2,1)}, bf16[2,256,512]{2,1,0:T(8,128)(2,1)S(1)}, u32[]{:S(2)}) copy-start(bf16[2,256,512]{2,1,0:T(8,128)(2,1)S(1)} %collective-permute-done) | copy-start | bytes 1572868
  19.3 6.5 %copy-start.11 = (bf16[2,256,512]{2,1,0:T(8,128)(2,1)}, bf16[2,256,512]{2,1,0:T(8,128)(2,1)S(1)}, u32[]{:S(2)}) copy-start(bf16[2,256,512]{2,1,0:T(8,128)(2,1)S(1)} %collective-permute-done.1) | copy-start | bytes 1572868
  19.3 2.7 %collective-permute-start.2 = (bf16[8,2,512]{2,0,1:T(8,128)(2,1)S(1)}, bf16[8,2,512]{2,0,1:T(8,128)(2,1)S(1)}, u32[]{:S(2)}, u32[]{:S(2)}) collective-permute-start(bf16[8,2,512]{2,0,1:T(8,128)(2,1)S(1)} %pad_maximum_fusion.5), channel_id=1, source_target_pairs={{0,1},{1,2},{2,3},{3,4},{4,5},{5,6},{6,7},{7,0},{8,9},{9,10},{10,1... | collective-permute-start | bytes 49160 | tf_op jit(solution)/shard_map/ppermute | solution.py:40
  20.7 4.4 %collective-permute-start.3 = (bf16[8,2,512]{2,0,1:T(8,128)(2,1)S(1)}, bf16[8,2,512]{2,0,1:T(8,128)(2,1)S(1)}, u32[]{:S(2)}, u32[]{:S(2)}) collective-permute-start(bf16[8,2,512]{2,0,1:T(8,128)(2,1)S(1)} %pad_maximum_fusion.6), channel_id=1, source_target_pairs={{0,7},{1,0},{2,1},{3,2},{4,3},{5,4},{6,5},{7,6},{8,15},{9,8},{10,9... | collective-permute-start | bytes 49160 | tf_op jit(solution)/shard_map/ppermute | solution.py:40
  43.8 6.7 %collective-permute-start.4 = (bf16[80,512]{1,0:T(8,128)(2,1)S(1)}, bf16[80,512]{1,0:T(8,128)(2,1)S(1)}, u32[]{:S(2)}, u32[]{:S(2)}) collective-permute-start(bf16[80,512]{1,0:T(8,128)(2,1)S(1)} %pad_maximum_fusion.2), channel_id=1, source_target_pairs={{0,8},{1,9},{2,10},{3,11},{4,12},{5,13},{6,14},{7,15},{8,16},{9,17... | collective-permute-start | bytes 245768 | tf_op jit(solution)/shard_map/ppermute | solution.py:40
  43.9 6.7 %collective-permute-start.5 = (bf16[80,512]{1,0:T(8,128)(2,1)S(1)}, bf16[80,512]{1,0:T(8,128)(2,1)S(1)}, u32[]{:S(2)}, u32[]{:S(2)}) collective-permute-start(bf16[80,512]{1,0:T(8,128)(2,1)S(1)} %pad_maximum_fusion.2), channel_id=1, source_target_pairs={{0,120},{1,121},{2,122},{3,123},{4,124},{5,125},{6,126},{7,127},{8... | collective-permute-start | bytes 245768 | tf_op jit(solution)/shard_map/ppermute | solution.py:40
  48.7 4.1 %collective-permute-start.6 = (bf16[16,512]{1,0:T(8,128)(2,1)S(1)}, bf16[16,512]{1,0:T(8,128)(2,1)S(1)}, u32[]{:S(2)}, u32[]{:S(2)}) collective-permute-start(bf16[16,512]{1,0:T(8,128)(2,1)S(1)} %get-tuple-element.39), channel_id=1, source_target_pairs={{0,16},{1,17},{2,18},{3,19},{4,20},{5,21},{6,22},{7,23},{8,24},{9,... | collective-permute-start | bytes 49160 | tf_op jit(solution)/shard_map/ppermute | solution.py:40
  50.5 19.0 %copy-start = (bf16[80,512]{1,0:T(8,128)(2,1)}, bf16[80,512]{1,0:T(8,128)(2,1)S(1)}, u32[]{:S(2)}) copy-start(bf16[80,512]{1,0:T(8,128)(2,1)S(1)} %collective-permute-done.4.refs_13_) | copy-start | bytes 245764
  50.6 18.9 %copy-start.1 = (bf16[80,512]{1,0:T(8,128)(2,1)}, bf16[80,512]{1,0:T(8,128)(2,1)S(1)}, u32[]{:S(2)}) copy-start(bf16[80,512]{1,0:T(8,128)(2,1)S(1)} %collective-permute-done.5.refs_15_) | copy-start | bytes 245764
  52.8 6.3 %collective-permute-start.7 = (bf16[64,512]{1,0:T(8,128)(2,1)S(1)}, bf16[64,512]{1,0:T(8,128)(2,1)S(1)}, u32[]{:S(2)}, u32[]{:S(2)}) collective-permute-start(bf16[64,512]{1,0:T(8,128)(2,1)S(1)} %pad_maximum_fusion.3), channel_id=1, source_target_pairs={{0,2},{1,3},{2,4},{3,5},{4,6},{5,7},{6,0},{7,1},{8,10},{9,11},{10,... | collective-permute-start | bytes 196616 | tf_op jit(solution)/shard_map/ppermute | solution.py:40
  52.9 6.3 %collective-permute-start.8 = (bf16[64,512]{1,0:T(8,128)(2,1)S(1)}, bf16[64,512]{1,0:T(8,128)(2,1)S(1)}, u32[]{:S(2)}, u32[]{:S(2)}) collective-permute-start(bf16[64,512]{1,0:T(8,128)(2,1)S(1)} %pad_maximum_fusion.3), channel_id=1, source_target_pairs={{0,4},{1,5},{2,6},{3,7},{4,0},{5,1},{6,2},{7,3},{8,12},{9,13},{10,... | collective-permute-start | bytes 196616 | tf_op jit(solution)/shard_map/ppermute | solution.py:40
  55.0 4.6 %collective-permute-start.9 = (bf16[64,512]{1,0:T(8,128)(2,1)S(1)}, bf16[64,512]{1,0:T(8,128)(2,1)S(1)}, u32[]{:S(2)}, u32[]{:S(2)}) collective-permute-start(bf16[64,512]{1,0:T(8,128)(2,1)S(1)} %pad_maximum_fusion.3), channel_id=1, source_target_pairs={{0,6},{1,7},{2,0},{3,1},{4,2},{5,3},{6,4},{7,5},{8,14},{9,15},{10,... | collective-permute-start | bytes 196616 | tf_op jit(solution)/shard_map/ppermute | solution.py:40
  55.1 20.6 %collective-permute-start.19 = (bf16[192,512]{1,0:T(8,128)(2,1)S(1)}, bf16[192,512]{1,0:T(8,128)(2,1)S(1)}, u32[]{:S(2)}, u32[]{:S(2)}) collective-permute-start(bf16[192,512]{1,0:T(8,128)(2,1)S(1)} %pad_maximum_fusion), channel_id=1, source_target_pairs={{0,1},{1,0},{2,3},{3,2},{4,5},{5,4},{6,7},{7,6},{8,9},{9,8},{10,11... | collective-permute-start | bytes 589832 | tf_op jit(solution)/shard_map/ppermute | solution.py:40
  56.3 19.5 %collective-permute-start.20 = (bf16[192,512]{1,0:T(8,128)(2,1)S(1)}, bf16[192,512]{1,0:T(8,128)(2,1)S(1)}, u32[]{:S(2)}, u32[]{:S(2)}) collective-permute-start(bf16[192,512]{1,0:T(8,128)(2,1)S(1)} %pad_maximum_fusion), channel_id=1, source_target_pairs={{0,7},{1,2},{2,1},{3,4},{4,3},{5,6},{6,5},{7,0},{8,15},{9,10},{10,... | collective-permute-start | bytes 589832 | tf_op jit(solution)/shard_map/ppermute | solution.py:40
  59.7 12.9 %copy-start.9 = (bf16[256,512]{1,0:T(8,128)(2,1)}, bf16[256,512]{1,0:T(8,128)(2,1)S(1)}, u32[]{:S(2)}) copy-start(bf16[256,512]{1,0:T(8,128)(2,1)S(1)} %constant_dynamic-update-slice_fusion.refs_3_) | copy-start | bytes 786436
  59.7 19.0 %copy-start.7 = (s32[1,1,2048]{2,1,0:T(1,128)S(1)}, s32[1,1,2048]{2,1,0:T(1,128)}, u32[]{:S(2)}) copy-start(s32[1,1,2048]{2,1,0:T(1,128)} %param.21) | copy-start | bytes 24580
  59.7 9.8 %collective-permute-start.10 = (bf16[256,512]{1,0:T(8,128)(2,1)S(1)}, bf16[256,512]{1,0:T(8,128)(2,1)S(1)}, u32[]{:S(2)}, u32[]{:S(2)}) collective-permute-start(bf16[256,512]{1,0:T(8,128)(2,1)S(1)} %constant_dynamic-update-slice_fusion.refs_3_), channel_id=1, source_target_pairs={{0,32},{1,33},{2,34},{3,35},{4,36},{5,37},{6,38},{7,39},{8,40},{9,... | collective-permute-start | bytes 786440 | tf_op jit(solution)/shard_map/ppermute | solution.py:40
  59.8 9.8 %collective-permute-start.11 = (bf16[256,512]{1,0:T(8,128)(2,1)S(1)}, bf16[256,512]{1,0:T(8,128)(2,1)S(1)}, u32[]{:S(2)}, u32[]{:S(2)}) collective-permute-start(bf16[256,512]{1,0:T(8,128)(2,1)S(1)} %constant_dynamic-update-slice_fusion.refs_3_), channel_id=1, source_target_pairs={{0,96},{1,97},{2,98},{3,99},{4,100},{5,101},{6,102},{7,103},{8,104... | collective-permute-start | bytes 786440 | tf_op jit(solution)/shard_map/ppermute | solution.py:40
  69.5 10.4 %copy-start.2 = (bf16[256,512]{1,0:T(8,128)(2,1)}, bf16[256,512]{1,0:T(8,128)(2,1)S(1)}, u32[]{:S(2)}) copy-start(bf16[256,512]{1,0:T(8,128)(2,1)S(1)} %collective-permute-done.10.refs_4_) | copy-start | bytes 786436
  69.5 10.4 %copy-start.3 = (bf16[256,512]{1,0:T(8,128)(2,1)}, bf16[256,512]{1,0:T(8,128)(2,1)S(1)}, u32[]{:S(2)}) copy-start(bf16[256,512]{1,0:T(8,128)(2,1)S(1)} %collective-permute-done.11.refs_5_) | copy-start | bytes 786436
  69.6 6.6 %collective-permute-start.12 = (bf16[128,512]{1,0:T(8,128)(2,1)S(1)}, bf16[128,512]{1,0:T(8,128)(2,1)S(1)}, u32[]{:S(2)}, u32[]{:S(2)}) collective-permute-start(bf16[128,512]{1,0:T(8,128)(2,1)S(1)} %slice.63), channel_id=1, source_target_pairs={{0,32},{1,33},{2,34},{3,35},{4,36},{5,37},{6,38},{7,39},{8,40},{9,... | collective-permute-start | bytes 393224 | tf_op jit(solution)/shard_map/ppermute | solution.py:40
  69.8 8.7 %collective-permute-start.13 = (bf16[128,512]{1,0:T(8,128)(2,1)S(1)}, bf16[128,512]{1,0:T(8,128)(2,1)S(1)}, u32[]{:S(2)}, u32[]{:S(2)}) collective-permute-start(bf16[128,512]{1,0:T(8,128)(2,1)S(1)} %slice.64), channel_id=1, source_target_pairs={{0,96},{1,97},{2,98},{3,99},{4,100},{5,101},{6,102},{7,103},{8,104... | collective-permute-start | bytes 393224 | tf_op jit(solution)/shard_map/ppermute | solution.py:40
  72.6 7.2 %collective-permute-start.14 = (bf16[256,512]{1,0:T(8,128)(2,1)S(1)}, bf16[256,512]{1,0:T(8,128)(2,1)S(1)}, u32[]{:S(2)}, u32[]{:S(2)}) collective-permute-start(bf16[256,512]{1,0:T(8,128)(2,1)S(1)} %constant_dynamic-update-slice_fusion.refs_3_), channel_id=1, source_target_pairs={{0,1},{1,0},{2,3},{3,2},{4,5},{5,4},{6,7},{7,6},{8,9},{9,8},{10,11... | collective-permute-start | bytes 786440 | tf_op jit(solution)/shard_map/ppermute | solution.py:40
  75.7 4.3 %copy-start.15 = (bf16[192,512]{1,0:T(8,128)(2,1)}, bf16[192,512]{1,0:T(8,128)(2,1)S(1)}, u32[]{:S(2)}) copy-start(bf16[192,512]{1,0:T(8,128)(2,1)S(1)} %collective-permute-done.19.refs_16_) | copy-start | bytes 589828
  75.7 4.2 %collective-permute-start.15 = (bf16[256,512]{1,0:T(8,128)(2,1)S(1)}, bf16[256,512]{1,0:T(8,128)(2,1)S(1)}, u32[]{:S(2)}, u32[]{:S(2)}) collective-permute-start(bf16[256,512]{1,0:T(8,128)(2,1)S(1)} %collective-permute-done.10.refs_4_), channel_id=1, source_target_pairs={{0,1},{1,0},{2,3},{3,2},{4,5},{5,4},{6,7},{7,6},{8,9},{9,8},{10,11... | collective-permute-start | bytes 786440 | tf_op jit(solution)/shard_map/ppermute | solution.py:40
  75.8 4.2 %copy-start.16 = (bf16[192,512]{1,0:T(8,128)(2,1)}, bf16[192,512]{1,0:T(8,128)(2,1)S(1)}, u32[]{:S(2)}) copy-start(bf16[192,512]{1,0:T(8,128)(2,1)S(1)} %collective-permute-done.20.refs_17_) | copy-start | bytes 589828
  75.8 4.1 %collective-permute-start.16 = (bf16[256,512]{1,0:T(8,128)(2,1)S(1)}, bf16[256,512]{1,0:T(8,128)(2,1)S(1)}, u32[]{:S(2)}, u32[]{:S(2)}) collective-permute-start(bf16[256,512]{1,0:T(8,128)(2,1)S(1)} %collective-permute-done.11.refs_5_), channel_id=1, source_target_pairs={{0,1},{1,0},{2,3},{3,2},{4,5},{5,4},{6,7},{7,6},{8,9},{9,8},{10,11... | collective-permute-start | bytes 786440 | tf_op jit(solution)/shard_map/ppermute | solution.py:40
  76.2 3.8 %copy-start.19 = (bf16[128,512]{1,0:T(8,128)(2,1)}, bf16[128,512]{1,0:T(8,128)(2,1)S(1)}, u32[]{:S(2)}) copy-start(bf16[128,512]{1,0:T(8,128)(2,1)S(1)} %collective-permute-done.12.refs_6_) | copy-start | bytes 393220
  76.2 3.6 %collective-permute-start.17 = (bf16[128,512]{1,0:T(8,128)(2,1)S(1)}, bf16[128,512]{1,0:T(8,128)(2,1)S(1)}, u32[]{:S(2)}, u32[]{:S(2)}) collective-permute-start(bf16[128,512]{1,0:T(8,128)(2,1)S(1)} %collective-permute-done.12.refs_6_), channel_id=1, source_target_pairs={{0,1},{1,0},{2,3},{3,2},{4,5},{5,4},{6,7},{7,6},{8,9},{9,8},{10,11... | collective-permute-start | bytes 393224 | tf_op jit(solution)/shard_map/ppermute | solution.py:40
  78.5 1.4 %copy-start.20 = (bf16[128,512]{1,0:T(8,128)(2,1)}, bf16[128,512]{1,0:T(8,128)(2,1)S(1)}, u32[]{:S(2)}) copy-start(bf16[128,512]{1,0:T(8,128)(2,1)S(1)} %collective-permute-done.13.refs_7_) | copy-start | bytes 393220
  78.5 1.3 %collective-permute-start.18 = (bf16[128,512]{1,0:T(8,128)(2,1)S(1)}, bf16[128,512]{1,0:T(8,128)(2,1)S(1)}, u32[]{:S(2)}, u32[]{:S(2)}) collective-permute-start(bf16[128,512]{1,0:T(8,128)(2,1)S(1)} %collective-permute-done.13.refs_7_), channel_id=1, source_target_pairs={{0,1},{1,0},{2,3},{3,2},{4,5},{5,4},{6,7},{7,6},{8,9},{9,8},{10,11... | collective-permute-start | bytes 393224 | tf_op jit(solution)/shard_map/ppermute | solution.py:40
  79.8 0.7 copy-start.12
  79.8 0.7 copy-start.21
  79.9 0.7 copy-start.22
  79.9 0.8 copy-start.13
  79.9 0.9 copy-start.14
  80.8 26.5 %copy-start.6 = (s32[3,4,256]{2,1,0:T(4,128)S(1)}, s32[3,4,256]{2,1,0:T(4,128)}, u32[]{:S(2)}) copy-start(s32[3,4,256]{2,1,0:T(4,128)} %param.24) | copy-start | bytes 36868
  98.9 6.4 %collective-permute-start.21 = (bf16[64,512]{1,0:T(8,128)(2,1)S(1)}, bf16[64,512]{1,0:T(8,128)(2,1)S(1)}, u32[]{:S(2)}, u32[]{:S(2)}) collective-permute-start(bf16[64,512]{1,0:T(8,128)(2,1)S(1)} %slice.76), channel_id=1, source_target_pairs={{0,8},{1,9},{2,10},{3,11},{4,12},{5,13},{6,14},{7,15},{8,16},{9,17... | collective-permute-start | bytes 196616 | tf_op jit(solution)/shard_map/ppermute | solution.py:40
  98.9 6.4 %collective-permute-start.22 = (bf16[64,512]{1,0:T(8,128)(2,1)S(1)}, bf16[64,512]{1,0:T(8,128)(2,1)S(1)}, u32[]{:S(2)}, u32[]{:S(2)}) collective-permute-start(bf16[64,512]{1,0:T(8,128)(2,1)S(1)} %slice.76), channel_id=1, source_target_pairs={{0,120},{1,121},{2,122},{3,123},{4,124},{5,125},{6,126},{7,127},{8... | collective-permute-start | bytes 196616 | tf_op jit(solution)/shard_map/ppermute | solution.py:40
  105.3 8.0 %copy-start.4 = (bf16[64,512]{1,0:T(8,128)(2,1)}, bf16[64,512]{1,0:T(8,128)(2,1)S(1)}, u32[]{:S(2)}) copy-start(bf16[64,512]{1,0:T(8,128)(2,1)S(1)} %collective-permute-done.21.above) | copy-start | bytes 196612
  105.3 8.0 %copy-start.5 = (bf16[64,512]{1,0:T(8,128)(2,1)}, bf16[64,512]{1,0:T(8,128)(2,1)S(1)}, u32[]{:S(2)}) copy-start(bf16[64,512]{1,0:T(8,128)(2,1)S(1)} %collective-permute-done.22.below) | copy-start | bytes 196612
  105.4 2.7 %collective-permute-start.23 = (bf16[192,512]{1,0:T(8,128)(2,1)S(1)}, bf16[192,512]{1,0:T(8,128)(2,1)S(1)}, u32[]{:S(2)}, u32[]{:S(2)}) collective-permute-start(bf16[192,512]{1,0:T(8,128)(2,1)S(1)} %pad_maximum_fusion.1), channel_id=1, source_target_pairs={{0,1},{1,0},{2,3},{3,2},{4,5},{5,4},{6,7},{7,6},{8,9},{9,8},{10,11... | collective-permute-start | bytes 589832 | tf_op jit(solution)/shard_map/ppermute | solution.py:40
  107.0 6.3 %collective-permute-start.24 = (bf16[192,512]{1,0:T(8,128)(2,1)S(1)}, bf16[192,512]{1,0:T(8,128)(2,1)S(1)}, u32[]{:S(2)}, u32[]{:S(2)}) collective-permute-start(bf16[192,512]{1,0:T(8,128)(2,1)S(1)} %pad_maximum_fusion.1), channel_id=1, source_target_pairs={{0,7},{1,2},{2,1},{3,4},{4,3},{5,6},{6,5},{7,0},{8,15},{9,10},{10,... | collective-permute-start | bytes 589832 | tf_op jit(solution)/shard_map/ppermute | solution.py:40
  108.1 5.2 %copy-start.17 = (bf16[192,512]{1,0:T(8,128)(2,1)}, bf16[192,512]{1,0:T(8,128)(2,1)S(1)}, u32[]{:S(2)}) copy-start(bf16[192,512]{1,0:T(8,128)(2,1)S(1)} %collective-permute-done.23.beside) | copy-start | bytes 589828
  113.3 0.7 copy-start.18

commit v3 on v2

v3 whole, which is shorter than its diff:
```python
import jax
import jax.numpy as jnp
from jax import lax
from jax.experimental import pallas as pl
from jax.experimental.pallas import tpu as pltpu
from jax.sharding import PartitionSpec as P

D = 512
AXES = ("band", "patch")
BANDS, PATCHES = 16, 8
EDGE_BLOCK = 1024
epsilon = 1e-05
F32, BF16 = jnp.float32, jnp.bfloat16


def split(device):
    band, patch = device // PATCHES, device % PATCHES
    return band // 4, band % 4, patch // 2, patch % 2


def torus(dy=0, dz=0, dx=0, dc=0):
    pairs = []
    for device in range(BANDS * PATCHES):
        y, z, x, c = split(device)
        band = (y + dy) % 4 * 4 + (z + dz) % 4
        patch = (x + dx) % 4 * 2 + (c + dc) % 2
        pairs.append((device, band * PATCHES + patch))
    return pairs


def plane(db, dp):
    return [
        (b * PATCHES + p, (b + db) % BANDS * PATCHES + (p + dp) % PATCHES)
        for b in range(BANDS)
        for p in range(PATCHES)
    ]


def send(values, pairs):
    return lax.ppermute(values, AXES, pairs)


def dot(a, b):
    return jnp.dot(a, b, preferred_element_type=F32)


def silu(v):
    half = 0.5 * v
    return half + half * jnp.tanh(half)


def layer_norm(v):
    centred = v - jnp.mean(v, axis=-1, keepdims=True)
    spread = jnp.mean(centred * centred, axis=-1, keepdims=True)
    return centred * lax.rsqrt(spread + epsilon)


def column(row):
    return jnp.transpose(jnp.broadcast_to(row, (8, row.shape[1])))[:, :1]


def pick_rows(row, count):
    col = column(row)
    lanes = lax.broadcasted_iota(jnp.int32, (row.shape[1], count), 1)
    return jnp.where(lanes == col, 1.0, 0.0).astype(BF16)


def add_rows(row, count):
    nodes = lax.broadcasted_iota(jnp.int32, (count, row.shape[1]), 0)
    return jnp.where(nodes == row, 1.0, 0.0).astype(BF16)


def weight(k):
    return pl.BlockSpec((None, D, D), lambda i: (k, 0, 0))


SMEM = pl.BlockSpec(memory_space=pltpu.SMEM)
VMEM = pl.BlockSpec(memory_space=pltpu.VMEM)
HBM = pl.BlockSpec(memory_space=pltpu.HBM)
ANY = pl.BlockSpec(memory_space=pl.ANY)


def stay(values):
    return pltpu.with_memory_space_constraint(values, pltpu.HBM)


class Fetched:
    def __init__(self, source, target, sem):
        self.copy, self.target, self.ready = pltpu.make_async_copy(source, target, sem), target, False
        self.copy.start()

    def __call__(self):
        if not self.ready:
            self.copy.wait()
            self.ready = True
        return self.target


def whole(shape):
    return pl.BlockSpec(shape, lambda i: (0,) * len(shape))


def params(mb):
    return pltpu.CompilerParams(
        dimension_semantics=("arbitrary",), vmem_limit_bytes=mb << 20
    )


def cost(rows, nbytes):
    return pl.CostEstimate(flops=2 * rows * D * D, bytes_accessed=nbytes, transcendentals=0)


def split_patch():
    band, patch = lax.axis_index("band"), lax.axis_index("patch")
    return band >> 2, band & 3, patch >> 1, patch & 1


def cell_index(sender):
    i = jnp.floor((sender.astype(F32) + 0.5) * (1.0 / 260)).astype(jnp.int32)
    j = sender - i * 260
    west, east = 2048 + i * 2 + j, 2064 - 258 + i * 2 + j
    return jnp.where(j < 2, west, jnp.where(j < 258, i * 256 + j - 2, east))


def near_index(sender, my_c):
    q, r = sender >> 8, sender & 255
    row = (q >= 3).astype(jnp.int32) + (q >= 6).astype(jnp.int32)
    col = q - 3 * row
    middle = jnp.where(row == 0, 0, jnp.where(row == 1, 64, 320))
    aside = jnp.where(col == 2 - 2 * my_c, 384, 576) + row * 64
    return jnp.where(col == 1, middle, aside) + r


def mesh_index(sender):
    my_y, my_z, my_x, my_c = split_patch()
    far = sender - 2304
    y, z, x, c, node = far >> 9, (far >> 7) & 3, (far >> 5) & 3, (far >> 4) & 1, far & 15
    kx, kz, kc = (my_x - x) & 3, (my_z - z) & 3, (my_c - c) & 1
    behind = jnp.where(my_z == 0, -1, 0)
    beyond = jnp.where(my_z == 3, 1, 0)
    turn = jnp.where(kz == 1, behind, jnp.where(kz == 3, beyond, 0))
    ky = (my_y - y + turn) & 3
    ky, kz = (jnp.where(k < 2, k, 5 - k) for k in (ky, kz))
    at = kc * 1024 + ky * 256 + kx * 64 + kz * 16 + node
    return jnp.where(sender < 2304, 2048 + near_index(sender, my_c), at)


def grid_body(blocks, x_ref, w0, w7, w8, sent, nxt, live):
    alive = blocks[lax.axis_index("band"), lax.axis_index("patch")] * 128
    live[...] = jnp.full(live.shape, alive, jnp.int32)
    x = x_ref[...]
    sent[...] = dot(x, w0[...]).astype(BF16)
    hidden = silu(dot(x, w7[...])).astype(BF16)
    nxt[...] = (x.astype(F32) + layer_norm(dot(hidden, w8[...]))).astype(BF16)


def grid_kernel(blocks, grid_flat, enc_w):
    blk = pl.BlockSpec((512, D), lambda i: (i, 0))
    return pl.pallas_call(
        grid_body,
        grid=(2,),
        in_specs=[SMEM, blk, weight(0), weight(7), weight(8)],
        out_specs=[blk] * 2 + [whole((8, 128))],
        out_shape=[jax.ShapeDtypeStruct((1024, D), BF16)] * 2
        + [jax.ShapeDtypeStruct((8, 128), jnp.int32)],
        compiler_params=params(60),
        cost_estimate=cost(5000, 5 << 20),
        name="grid_cells",
    )(blocks, grid_flat, *[enc_w] * 3)


def lead_body(feat, cells, d1, w2, w4, before, self_part):
    g = cells[...]
    recv = dot(g, d1[...]).astype(BF16).astype(F32)
    self_part[...] = dot(g, w4[...])
    for k in range(3):
        before[k] = (dot(feat[k], w2[...]) + recv).astype(before.dtype)


def lead_kernel(feats, grid_next, dec_w):
    lat, lon = feats.shape[1:3]
    blk = pl.BlockSpec((lon, D), lambda i: (i, 0))
    edges = pl.BlockSpec((3, None, lon, D), lambda i: (0, i, 0, 0))
    return pl.pallas_call(
        lead_body,
        grid=(lat,),
        in_specs=[edges, blk, weight(1), weight(2), weight(4)],
        out_specs=[edges, blk],
        out_shape=[
            jax.ShapeDtypeStruct(feats.shape, BF16),
            jax.ShapeDtypeStruct(grid_next.shape, F32),
        ],
        compiler_params=params(60),
        cost_estimate=cost(8000, 10 << 20),
        name="decoder_lead",
    )(feats, grid_next, *[dec_w] * 3)


def edge_sum(before, hidden_weight, target):
    hidden = silu(before).astype(BF16)
    message = layer_norm(dot(hidden, hidden_weight)).astype(BF16)
    return dot(add_rows(target, 256), message)


def node_update(m, total, w4, w5, w6):
    hid = silu(dot(m, w4()[...]) + dot(total.astype(BF16), w5()[...])).astype(BF16)
    return (m.astype(F32) + layer_norm(dot(hid, w6()[...]))).astype(BF16)


def enc_body(
    live, snd, rcv, feat, own, top, bottom, west, east, mesh_ref, enc_w, proc_w,
    nxt, psend, precv, both, rim, coarse,
    table, feat_v, rim_v, side_v, mesh_v, weights, index, live_v, sems,
):
    count = iter(range(sems.shape[0]))

    def fetch(source, target):
        return Fetched(source, target, sems.at[next(count)])

    steps = feat.shape[0] // EDGE_BLOCK
    w0 = fetch(enc_w.at[0], weights.at[0])
    rims = [fetch(top, rim_v.at[0]), fetch(bottom, rim_v.at[1])]
    sides = [fetch(v, side_v.at[pl.ds(16 * k, 16)]) for k, v in enumerate((west, east))]
    mesh = fetch(mesh_ref, mesh_v)
    w1 = fetch(enc_w.at[1], weights.at[1])
    mine = fetch(own, table.at[pl.ds(512, 1024)])
    w2, w3 = (fetch(enc_w.at[k], weights.at[k]) for k in (2, 3))
    feats = [fetch(snd, index.at[0]), fetch(rcv, index.at[1]), fetch(live, live_v)]
    for k in range(steps):
        rows = pl.ds(k * EDGE_BLOCK, EDGE_BLOCK)
        feats.append(fetch(feat.at[rows], feat_v.at[rows]))
    w4, w5, w6 = (fetch(enc_w.at[k], weights.at[k]) for k in (4, 5, 6))
    p0, p1 = (fetch(proc_w.at[k], weights.at[7 + k]) for k in (0, 1))

    table[2080:2176] = jnp.zeros((96, D), BF16)
    table[0:512] = dot(rims[0]()[...], w0()[...]).astype(BF16)
    table[1536:2048] = dot(rims[1]()[...], w0()[...]).astype(BF16)
    sides[0](), sides[1]()
    table[2048:2080] = dot(side_v[...], w0()[...]).astype(BF16)
    table[2176:2432] = dot(mesh()[...], w1()[...]).astype(BF16)
    mine()
    for ready in (w2, w3, *feats):
        ready()
    alive = live_v[0:1, 0:1]

    def edges(k, total):
        at = pl.ds(pl.multiple_of(k * EDGE_BLOCK, EDGE_BLOCK), EDGE_BLOCK)
        receiver = index[1, 0, :, at]
        sender = cell_index(index[0, 0, :, at])
        ones = jnp.concatenate([pick_rows(sender, 2176), pick_rows(receiver, 256)], axis=1)
        x = feat_v[at]
        before = dot(x, w2()[...]) + dot(ones, table[...])
        edge = k * EDGE_BLOCK + lax.broadcasted_iota(jnp.int32, (1, EDGE_BLOCK), 1)
        return total + edge_sum(before, w3()[...], jnp.where(edge < alive, receiver, -1))

    total = lax.fori_loop(0, steps, edges, jnp.zeros((256, D), F32))
    new = node_update(mesh()[...], total, w4, w5, w6)
    sent = dot(new, p0()[...]).astype(BF16)
    psend[...] = sent
    both[0:64], both[64:80] = sent[0:64], sent[240:256]
    coarse[...], rim[...] = sent[240:256], sent[0:64]
    nxt[...] = new
    precv[...] = dot(new, p1()[...]).astype(BF16)


def enc_kernel(live, senders, receivers, feats, own, top, bottom, west, east, mesh_flat, enc_w, proc_w):
    node = jax.ShapeDtypeStruct((256, D), BF16)
    return pl.pallas_call(
        enc_body,
        in_specs=[HBM] * 5 + [ANY] * 4 + [HBM] * 3,
        out_specs=[VMEM] * 6,
        out_shape=[node] * 3
        + [jax.ShapeDtypeStruct((rows, D), BF16) for rows in (80, 64, 16)],
        scratch_shapes=[
            pltpu.VMEM((2432, D), BF16),
            pltpu.VMEM(feats.shape, BF16),
            pltpu.VMEM((2, 512, D), BF16),
            pltpu.VMEM((32, D), BF16),
            pltpu.VMEM((256, D), BF16),
            pltpu.VMEM((9, D, D), BF16),
            pltpu.VMEM((2, *senders.shape), jnp.int32),
            pltpu.VMEM((8, 128), jnp.int32),
            pltpu.SemaphoreType.DMA((21,)),
        ],
        compiler_params=pltpu.CompilerParams(vmem_limit_bytes=36 << 20),
        cost_estimate=cost(25000, 10 << 20),
        name="encoder_edges",
    )(
        stay(live), stay(senders), stay(receivers), stay(feats), stay(own), top, bottom, west, east,
        stay(mesh_flat), stay(enc_w), stay(proc_w),
    )


COARSE = ((0, 256), (256, 256), (512, 256), (768, 128), (896, 128))
NEAR = ((2048, 64), (2112, 256), (2368, 64), (2432, 192), (2624, 192))


def proc_body(*refs):
    snd, rcv, feat = refs[:3]
    pieces, (recv, mesh_ref, proc_w, dec_w) = refs[3:18], refs[18:22]
    dsend, rim, table, feat_v, mesh_v, weights, index, sems = refs[22:]
    count = iter(range(sems.shape[0]))

    def fetch(source, target):
        return Fetched(source, target, sems.at[next(count)])

    places = COARSE + tuple((at + 1024, rows) for at, rows in COARSE) + NEAR
    first = [fetch(recv, table.at[pl.ds(2816, 256)])]
    for piece, (at, rows) in zip(pieces, places):
        first.append(fetch(piece.at[pl.ds(0, rows)], table.at[pl.ds(at, rows)]))
    first += [fetch(proc_w.at[k], weights.at[k - 2]) for k in (2, 3)]
    first += [fetch(feat, feat_v), fetch(snd, index.at[0]), fetch(rcv, index.at[1])]
    mesh = fetch(mesh_ref, mesh_v)
    w4, w5, w6 = (fetch(proc_w.at[k], weights.at[k - 2]) for k in (4, 5, 6))
    d0 = fetch(dec_w.at[0], weights.at[5])
    for ready in first:
        ready()

    def edges(k, total):
        at = pl.ds(pl.multiple_of(k * EDGE_BLOCK, EDGE_BLOCK), EDGE_BLOCK)
        receiver = index[1, 0, :, at]
        sender = mesh_index(index[0, 0, :, at])
        ones = jnp.concatenate([pick_rows(sender, 2816), pick_rows(receiver, 256)], axis=1)
        x = feat_v[at]
        before = dot(x, weights[0]) + dot(ones, table[...])
        return total + edge_sum(before, weights[1], receiver)

    total = lax.fori_loop(0, feat.shape[0] // EDGE_BLOCK, edges, jnp.zeros((256, D), F32))
    new = node_update(mesh()[...], total, w4, w5, w6)
    sent = dot(new, d0()[...]).astype(BF16)
    dsend[...] = sent
    rim[...] = sent[0:64]


def proc_kernel(feats, senders, receivers, pieces, recv, mesh_next, proc_w, dec_w):
    return pl.pallas_call(
        proc_body,
        in_specs=[HBM] * 3 + [ANY] * 15 + [HBM] * 4,
        out_specs=[VMEM] * 2,
        out_shape=[jax.ShapeDtypeStruct((256, D), BF16), jax.ShapeDtypeStruct((64, D), BF16)],
        scratch_shapes=[
            pltpu.VMEM((3072, D), BF16),
            pltpu.VMEM(feats.shape, BF16),
            pltpu.VMEM((256, D), BF16),
            pltpu.VMEM((6, D, D), BF16),
            pltpu.VMEM((2, *senders.shape), jnp.int32),
            pltpu.SemaphoreType.DMA((26,)),
        ],
        compiler_params=pltpu.CompilerParams(vmem_limit_bytes=36 << 20),
        cost_estimate=cost(25000, 10 << 20),
        name="mesh_edges",
    )(
        stay(senders), stay(receivers), stay(feats), *pieces, stay(recv), stay(mesh_next),
        stay(proc_w), stay(dec_w),
    )


def dec_body(snd, lead, above, own, below, beside, across, cells, self_part, w3, w5, w6, out, near):
    @pl.when(pl.program_id(0) == 0)
    def _():
        near[0:64] = above[...]
        near[64:320] = own[...]
        near[320:384] = below[...]
        near[384:576] = beside[...]
        near[576:768] = across[...]

    n = cells.shape[0]
    my_c = lax.axis_index("patch") & 1
    row = pl.ds(pl.program_id(0), 1)
    ones = [pick_rows(near_index(snd[k, row], my_c), 768) for k in range(3)]
    ones = jnp.concatenate(ones, axis=0)
    before = lead[...].astype(F32).reshape(3 * n, D) + dot(ones, near[...])
    hidden = silu(before).astype(BF16)
    message = layer_norm(dot(hidden, w3[...])).astype(BF16).astype(F32).reshape(3, n, D)
    summed = message[0] + message[1] + message[2]
    hid = silu(self_part[...] + dot(summed.astype(BF16), w5[...])).astype(BF16)
    out[...] = (cells[...].astype(F32) + layer_norm(dot(hid, w6[...]))).astype(BF16)


def dec_kernel(lead, senders, near, grid_next, self_part, dec_w):
    lat, lon = senders.shape[1:]
    blk = pl.BlockSpec((lon, D), lambda i: (i, 0))
    return pl.pallas_call(
        dec_body,
        grid=(lat,),
        in_specs=[
            whole(senders.shape),
            pl.BlockSpec((3, None, lon, D), lambda i: (0, i, 0, 0)),
        ]
        + [whole(rows.shape) for rows in near]
        + [blk, blk, weight(3), weight(5), weight(6)],
        out_specs=blk,
        out_shape=jax.ShapeDtypeStruct((lat * lon, D), BF16),
        scratch_shapes=[pltpu.VMEM((768, D), BF16)],
        compiler_params=params(36),
        cost_estimate=cost(15000, 9 << 20),
        name="decoder_edges",
    )(senders, lead, *near, grid_next, self_part, *[dec_w] * 3)


SWAP = [(d, d ^ 1) for d in range(BANDS * PATCHES)]
CROSS = [
    (d, d // PATCHES * PATCHES + (d % PATCHES + (1 if d % 2 else -1)) % PATCHES)
    for d in range(BANDS * PATCHES)
]


def mesh_rows(own, both, rim, rows, lead):
    above, below = send(both, plane(1, 0)), send(both, plane(-1, 0))
    rows = jnp.concatenate([rows, above[64:], below[64:], send(rows, torus(dz=2))], axis=0)
    third, second, first = lax.optimization_barrier([send(rows, torus(dx=k)) for k in (3, 2, 1)])
    here = jnp.concatenate([rows, first, second, third], axis=0)
    below, above, here, given = lax.optimization_barrier((below, above, here, lead[0]))
    col = jnp.concatenate([above[:64], rim, below[:64]], axis=0)
    across, beside = lax.optimization_barrier((send(col, CROSS), send(col, SWAP)))
    lead = lead[1](given)
    ahead, behind = send(here, torus(dy=1)), send(here, torus(dy=-1))
    behind, ahead, lead = lax.optimization_barrier((behind, ahead, lead))
    high, low = lax.optimization_barrier(
        (send(behind[128:], torus(dy=-1)), send(ahead[:128], torus(dy=1)))
    )
    far = low, high
    coarse = [here, ahead, behind, *far]
    return coarse + [send(v, SWAP) for v in coarse] + [above, own, below, beside, across], lead


def near_rows(own, rim):
    above, below = send(rim, plane(1, 0)), send(rim, plane(-1, 0))
    col = jnp.concatenate([above, rim, below], axis=0)
    across, beside = lax.optimization_barrier((send(col, CROSS), send(col, SWAP)))
    return above, own, below, beside, across


def shards(
    grid_state,
    mesh_state,
    g2m_features,
    g2m_sender,
    g2m_receiver,
    g2m_blocks,
    proc_features,
    proc_sender,
    proc_receiver,
    dec_features,
    dec_sender,
    enc_weights,
    proc_weights,
    dec_weights,
):
    cells = grid_state.reshape(1024, D)
    nodes = mesh_state.reshape(256, D)
    top = send(grid_state[2:4], plane(1, 0))
    bottom = send(grid_state[0:2], plane(-1, 0))
    grid_send, grid_next, live = grid_kernel(g2m_blocks, cells, enc_weights)
    bottom, top, grid_send = lax.optimization_barrier((bottom, top, grid_send))
    first = jnp.concatenate([top[:, :2], grid_state[:, :2], bottom[:, :2]], axis=0)
    final = jnp.concatenate([top[:, 254:], grid_state[:, 254:], bottom[:, 254:]], axis=0)
    west = send(final.reshape(16, D), plane(0, 1))
    east = send(first.reshape(16, D), plane(0, -1))

    mesh_next, proc_send, proc_recv, both, rim, coarse = enc_kernel(
        live, g2m_sender, g2m_receiver, g2m_features.reshape(-1, D),
        grid_send, top.reshape(512, D), bottom.reshape(512, D), west, east, nodes,
        enc_weights, proc_weights,
    )
    pieces, (lead, self_part) = mesh_rows(
        proc_send, both, rim, coarse, (grid_next, lambda g: lead_kernel(dec_features, g, dec_weights))
    )
    dec_send, rim = proc_kernel(
        proc_features.reshape(-1, D), proc_sender, proc_receiver, pieces, proc_recv,
        mesh_next, proc_weights, dec_weights,
    )
    out = dec_kernel(
        lead, dec_sender, near_rows(dec_send, rim), grid_next, self_part, dec_weights
    )
    return out.reshape(grid_state.shape)


def solution(mesh):
    placed = (
        P("band", "patch", None),
        P("band", "patch", None, None),
        P("band", "patch", None, None),
        P("band", "patch", None),
        P("band", "patch", None),
        P(),
        P("band", "patch", None, None),
        P("band", "patch", None),
        P("band", "patch", None),
        P(None, "band", "patch", None),
        P(None, "band", "patch"),
        P(),
        P(),
        P(),
    )
    return jax.shard_map(
        shards, mesh=mesh, in_specs=placed, out_specs=P("band", "patch", None), check_vma=False
    )
```

time: 128 us -> 122 us (0.953)
  waiting for transfers between devices: 19 us -> 29.1 us
  local copies, waits for them, and re-layouts: 8.1 us -> 3.56 us
  starting transfers between devices: 37.4 us -> 32.9 us
  Pallas kernels: 59 us -> 55.6 us
  other arithmetic: 3.39 us -> 0.08 us
    ppermute x25, waiting for transfers between devices: 19 us -> 29.1 us  [send(): return lax.ppermute(values, AXES, pairs)]
    ppermute x25, starting transfers between devices: 37.4 us -> 32.9 us  [send(): return lax.ppermute(values, AXES, pairs)]
    pallas_call x4, Pallas kernels: 51.9 us -> 48.4 us  [the longest x1 17.1 us: proc_kernel(): pl.pallas_call(proc_body, in_specs=[HBM] * 3 + [ANY] * 15 + [HBM] * 4, ou...]
    slice x12 -> x4, local copies, waits for them, and re-layouts: 4.55 us -> 2.08 us  [the longest x1 1.27 us: shards(): top = send(grid_state[2:4], plane(1, 0))]
    select_n x2 -> x0, other arithmetic: 1.79 us -> none  [the longest x1 1.14 us: mesh_index(): jnp.where(sender < 2304, 2048 + near_index(jnp.minimum(sender, 2303)), far)]
  transfers between devices with their start and end apart: 25 -> 25, of which waited for: 9 -> 13; matrix products, arithmetic and copies ran while one was open for 4% -> 2% of each run, Pallas kernels for 9% -> 10%
where the time goes in v3:
time: 122 us; the launch traced here: 121 us
  Pallas kernels  55.6 us (46%)
  starting transfers between devices  32.9 us (27%)
  waiting for transfers between devices  29.1 us (24%)
  local copies, waits for them, and re-layouts  3.56 us (3%)
    ppermute x25, starting transfers between devices, send(): return lax.ppermute(values, AXES, pairs)  32.9 us
    ppermute x25, waiting for transfers between devices, send(): return lax.ppermute(values, AXES, pairs)  29.1 us
    pallas_call x1, Pallas kernels, proc_kernel(): pl.pallas_call(proc_body, in_specs=[HBM] * 3 + [ANY] * 15 + [HBM] * 4, ou...  17.1 us
    pallas_call x1, Pallas kernels, enc_kernel(): pl.pallas_call(enc_body, in_specs=[HBM] * 5 + [ANY] * 4 + [HBM] * 3, out_...  14.7 us
    pallas_call x1, Pallas kernels, dec_kernel(): pl.pallas_call(dec_body, grid=(lat,), in_specs=[whole(senders.shape), pl....  11.7 us
    pallas_call x1, Pallas kernels, lead_kernel(): pl.pallas_call(lead_body, grid=(lat,), in_specs=[edges, blk, weight(1), w...  7.15 us
    pallas_call x1, Pallas kernels, grid_kernel(): pl.pallas_call(grid_body, grid=(2,), in_specs=[SMEM, blk, weight(0), weig...  4.95 us
  transfers between devices with their start and end apart: 25, of which 13 were waited for; matrix products, arithmetic and copies ran while one was open for 2% of the time, Pallas kernels for 10%

profile of v3, /device:TPU:7, one launch (start us, length us, event | category | flops | bytes accessed | tf_op | source)
XLA Modules:
  0.0 121.5 jit_solution(16632997193118741860)
XLA Ops:
  0.0 1.3 %fusion.1 = (bf16[2,256,512]{2,1,0:T(8,128)(2,1)S(1)}, bf16[2,256,512]{2,1,0:T(8,128)(2,1)S(1)}) fusion(bf16[4,256,512]{2,1,0:T(8,128)(2,1)} %param.14), kind=kLoop, calls=%fused_computation.15 | loop fusion | bytes 2097152 | tf_op jit(solution)/shard_map/slice | solution.py:452
  1.3 1.7 %collective-permute-start.1 = (bf16[2,256,512]{2,1,0:T(8,128)(2,1)S(1)}, bf16[2,256,512]{2,1,0:T(8,128)(2,1)S(1)}, u32[]{:S(2)}, u32[]{:S(2)}) collective-permute-start(bf16[2,256,512]{2,1,0:T(8,128)(2,1)S(1)} %get-tuple-element.73), channel_id=1, source_target_pairs={{0,8},{1,9},{2,10},{3,11},{4,12},{5,13},{6,14},{7,15},{8,16},{9,17... | collective-permute-start | bytes 1572872 | tf_op jit(solution)/shard_map/ppermute | solution.py:40
  3.0 4.7 %collective-permute-start = (bf16[2,256,512]{2,1,0:T(8,128)(2,1)S(1)}, bf16[2,256,512]{2,1,0:T(8,128)(2,1)S(1)}, u32[]{:S(2)}, u32[]{:S(2)}) collective-permute-start(bf16[2,256,512]{2,1,0:T(8,128)(2,1)S(1)} %get-tuple-element.74), channel_id=1, source_target_pairs={{0,120},{1,121},{2,122},{3,123},{4,124},{5,125},{6,126},{7,127},{8... | collective-permute-start | bytes 1572872 | tf_op jit(solution)/shard_map/ppermute | solution.py:40
  7.6 1.4 %copy.35.blocks = s32[16,8]{1,0:T(8,128)} copy(s32[16,8]{0,1:T(8,128)} %param.19) | data formatting | bytes 1024 | tf_op args[5]
  9.0 0.8 fusion
  9.8 4.9 %grid_cells.1 = (bf16[1024,512]{1,0:T(8,128)(2,1)}, bf16[1024,512]{1,0:T(8,128)(2,1)}, s32[8,128]{1,0:T(8,128)}) custom-call(s32[16,8]{1,0:T(8,128)} %copy.35.blocks, bf16[1024,512]{1,0:T(8,128)(2,1)} %bitcast.9, bf16[9,512,512]{2,1,0:T(8,128)(2,1)} %enc_w.1, bf16[9,512,512]{2,1,0:T(8,128)(2,1)} %enc_w.1, bf16[9,512,512]{2,1,0:T(8,128)(2,1)} %enc_w.1), custom_call_target="tpu_custom_call" | custom-call | flops 2621440000 | bytes 5242880 | tf_op jit(solution)/shard_map/grid_cells/pallas_call | solution.py:159
  14.7 4.5 %collective-permute-done.1 = bf16[2,256,512]{2,1,0:T(8,128)(2,1)S(1)} collective-permute-done((bf16[2,256,512]{2,1,0:T(8,128)(2,1)S(1)}, bf16[2,256,512]{2,1,0:T(8,128)(2,1)S(1)}, u32[]{:S(2)}, u32[]{:S(2)}) %collective-permute-start.1) | collective-permute-done | bytes 524320 | tf_op jit(solution)/shard_map/ppermute | solution.py:40
  19.2 0.0 collective-permute-done
  19.3 1.3 %collective-permute-start.2 = (bf16[16,512]{1,0:T(8,128)(2,1)S(1)}, bf16[16,512]{1,0:T(8,128)(2,1)S(1)}, u32[]{:S(2)}, u32[]{:S(2)}) collective-permute-start(bf16[16,512]{1,0:T(8,128)(2,1)S(1)} %reshape.31), channel_id=1, source_target_pairs={{0,1},{1,2},{2,3},{3,4},{4,5},{5,6},{6,7},{7,0},{8,9},{9,10},{10,1... | collective-permute-start | bytes 49160 | tf_op jit(solution)/shard_map/ppermute | solution.py:40
  20.7 0.0 collective-permute-start.3
  20.7 0.9 collective-permute-done.2.west
  21.5 3.5 %collective-permute-done.3.east = bf16[16,512]{1,0:T(8,128)(2,1)S(1)} collective-permute-done((bf16[16,512]{1,0:T(8,128)(2,1)S(1)}, bf16[16,512]{1,0:T(8,128)(2,1)S(1)}, u32[]{:S(2)}, u32[]{:S(2)}) %collective-permute-start.3) | collective-permute-done | bytes 16416 | tf_op jit(solution)/shard_map/ppermute | solution.py:40
  25.0 14.7 %encoder_edges.1 = (bf16[256,512]{1,0:T(8,128)(2,1)S(1)}, bf16[256,512]{1,0:T(8,128)(2,1)S(1)}, bf16[256,512]{1,0:T(8,128)(2,1)S(1)}, bf16[80,512]{1,0:T(8,128)(...) custom-call(s32[8,128]{1,0:T(8,128)} %get-tuple-element.38.live, s32[1,1,2048]{2,1,0:T(1,128)} %snd.2, ...), custom_call_target="tpu_custom_call" | custom-call | flops 13107200000 | bytes 10485760 | tf_op jit(solution)/shard_map/encoder_edges/pallas_call | solution.py:268
  39.8 0.0 copy-start.6
  39.8 0.1 collective-permute-start.5
  39.8 4.9 %collective-permute-start.4 = (bf16[80,512]{1,0:T(8,128)(2,1)S(1)}, bf16[80,512]{1,0:T(8,128)(2,1)S(1)}, u32[]{:S(2)}, u32[]{:S(2)}) collective-permute-start(bf16[80,512]{1,0:T(8,128)(2,1)S(1)} %get-tuple-element.43), channel_id=1, source_target_pairs={{0,120},{1,121},{2,122},{3,123},{4,124},{5,125},{6,126},{7,127},{8... | collective-permute-start | bytes 245768 | tf_op jit(solution)/shard_map/ppermute | solution.py:40
  44.8 1.7 %collective-permute-done.5.refs_13_ = bf16[80,512]{1,0:T(8,128)(2,1)S(1)} collective-permute-done((bf16[80,512]{1,0:T(8,128)(2,1)S(1)}, bf16[80,512]{1,0:T(8,128)(2,1)S(1)}, u32[]{:S(2)}, u32[]{:S(2)}) %collective-permute-start.5) | collective-permute-done | bytes 81952 | tf_op jit(solution)/shard_map/ppermute | solution.py:40
  46.6 2.3 %collective-permute-done.6 = bf16[16,512]{1,0:T(8,128)(2,1)S(1)} collective-permute-done((bf16[16,512]{1,0:T(8,128)(2,1)S(1)}, bf16[16,512]{1,0:T(8,128)(2,1)S(1)}, u32[]{:S(2)}, u32[]{:S(2)}) %collective-permute-start.6) | collective-permute-done | bytes 16416 | tf_op jit(solution)/shard_map/ppermute | solution.py:40
  48.9 2.2 %collective-permute-start.8 = (bf16[64,512]{1,0:T(8,128)(2,1)S(1)}, bf16[64,512]{1,0:T(8,128)(2,1)S(1)}, u32[]{:S(2)}, u32[]{:S(2)}) collective-permute-start(bf16[64,512]{1,0:T(8,128)(2,1)S(1)} %pad_maximum_fusion.1), channel_id=1, source_target_pairs={{0,4},{1,5},{2,6},{3,7},{4,0},{5,1},{6,2},{7,3},{8,12},{9,13},{10,... | collective-permute-start | bytes 196616 | tf_op jit(solution)/shard_map/ppermute | solution.py:40
  51.1 0.9 collective-permute-done.9
  52.0 1.6 %collective-permute-done.8 = bf16[64,512]{1,0:T(8,128)(2,1)S(1)} collective-permute-done((bf16[64,512]{1,0:T(8,128)(2,1)S(1)}, bf16[64,512]{1,0:T(8,128)(2,1)S(1)}, u32[]{:S(2)}, u32[]{:S(2)}) %collective-permute-start.8) | collective-permute-done | bytes 65568 | tf_op jit(solution)/shard_map/ppermute | solution.py:40
  53.6 2.4 %collective-permute-done.7 = bf16[64,512]{1,0:T(8,128)(2,1)S(1)} collective-permute-done((bf16[64,512]{1,0:T(8,128)(2,1)S(1)}, bf16[64,512]{1,0:T(8,128)(2,1)S(1)}, u32[]{:S(2)}, u32[]{:S(2)}) %collective-permute-start.7) | collective-permute-done | bytes 65568 | tf_op jit(solution)/shard_map/ppermute | solution.py:40
  56.0 0.1 collective-permute-start.11
  56.1 2.7 %collective-permute-start.10 = (bf16[256,512]{1,0:T(8,128)(2,1)S(1)}, bf16[256,512]{1,0:T(8,128)(2,1)S(1)}, u32[]{:S(2)}, u32[]{:S(2)}) collective-permute-start(bf16[256,512]{1,0:T(8,128)(2,1)S(1)} %constant_dynamic-update-slice_fusion.refs_3_), channel_id=1, source_target_pairs={{0,96},{1,97},{2,98},{3,99},{4,100},{5,101},{6,102},{7,103},{8,104... | collective-permute-start | bytes 786440 | tf_op jit(solution)/shard_map/ppermute | solution.py:40
  58.8 7.1 %decoder_lead.1 = (bf16[3,4,256,512]{3,2,1,0:T(8,128)(2,1)}, f32[1024,512]{1,0:T(8,128)}) custom-call(bf16[3,4,256,512]{3,2,1,0:T(8,128)(2,1)} %feat.1, bf16[1024,512]{1,0:T(8,128)(2,1)} %get-tuple-element.50.cells, bf16[7,512,512]{2,1,0:T(8,128)(2,1)} %w6.1, bf16[7,512,512]{2,1,0:T(8,128)(2,1)} %w6.1, bf16[7,512,512]{2,1,0:T(8,128)(2,1)} %w6.1), custom_call_target="tpu_custom_call" | custom-call | flops 4194304000 | bytes 10485760 | tf_op jit(solution)/shard_map/decoder_lead/pallas_call | solution.py:184
  65.9 0.0 collective-permute-done.11.refs_4_
  65.9 0.0 collective-permute-done.10.refs_5_
  66.0 0.1 collective-permute-start.12
  66.1 1.5 %collective-permute-start.13 = (bf16[128,512]{1,0:T(8,128)(2,1)S(1)}, bf16[128,512]{1,0:T(8,128)(2,1)S(1)}, u32[]{:S(2)}, u32[]{:S(2)}) collective-permute-start(bf16[128,512]{1,0:T(8,128)(2,1)S(1)} %slice.53), channel_id=1, source_target_pairs={{0,32},{1,33},{2,34},{3,35},{4,36},{5,37},{6,38},{7,39},{8,40},{9,... | collective-permute-start | bytes 393224 | tf_op jit(solution)/shard_map/ppermute | solution.py:40
  67.5 3.1 %collective-permute-start.20 = (bf16[192,512]{1,0:T(8,128)(2,1)S(1)}, bf16[192,512]{1,0:T(8,128)(2,1)S(1)}, u32[]{:S(2)}, u32[]{:S(2)}) collective-permute-start(bf16[192,512]{1,0:T(8,128)(2,1)S(1)} %pad_maximum_fusion), channel_id=1, source_target_pairs={{0,1},{1,0},{2,3},{3,2},{4,5},{5,4},{6,7},{7,6},{8,9},{9,8},{10,11... | collective-permute-start | bytes 589832 | tf_op jit(solution)/shard_map/ppermute | solution.py:40
  70.6 0.3 collective-permute-start.19
  70.9 2.4 %collective-permute-start.15 = (bf16[256,512]{1,0:T(8,128)(2,1)S(1)}, bf16[256,512]{1,0:T(8,128)(2,1)S(1)}, u32[]{:S(2)}, u32[]{:S(2)}) collective-permute-start(bf16[256,512]{1,0:T(8,128)(2,1)S(1)} %collective-permute-done.11.refs_4_), channel_id=1, source_target_pairs={{0,1},{1,0},{2,3},{3,2},{4,5},{5,4},{6,7},{7,6},{8,9},{9,8},{10,11... | collective-permute-start | bytes 786440 | tf_op jit(solution)/shard_map/ppermute | solution.py:40
  73.3 2.0 %collective-permute-start.16 = (bf16[256,512]{1,0:T(8,128)(2,1)S(1)}, bf16[256,512]{1,0:T(8,128)(2,1)S(1)}, u32[]{:S(2)}, u32[]{:S(2)}) collective-permute-start(bf16[256,512]{1,0:T(8,128)(2,1)S(1)} %collective-permute-done.10.refs_5_), channel_id=1, source_target_pairs={{0,1},{1,0},{2,3},{3,2},{4,5},{5,4},{6,7},{7,6},{8,9},{9,8},{10,11... | collective-permute-start | bytes 786440 | tf_op jit(solution)/shard_map/ppermute | solution.py:40
  75.3 0.0 collective-permute-start.17
  75.3 1.7 %collective-permute-done.19.refs_17_ = bf16[192,512]{1,0:T(8,128)(2,1)S(1)} collective-permute-done((bf16[192,512]{1,0:T(8,128)(2,1)S(1)}, bf16[192,512]{1,0:T(8,128)(2,1)S(1)}, u32[]{:S(2)}, u32[]{:S(2)}) %collective-permute-start.19) | collective-permute-done | bytes 196640 | tf_op jit(solution)/shard_map/ppermute | solution.py:40
  76.9 1.3 %collective-permute-done.18.refs_12_ = bf16[128,512]{1,0:T(8,128)(2,1)S(1)} collective-permute-done((bf16[128,512]{1,0:T(8,128)(2,1)S(1)}, bf16[128,512]{1,0:T(8,128)(2,1)S(1)}, u32[]{:S(2)}, u32[]{:S(2)}) %collective-permute-start.18) | collective-permute-done | bytes 131104 | tf_op jit(solution)/shard_map/ppermute | solution.py:40
  78.3 0.0 collective-permute-done.15.refs_9_
  78.3 0.0 collective-permute-done.16.refs_10_
  78.3 0.0 copy-start.2
  78.3 17.1 %mesh_edges.1 = (bf16[256,512]{1,0:T(8,128)(2,1)S(1)}, bf16[64,512]{1,0:T(8,128)(2,1)S(1)}) custom-call(s32[1,1,2048]{2,1,0:T(1,128)} %refs_0_.1, s32[1,1,2048]{2,1,0:T(1,128)} %refs_1_.1, bf16[2048,512]{1,0:T(8,128)(2,1)} %bitcast.11, bf16[256,512]{1,0:T(8,128)(2,1)S(1)} %constant_dynamic-update-slice_fusion.refs_3_, ...), custom_call_target="tpu_custom_call" | custom-call | flops 13107200000 | bytes 10485760 | tf_op jit(solution)/shard_map/mesh_edges/pallas_call | solution.py:336
  95.5 0.1 collective-permute-start.21
  95.5 4.8 %collective-permute-start.22 = (bf16[64,512]{1,0:T(8,128)(2,1)S(1)}, bf16[64,512]{1,0:T(8,128)(2,1)S(1)}, u32[]{:S(2)}, u32[]{:S(2)}) collective-permute-start(bf16[64,512]{1,0:T(8,128)(2,1)S(1)} %get-tuple-element.66), channel_id=1, source_target_pairs={{0,120},{1,121},{2,122},{3,123},{4,124},{5,125},{6,126},{7,127},{8... | collective-permute-start | bytes 196616 | tf_op jit(solution)/shard_map/ppermute | solution.py:40
  100.3 2.1 %collective-permute-done.21.above = bf16[64,512]{1,0:T(8,128)(2,1)S(1)} collective-permute-done((bf16[64,512]{1,0:T(8,128)(2,1)S(1)}, bf16[64,512]{1,0:T(8,128)(2,1)S(1)}, u32[]{:S(2)}, u32[]{:S(2)}) %collective-permute-start.21) | collective-permute-done | bytes 65568 | tf_op jit(solution)/shard_map/ppermute | solution.py:40
  102.5 1.0 collective-permute-start.24
  103.5 0.1 collective-permute-start.23
  103.6 1.0 collective-permute-done.24.beside
  104.6 5.2 %collective-permute-done.23.across = bf16[192,512]{1,0:T(8,128)(2,1)S(1)} collective-permute-done((bf16[192,512]{1,0:T(8,128)(2,1)S(1)}, bf16[192,512]{1,0:T(8,128)(2,1)S(1)}, u32[]{:S(2)}, u32[]{:S(2)}) %collective-permute-start.23) | collective-permute-done | bytes 196640 | tf_op jit(solution)/shard_map/ppermute | solution.py:40
  109.8 11.7 %decoder_edges.1 = bf16[1024,512]{1,0:T(8,128)(2,1)} custom-call(s32[3,4,256]{2,1,0:T(4,128)S(1)} %copy-done.2, bf16[3,4,256,512]{3,2,1,0:T(8,128)(2,1)S(1)} %copy-done.3, bf16[64,512]{1,0:T(8,128)(2,1)S(1)} %collective-permute-done.21.above, bf16[256,512]{1,0:T(8,128)(2,1)S(1)} %get-tuple-element.67.own, bf16[64,512]{1,0:T(8,128)(2,1)S(1)} %collective-permute-done.22.below, ...), custom_call_target="tpu_custom_call" | custom-call | flops 7864320000 | bytes 9437184 | tf_op jit(solution)/shard_map/decoder_edges/pallas_call | solution.py:383
  (45 shorter events, 0.3 us)
Async XLA Ops:
  1.3 17.9 %collective-permute-start.1 = (bf16[2,256,512]{2,1,0:T(8,128)(2,1)S(1)}, bf16[2,256,512]{2,1,0:T(8,128)(2,1)S(1)}, u32[]{:S(2)}, u32[]{:S(2)}) collective-permute-start(bf16[2,256,512]{2,1,0:T(8,128)(2,1)S(1)} %get-tuple-element.73), channel_id=1, source_target_pairs={{0,8},{1,9},{2,10},{3,11},{4,12},{5,13},{6,14},{7,15},{8,16},{9,17... | collective-permute-start | bytes 1572872 | tf_op jit(solution)/shard_map/ppermute | solution.py:40
  3.0 16.2 %collective-permute-start = (bf16[2,256,512]{2,1,0:T(8,128)(2,1)S(1)}, bf16[2,256,512]{2,1,0:T(8,128)(2,1)S(1)}, u32[]{:S(2)}, u32[]{:S(2)}) collective-permute-start(bf16[2,256,512]{2,1,0:T(8,128)(2,1)S(1)} %get-tuple-element.74), channel_id=1, source_target_pairs={{0,120},{1,121},{2,122},{3,123},{4,124},{5,125},{6,126},{7,127},{8... | collective-permute-start | bytes 1572872 | tf_op jit(solution)/shard_map/ppermute | solution.py:40
  19.3 2.2 %collective-permute-start.2 = (bf16[16,512]{1,0:T(8,128)(2,1)S(1)}, bf16[16,512]{1,0:T(8,128)(2,1)S(1)}, u32[]{:S(2)}, u32[]{:S(2)}) collective-permute-start(bf16[16,512]{1,0:T(8,128)(2,1)S(1)} %reshape.31), channel_id=1, source_target_pairs={{0,1},{1,2},{2,3},{3,4},{4,5},{5,6},{6,7},{7,0},{8,9},{9,10},{10,1... | collective-permute-start | bytes 49160 | tf_op jit(solution)/shard_map/ppermute | solution.py:40
  20.7 4.4 %collective-permute-start.3 = (bf16[16,512]{1,0:T(8,128)(2,1)S(1)}, bf16[16,512]{1,0:T(8,128)(2,1)S(1)}, u32[]{:S(2)}, u32[]{:S(2)}) collective-permute-start(bf16[16,512]{1,0:T(8,128)(2,1)S(1)} %reshape.32), channel_id=1, source_target_pairs={{0,7},{1,0},{2,1},{3,2},{4,3},{5,4},{6,5},{7,6},{8,15},{9,8},{10,9... | collective-permute-start | bytes 49160 | tf_op jit(solution)/shard_map/ppermute | solution.py:40
  39.7 16.3 %copy-start.5 = (bf16[256,512]{1,0:T(8,128)(2,1)}, bf16[256,512]{1,0:T(8,128)(2,1)S(1)}, u32[]{:S(2)}) copy-start(bf16[256,512]{1,0:T(8,128)(2,1)S(1)} %get-tuple-element.65.refs_19_) | copy-start | bytes 786436
  39.8 16.3 %copy-start.6 = (bf16[256,512]{1,0:T(8,128)(2,1)}, bf16[256,512]{1,0:T(8,128)(2,1)S(1)}, u32[]{:S(2)}) copy-start(bf16[256,512]{1,0:T(8,128)(2,1)S(1)} %get-tuple-element.64.refs_18_) | copy-start | bytes 786436
  39.8 6.8 %collective-permute-start.5 = (bf16[80,512]{1,0:T(8,128)(2,1)S(1)}, bf16[80,512]{1,0:T(8,128)(2,1)S(1)}, u32[]{:S(2)}, u32[]{:S(2)}) collective-permute-start(bf16[80,512]{1,0:T(8,128)(2,1)S(1)} %get-tuple-element.43), channel_id=1, source_target_pairs={{0,8},{1,9},{2,10},{3,11},{4,12},{5,13},{6,14},{7,15},{8,16},{9,17... | collective-permute-start | bytes 245768 | tf_op jit(solution)/shard_map/ppermute | solution.py:40
  39.8 6.7 %collective-permute-start.4 = (bf16[80,512]{1,0:T(8,128)(2,1)S(1)}, bf16[80,512]{1,0:T(8,128)(2,1)S(1)}, u32[]{:S(2)}, u32[]{:S(2)}) collective-permute-start(bf16[80,512]{1,0:T(8,128)(2,1)S(1)} %get-tuple-element.43), channel_id=1, source_target_pairs={{0,120},{1,121},{2,122},{3,123},{4,124},{5,125},{6,126},{7,127},{8... | collective-permute-start | bytes 245768 | tf_op jit(solution)/shard_map/ppermute | solution.py:40
  44.8 4.1 %collective-permute-start.6 = (bf16[16,512]{1,0:T(8,128)(2,1)S(1)}, bf16[16,512]{1,0:T(8,128)(2,1)S(1)}, u32[]{:S(2)}, u32[]{:S(2)}) collective-permute-start(bf16[16,512]{1,0:T(8,128)(2,1)S(1)} %get-tuple-element.44), channel_id=1, source_target_pairs={{0,16},{1,17},{2,18},{3,19},{4,20},{5,21},{6,22},{7,23},{8,24},{9,... | collective-permute-start | bytes 49160 | tf_op jit(solution)/shard_map/ppermute | solution.py:40
  48.9 3.1 %collective-permute-start.9 = (bf16[64,512]{1,0:T(8,128)(2,1)S(1)}, bf16[64,512]{1,0:T(8,128)(2,1)S(1)}, u32[]{:S(2)}, u32[]{:S(2)}) collective-permute-start(bf16[64,512]{1,0:T(8,128)(2,1)S(1)} %pad_maximum_fusion.1), channel_id=1, source_target_pairs={{0,2},{1,3},{2,4},{3,5},{4,6},{5,7},{6,0},{7,1},{8,10},{9,11},{10,... | collective-permute-start | bytes 196616 | tf_op jit(solution)/shard_map/ppermute | solution.py:40
  48.9 4.7 %collective-permute-start.8 = (bf16[64,512]{1,0:T(8,128)(2,1)S(1)}, bf16[64,512]{1,0:T(8,128)(2,1)S(1)}, u32[]{:S(2)}, u32[]{:S(2)}) collective-permute-start(bf16[64,512]{1,0:T(8,128)(2,1)S(1)} %pad_maximum_fusion.1), channel_id=1, source_target_pairs={{0,4},{1,5},{2,6},{3,7},{4,0},{5,1},{6,2},{7,3},{8,12},{9,13},{10,... | collective-permute-start | bytes 196616 | tf_op jit(solution)/shard_map/ppermute | solution.py:40
  51.1 4.9 %collective-permute-start.7 = (bf16[64,512]{1,0:T(8,128)(2,1)S(1)}, bf16[64,512]{1,0:T(8,128)(2,1)S(1)}, u32[]{:S(2)}, u32[]{:S(2)}) collective-permute-start(bf16[64,512]{1,0:T(8,128)(2,1)S(1)} %pad_maximum_fusion.1), channel_id=1, source_target_pairs={{0,6},{1,7},{2,0},{3,1},{4,2},{5,3},{6,4},{7,5},{8,14},{9,15},{10,... | collective-permute-start | bytes 196616 | tf_op jit(solution)/shard_map/ppermute | solution.py:40
  56.0 9.9 %collective-permute-start.11 = (bf16[256,512]{1,0:T(8,128)(2,1)S(1)}, bf16[256,512]{1,0:T(8,128)(2,1)S(1)}, u32[]{:S(2)}, u32[]{:S(2)}) collective-permute-start(bf16[256,512]{1,0:T(8,128)(2,1)S(1)} %constant_dynamic-update-slice_fusion.refs_3_), channel_id=1, source_target_pairs={{0,32},{1,33},{2,34},{3,35},{4,36},{5,37},{6,38},{7,39},{8,40},{9,... | collective-permute-start | bytes 786440 | tf_op jit(solution)/shard_map/ppermute | solution.py:40
  56.1 9.8 %collective-permute-start.10 = (bf16[256,512]{1,0:T(8,128)(2,1)S(1)}, bf16[256,512]{1,0:T(8,128)(2,1)S(1)}, u32[]{:S(2)}, u32[]{:S(2)}) collective-permute-start(bf16[256,512]{1,0:T(8,128)(2,1)S(1)} %constant_dynamic-update-slice_fusion.refs_3_), channel_id=1, source_target_pairs={{0,96},{1,97},{2,98},{3,99},{4,100},{5,101},{6,102},{7,103},{8,104... | collective-permute-start | bytes 786440 | tf_op jit(solution)/shard_map/ppermute | solution.py:40
  66.0 4.9 %collective-permute-start.12 = (bf16[128,512]{1,0:T(8,128)(2,1)S(1)}, bf16[128,512]{1,0:T(8,128)(2,1)S(1)}, u32[]{:S(2)}, u32[]{:S(2)}) collective-permute-start(bf16[128,512]{1,0:T(8,128)(2,1)S(1)} %slice.52), channel_id=1, source_target_pairs={{0,96},{1,97},{2,98},{3,99},{4,100},{5,101},{6,102},{7,103},{8,104... | collective-permute-start | bytes 393224 | tf_op jit(solution)/shard_map/ppermute | solution.py:40
  66.1 7.2 %collective-permute-start.13 = (bf16[128,512]{1,0:T(8,128)(2,1)S(1)}, bf16[128,512]{1,0:T(8,128)(2,1)S(1)}, u32[]{:S(2)}, u32[]{:S(2)}) collective-permute-start(bf16[128,512]{1,0:T(8,128)(2,1)S(1)} %slice.53), channel_id=1, source_target_pairs={{0,32},{1,33},{2,34},{3,35},{4,36},{5,37},{6,38},{7,39},{8,40},{9,... | collective-permute-start | bytes 393224 | tf_op jit(solution)/shard_map/ppermute | solution.py:40
  67.5 7.7 %collective-permute-start.20 = (bf16[192,512]{1,0:T(8,128)(2,1)S(1)}, bf16[192,512]{1,0:T(8,128)(2,1)S(1)}, u32[]{:S(2)}, u32[]{:S(2)}) collective-permute-start(bf16[192,512]{1,0:T(8,128)(2,1)S(1)} %pad_maximum_fusion), channel_id=1, source_target_pairs={{0,1},{1,0},{2,3},{3,2},{4,5},{5,4},{6,7},{7,6},{8,9},{9,8},{10,11... | collective-permute-start | bytes 589832 | tf_op jit(solution)/shard_map/ppermute | solution.py:40
  70.6 6.3 %collective-permute-start.19 = (bf16[192,512]{1,0:T(8,128)(2,1)S(1)}, bf16[192,512]{1,0:T(8,128)(2,1)S(1)}, u32[]{:S(2)}, u32[]{:S(2)}) collective-permute-start(bf16[192,512]{1,0:T(8,128)(2,1)S(1)} %pad_maximum_fusion), channel_id=1, source_target_pairs={{0,7},{1,2},{2,1},{3,4},{4,3},{5,6},{6,5},{7,0},{8,15},{9,10},{10,... | collective-permute-start | bytes 589832 | tf_op jit(solution)/shard_map/ppermute | solution.py:40
  70.9 6.1 %collective-permute-start.14 = (bf16[256,512]{1,0:T(8,128)(2,1)S(1)}, bf16[256,512]{1,0:T(8,128)(2,1)S(1)}, u32[]{:S(2)}, u32[]{:S(2)}) collective-permute-start(bf16[256,512]{1,0:T(8,128)(2,1)S(1)} %constant_dynamic-update-slice_fusion.refs_3_), channel_id=1, source_target_pairs={{0,1},{1,0},{2,3},{3,2},{4,5},{5,4},{6,7},{7,6},{8,9},{9,8},{10,11... | collective-permute-start | bytes 786440 | tf_op jit(solution)/shard_map/ppermute | solution.py:40
  70.9 7.4 %collective-permute-start.15 = (bf16[256,512]{1,0:T(8,128)(2,1)S(1)}, bf16[256,512]{1,0:T(8,128)(2,1)S(1)}, u32[]{:S(2)}, u32[]{:S(2)}) collective-permute-start(bf16[256,512]{1,0:T(8,128)(2,1)S(1)} %collective-permute-done.11.refs_4_), channel_id=1, source_target_pairs={{0,1},{1,0},{2,3},{3,2},{4,5},{5,4},{6,7},{7,6},{8,9},{9,8},{10,11... | collective-permute-start | bytes 786440 | tf_op jit(solution)/shard_map/ppermute | solution.py:40
  73.3 5.0 %collective-permute-start.16 = (bf16[256,512]{1,0:T(8,128)(2,1)S(1)}, bf16[256,512]{1,0:T(8,128)(2,1)S(1)}, u32[]{:S(2)}, u32[]{:S(2)}) collective-permute-start(bf16[256,512]{1,0:T(8,128)(2,1)S(1)} %collective-permute-done.10.refs_5_), channel_id=1, source_target_pairs={{0,1},{1,0},{2,3},{3,2},{4,5},{5,4},{6,7},{7,6},{8,9},{9,8},{10,11... | collective-permute-start | bytes 786440 | tf_op jit(solution)/shard_map/ppermute | solution.py:40
  75.3 1.7 %collective-permute-start.17 = (bf16[128,512]{1,0:T(8,128)(2,1)S(1)}, bf16[128,512]{1,0:T(8,128)(2,1)S(1)}, u32[]{:S(2)}, u32[]{:S(2)}) collective-permute-start(bf16[128,512]{1,0:T(8,128)(2,1)S(1)} %collective-permute-done.13.refs_6_), channel_id=1, source_target_pairs={{0,1},{1,0},{2,3},{3,2},{4,5},{5,4},{6,7},{7,6},{8,9},{9,8},{10,11... | collective-permute-start | bytes 393224 | tf_op jit(solution)/shard_map/ppermute | solution.py:40
  76.9 1.3 %collective-permute-start.18 = (bf16[128,512]{1,0:T(8,128)(2,1)S(1)}, bf16[128,512]{1,0:T(8,128)(2,1)S(1)}, u32[]{:S(2)}, u32[]{:S(2)}) collective-permute-start(bf16[128,512]{1,0:T(8,128)(2,1)S(1)} %collective-permute-done.12.refs_7_), channel_id=1, source_target_pairs={{0,1},{1,0},{2,3},{3,2},{4,5},{5,4},{6,7},{7,6},{8,9},{9,8},{10,11... | collective-permute-start | bytes 393224 | tf_op jit(solution)/shard_map/ppermute | solution.py:40
  78.3 31.5 %copy-start = (bf16[7,512,512]{2,1,0:T(8,128)(2,1)S(1)}, bf16[7,512,512]{2,1,0:T(8,128)(2,1)}, u32[]{:S(2)}) copy-start(bf16[7,512,512]{2,1,0:T(8,128)(2,1)} %w6.1) | copy-start | bytes 11010052
  78.3 31.5 %copy-start.1 = (bf16[1024,512]{1,0:T(8,128)(2,1)S(1)}, bf16[1024,512]{1,0:T(8,128)(2,1)}, u32[]{:S(2)}) copy-start(bf16[1024,512]{1,0:T(8,128)(2,1)} %get-tuple-element.50.cells) | copy-start | bytes 3145732
  78.3 31.5 %copy-start.2 = (s32[3,4,256]{2,1,0:T(4,128)S(1)}, s32[3,4,256]{2,1,0:T(4,128)}, u32[]{:S(2)}) copy-start(s32[3,4,256]{2,1,0:T(4,128)} %snd.3) | copy-start | bytes 36868
  78.3 31.5 %copy-start.3 = (bf16[3,4,256,512]{3,2,1,0:T(8,128)(2,1)S(1)}, bf16[3,4,256,512]{3,2,1,0:T(8,128)(2,1)}, u32[]{:S(2)}) copy-start(bf16[3,4,256,512]{3,2,1,0:T(8,128)(2,1)} %get-tuple-element.53.lead) | copy-start | bytes 9437188
  78.3 31.5 %copy-start.4 = (f32[1024,512]{1,0:T(8,128)S(1)}, f32[1024,512]{1,0:T(8,128)}, u32[]{:S(2)}) copy-start(f32[1024,512]{1,0:T(8,128)} %get-tuple-element.70.self_part) | copy-start | bytes 6291460
  95.5 6.9 %collective-permute-start.21 = (bf16[64,512]{1,0:T(8,128)(2,1)S(1)}, bf16[64,512]{1,0:T(8,128)(2,1)S(1)}, u32[]{:S(2)}, u32[]{:S(2)}) collective-permute-start(bf16[64,512]{1,0:T(8,128)(2,1)S(1)} %get-tuple-element.66), channel_id=1, source_target_pairs={{0,8},{1,9},{2,10},{3,11},{4,12},{5,13},{6,14},{7,15},{8,16},{9,17... | collective-permute-start | bytes 196616 | tf_op jit(solution)/shard_map/ppermute | solution.py:40
  95.5 6.9 %collective-permute-start.22 = (bf16[64,512]{1,0:T(8,128)(2,1)S(1)}, bf16[64,512]{1,0:T(8,128)(2,1)S(1)}, u32[]{:S(2)}, u32[]{:S(2)}) collective-permute-start(bf16[64,512]{1,0:T(8,128)(2,1)S(1)} %get-tuple-element.66), channel_id=1, source_target_pairs={{0,120},{1,121},{2,122},{3,123},{4,124},{5,125},{6,126},{7,127},{8... | collective-permute-start | bytes 196616 | tf_op jit(solution)/shard_map/ppermute | solution.py:40
  102.5 2.1 %collective-permute-start.24 = (bf16[192,512]{1,0:T(8,128)(2,1)S(1)}, bf16[192,512]{1,0:T(8,128)(2,1)S(1)}, u32[]{:S(2)}, u32[]{:S(2)}) collective-permute-start(bf16[192,512]{1,0:T(8,128)(2,1)S(1)} %constant_dynamic-update-slice_fusion.7), channel_id=1, source_target_pairs={{0,1},{1,0},{2,3},{3,2},{4,5},{5,4},{6,7},{7,6},{8,9},{9,8},{10,11... | collective-permute-start | bytes 589832 | tf_op jit(solution)/shard_map/ppermute | solution.py:40
  103.5 6.3 %collective-permute-start.23 = (bf16[192,512]{1,0:T(8,128)(2,1)S(1)}, bf16[192,512]{1,0:T(8,128)(2,1)S(1)}, u32[]{:S(2)}, u32[]{:S(2)}) collective-permute-start(bf16[192,512]{1,0:T(8,128)(2,1)S(1)} %constant_dynamic-update-slice_fusion.7), channel_id=1, source_target_pairs={{0,7},{1,2},{2,1},{3,4},{4,3},{5,6},{6,5},{7,0},{8,15},{9,10},{10,... | collective-permute-start | bytes 589832 | tf_op jit(solution)/shard_map/ppermute | solution.py:40

commit v4 on v3

--- a/solution.py
+++ b/solution.py
@@ -82,6 +82,11 @@
 
 def stay(values):
     return pltpu.with_memory_space_constraint(values, pltpu.HBM)
+
+
+def fetch_rows(fetch, source, target, rows=256):
+    parts = [pl.ds(at, rows) for at in range(0, source.shape[0], rows)]
+    return [fetch(source.at[part], target.at[part]) for part in parts]
 
 
 class Fetched:
@@ -223,12 +228,10 @@
     sides = [fetch(v, side_v.at[pl.ds(16 * k, 16)]) for k, v in enumerate((west, east))]
     mesh = fetch(mesh_ref, mesh_v)
     w1 = fetch(enc_w.at[1], weights.at[1])
-    mine = fetch(own, table.at[pl.ds(512, 1024)])
+    mine = fetch_rows(fetch, own, table.at[pl.ds(512, 1024)])
     w2, w3 = (fetch(enc_w.at[k], weights.at[k]) for k in (2, 3))
     feats = [fetch(snd, index.at[0]), fetch(rcv, index.at[1]), fetch(live, live_v)]
-    for k in range(steps):
-        rows = pl.ds(k * EDGE_BLOCK, EDGE_BLOCK)
-        feats.append(fetch(feat.at[rows], feat_v.at[rows]))
+    feats += fetch_rows(fetch, feat, feat_v)
     w4, w5, w6 = (fetch(enc_w.at[k], weights.at[k]) for k in (4, 5, 6))
     p0, p1 = (fetch(proc_w.at[k], weights.at[7 + k]) for k in (0, 1))
 
@@ -238,7 +241,8 @@
     sides[0](), sides[1]()
     table[2048:2080] = dot(side_v[...], w0()[...]).astype(BF16)
     table[2176:2432] = dot(mesh()[...], w1()[...]).astype(BF16)
-    mine()
+    for ready in mine:
+        ready()
     for ready in (w2, w3, *feats):
         ready()
     alive = live_v[0:1, 0:1]
@@ -280,7 +284,7 @@
             pltpu.VMEM((9, D, D), BF16),
             pltpu.VMEM((2, *senders.shape), jnp.int32),
             pltpu.VMEM((8, 128), jnp.int32),
-            pltpu.SemaphoreType.DMA((21,)),
+            pltpu.SemaphoreType.DMA((32,)),
         ],
         compiler_params=pltpu.CompilerParams(vmem_limit_bytes=36 << 20),
         cost_estimate=cost(25000, 10 << 20),
@@ -305,11 +309,11 @@
         return Fetched(source, target, sems.at[next(count)])
 
     places = COARSE + tuple((at + 1024, rows) for at, rows in COARSE) + NEAR
-    first = [fetch(recv, table.at[pl.ds(2816, 256)])]
+    first = [fetch(snd, index.at[0]), fetch(rcv, index.at[1]), fetch(recv, table.at[pl.ds(2816, 256)])]
+    first += [fetch(proc_w.at[k], weights.at[k - 2]) for k in (2, 3)]
+    first += fetch_rows(fetch, feat, feat_v)
     for piece, (at, rows) in zip(pieces, places):
         first.append(fetch(piece.at[pl.ds(0, rows)], table.at[pl.ds(at, rows)]))
-    first += [fetch(proc_w.at[k], weights.at[k - 2]) for k in (2, 3)]
-    first += [fetch(feat, feat_v), fetch(snd, index.at[0]), fetch(rcv, index.at[1])]
     mesh = fetch(mesh_ref, mesh_v)
     w4, w5, w6 = (fetch(proc_w.at[k], weights.at[k - 2]) for k in (4, 5, 6))
     d0 = fetch(dec_w.at[0], weights.at[5])
@@ -344,7 +348,7 @@
             pltpu.VMEM((256, D), BF16),
             pltpu.VMEM((6, D, D), BF16),
             pltpu.VMEM((2, *senders.shape), jnp.int32),
-            pltpu.SemaphoreType.DMA((26,)),
+            pltpu.SemaphoreType.DMA((34,)),
         ],
         compiler_params=pltpu.CompilerParams(vmem_limit_bytes=36 << 20),
         cost_estimate=cost(25000, 10 << 20),

time: 122 us -> 120 us (0.984)
  Pallas kernels: 55.6 us -> 53.6 us
    pallas_call x1, Pallas kernels: 17.1 us -> 15.1 us  [proc_kernel(): pl.pallas_call(proc_body, in_specs=[HBM] * 3 + [ANY] * 15 + [HBM] * 4, ou...]
where the time goes in v4:
time: 120 us; the launch traced here: 119 us
  Pallas kernels  53.6 us (45%)
  starting transfers between devices  32.9 us (27%)
  waiting for transfers between devices  29.1 us (24%)
  local copies, waits for them, and re-layouts  3.56 us (3%)
    ppermute x25, starting transfers between devices, send(): return lax.ppermute(values, AXES, pairs)  32.9 us
    ppermute x25, waiting for transfers between devices, send(): return lax.ppermute(values, AXES, pairs)  29.1 us
    pallas_call x1, Pallas kernels, proc_kernel(): pl.pallas_call(proc_body, in_specs=[HBM] * 3 + [ANY] * 15 + [HBM] * 4, ou...  15.1 us
    pallas_call x1, Pallas kernels, enc_kernel(): pl.pallas_call(enc_body, in_specs=[HBM] * 5 + [ANY] * 4 + [HBM] * 3, out_...  14.7 us
    pallas_call x1, Pallas kernels, dec_kernel(): pl.pallas_call(dec_body, grid=(lat,), in_specs=[whole(senders.shape), pl....  11.7 us
    pallas_call x1, Pallas kernels, lead_kernel(): pl.pallas_call(lead_body, grid=(lat,), in_specs=[edges, blk, weight(1), w...  7.15 us
    pallas_call x1, Pallas kernels, grid_kernel(): pl.pallas_call(grid_body, grid=(2,), in_specs=[SMEM, blk, weight(0), weig...  4.95 us
  transfers between devices with their start and end apart: 25, of which 13 were waited for; matrix products, arithmetic and copies ran while one was open for 2% of the time, Pallas kernels for 10%

profile of v4, /device:TPU:7, one launch (start us, length us, event | category | flops | bytes accessed | tf_op | source)
XLA Modules:
  0.0 119.5 jit_solution(6143974023633812578)
XLA Ops:
  0.0 1.3 %fusion.1 = (bf16[2,256,512]{2,1,0:T(8,128)(2,1)S(1)}, bf16[2,256,512]{2,1,0:T(8,128)(2,1)S(1)}) fusion(bf16[4,256,512]{2,1,0:T(8,128)(2,1)} %param.14), kind=kLoop, calls=%fused_computation.15 | loop fusion | bytes 2097152 | tf_op jit(solution)/shard_map/slice | solution.py:456
  1.3 1.7 %collective-permute-start.1 = (bf16[2,256,512]{2,1,0:T(8,128)(2,1)S(1)}, bf16[2,256,512]{2,1,0:T(8,128)(2,1)S(1)}, u32[]{:S(2)}, u32[]{:S(2)}) collective-permute-start(bf16[2,256,512]{2,1,0:T(8,128)(2,1)S(1)} %get-tuple-element.73), channel_id=1, source_target_pairs={{0,8},{1,9},{2,10},{3,11},{4,12},{5,13},{6,14},{7,15},{8,16},{9,17... | collective-permute-start | bytes 1572872 | tf_op jit(solution)/shard_map/ppermute | solution.py:40
  3.0 4.7 %collective-permute-start = (bf16[2,256,512]{2,1,0:T(8,128)(2,1)S(1)}, bf16[2,256,512]{2,1,0:T(8,128)(2,1)S(1)}, u32[]{:S(2)}, u32[]{:S(2)}) collective-permute-start(bf16[2,256,512]{2,1,0:T(8,128)(2,1)S(1)} %get-tuple-element.74), channel_id=1, source_target_pairs={{0,120},{1,121},{2,122},{3,123},{4,124},{5,125},{6,126},{7,127},{8... | collective-permute-start | bytes 1572872 | tf_op jit(solution)/shard_map/ppermute | solution.py:40
  7.6 1.4 %copy.35.blocks = s32[16,8]{1,0:T(8,128)} copy(s32[16,8]{0,1:T(8,128)} %param.19) | data formatting | bytes 1024 | tf_op args[5]
  9.0 0.8 fusion
  9.8 4.9 %grid_cells.1 = (bf16[1024,512]{1,0:T(8,128)(2,1)}, bf16[1024,512]{1,0:T(8,128)(2,1)}, s32[8,128]{1,0:T(8,128)}) custom-call(s32[16,8]{1,0:T(8,128)} %copy.35.blocks, bf16[1024,512]{1,0:T(8,128)(2,1)} %bitcast.9, bf16[9,512,512]{2,1,0:T(8,128)(2,1)} %enc_w.1, bf16[9,512,512]{2,1,0:T(8,128)(2,1)} %enc_w.1, bf16[9,512,512]{2,1,0:T(8,128)(2,1)} %enc_w.1), custom_call_target="tpu_custom_call" | custom-call | flops 2621440000 | bytes 5242880 | tf_op jit(solution)/shard_map/grid_cells/pallas_call | solution.py:164
  14.7 4.5 %collective-permute-done.1 = bf16[2,256,512]{2,1,0:T(8,128)(2,1)S(1)} collective-permute-done((bf16[2,256,512]{2,1,0:T(8,128)(2,1)S(1)}, bf16[2,256,512]{2,1,0:T(8,128)(2,1)S(1)}, u32[]{:S(2)}, u32[]{:S(2)}) %collective-permute-start.1) | collective-permute-done | bytes 524320 | tf_op jit(solution)/shard_map/ppermute | solution.py:40
  19.3 1.3 %collective-permute-start.2 = (bf16[16,512]{1,0:T(8,128)(2,1)S(1)}, bf16[16,512]{1,0:T(8,128)(2,1)S(1)}, u32[]{:S(2)}, u32[]{:S(2)}) collective-permute-start(bf16[16,512]{1,0:T(8,128)(2,1)S(1)} %reshape.31), channel_id=1, source_target_pairs={{0,1},{1,2},{2,3},{3,4},{4,5},{5,6},{6,7},{7,0},{8,9},{9,10},{10,1... | collective-permute-start | bytes 49160 | tf_op jit(solution)/shard_map/ppermute | solution.py:40
  20.7 0.0 collective-permute-start.3
  20.7 0.9 collective-permute-done.2.west
  21.5 3.5 %collective-permute-done.3.east = bf16[16,512]{1,0:T(8,128)(2,1)S(1)} collective-permute-done((bf16[16,512]{1,0:T(8,128)(2,1)S(1)}, bf16[16,512]{1,0:T(8,128)(2,1)S(1)}, u32[]{:S(2)}, u32[]{:S(2)}) %collective-permute-start.3) | collective-permute-done | bytes 16416 | tf_op jit(solution)/shard_map/ppermute | solution.py:40
  25.0 14.7 %encoder_edges.1 = (bf16[256,512]{1,0:T(8,128)(2,1)S(1)}, bf16[256,512]{1,0:T(8,128)(2,1)S(1)}, bf16[256,512]{1,0:T(8,128)(2,1)S(1)}, bf16[80,512]{1,0:T(8,128)(...) custom-call(s32[8,128]{1,0:T(8,128)} %get-tuple-element.38.live, s32[1,1,2048]{2,1,0:T(1,128)} %snd.2, ...), custom_call_target="tpu_custom_call" | custom-call | flops 13107200000 | bytes 10485760 | tf_op jit(solution)/shard_map/encoder_edges/pallas_call | solution.py:272
  39.8 0.0 copy-start.6
  39.8 0.1 collective-permute-start.5
  39.9 5.0 %collective-permute-start.4 = (bf16[80,512]{1,0:T(8,128)(2,1)S(1)}, bf16[80,512]{1,0:T(8,128)(2,1)S(1)}, u32[]{:S(2)}, u32[]{:S(2)}) collective-permute-start(bf16[80,512]{1,0:T(8,128)(2,1)S(1)} %get-tuple-element.43), channel_id=1, source_target_pairs={{0,120},{1,121},{2,122},{3,123},{4,124},{5,125},{6,126},{7,127},{8... | collective-permute-start | bytes 245768 | tf_op jit(solution)/shard_map/ppermute | solution.py:40
  44.8 0.0 collective-permute-start.6
  44.8 1.7 %collective-permute-done.5.refs_13_ = bf16[80,512]{1,0:T(8,128)(2,1)S(1)} collective-permute-done((bf16[80,512]{1,0:T(8,128)(2,1)S(1)}, bf16[80,512]{1,0:T(8,128)(2,1)S(1)}, u32[]{:S(2)}, u32[]{:S(2)}) %collective-permute-start.5) | collective-permute-done | bytes 81952 | tf_op jit(solution)/shard_map/ppermute | solution.py:40
  46.6 0.0 collective-permute-done.4.refs_15_
  46.6 2.3 %collective-permute-done.6 = bf16[16,512]{1,0:T(8,128)(2,1)S(1)} collective-permute-done((bf16[16,512]{1,0:T(8,128)(2,1)S(1)}, bf16[16,512]{1,0:T(8,128)(2,1)S(1)}, u32[]{:S(2)}, u32[]{:S(2)}) %collective-permute-start.6) | collective-permute-done | bytes 16416 | tf_op jit(solution)/shard_map/ppermute | solution.py:40
  48.9 0.0 collective-permute-start.9
  48.9 2.2 %collective-permute-start.8 = (bf16[64,512]{1,0:T(8,128)(2,1)S(1)}, bf16[64,512]{1,0:T(8,128)(2,1)S(1)}, u32[]{:S(2)}, u32[]{:S(2)}) collective-permute-start(bf16[64,512]{1,0:T(8,128)(2,1)S(1)} %pad_maximum_fusion.1), channel_id=1, source_target_pairs={{0,4},{1,5},{2,6},{3,7},{4,0},{5,1},{6,2},{7,3},{8,12},{9,13},{10,... | collective-permute-start | bytes 196616 | tf_op jit(solution)/shard_map/ppermute | solution.py:40
  51.1 0.0 collective-permute-start.7
  51.1 0.9 collective-permute-done.9
  52.0 1.6 %collective-permute-done.8 = bf16[64,512]{1,0:T(8,128)(2,1)S(1)} collective-permute-done((bf16[64,512]{1,0:T(8,128)(2,1)S(1)}, bf16[64,512]{1,0:T(8,128)(2,1)S(1)}, u32[]{:S(2)}, u32[]{:S(2)}) %collective-permute-start.8) | collective-permute-done | bytes 65568 | tf_op jit(solution)/shard_map/ppermute | solution.py:40
  53.6 2.3 %collective-permute-done.7 = bf16[64,512]{1,0:T(8,128)(2,1)S(1)} collective-permute-done((bf16[64,512]{1,0:T(8,128)(2,1)S(1)}, bf16[64,512]{1,0:T(8,128)(2,1)S(1)}, u32[]{:S(2)}, u32[]{:S(2)}) %collective-permute-start.7) | collective-permute-done | bytes 65568 | tf_op jit(solution)/shard_map/ppermute | solution.py:40
  56.0 0.1 collective-permute-start.11
  56.1 2.7 %collective-permute-start.10 = (bf16[256,512]{1,0:T(8,128)(2,1)S(1)}, bf16[256,512]{1,0:T(8,128)(2,1)S(1)}, u32[]{:S(2)}, u32[]{:S(2)}) collective-permute-start(bf16[256,512]{1,0:T(8,128)(2,1)S(1)} %constant_dynamic-update-slice_fusion.refs_3_), channel_id=1, source_target_pairs={{0,96},{1,97},{2,98},{3,99},{4,100},{5,101},{6,102},{7,103},{8,104... | collective-permute-start | bytes 786440 | tf_op jit(solution)/shard_map/ppermute | solution.py:40
  58.7 7.1 %decoder_lead.1 = (bf16[3,4,256,512]{3,2,1,0:T(8,128)(2,1)}, f32[1024,512]{1,0:T(8,128)}) custom-call(bf16[3,4,256,512]{3,2,1,0:T(8,128)(2,1)} %feat.1, bf16[1024,512]{1,0:T(8,128)(2,1)} %get-tuple-element.50.cells, bf16[7,512,512]{2,1,0:T(8,128)(2,1)} %w6.1, bf16[7,512,512]{2,1,0:T(8,128)(2,1)} %w6.1, bf16[7,512,512]{2,1,0:T(8,128)(2,1)} %w6.1), custom_call_target="tpu_custom_call" | custom-call | flops 4194304000 | bytes 10485760 | tf_op jit(solution)/shard_map/decoder_lead/pallas_call | solution.py:189
  65.9 0.0 collective-permute-done.11.refs_4_
  65.9 0.1 collective-permute-start.12
  66.0 1.5 %collective-permute-start.13 = (bf16[128,512]{1,0:T(8,128)(2,1)S(1)}, bf16[128,512]{1,0:T(8,128)(2,1)S(1)}, u32[]{:S(2)}, u32[]{:S(2)}) collective-permute-start(bf16[128,512]{1,0:T(8,128)(2,1)S(1)} %slice.53), channel_id=1, source_target_pairs={{0,32},{1,33},{2,34},{3,35},{4,36},{5,37},{6,38},{7,39},{8,40},{9,... | collective-permute-start | bytes 393224 | tf_op jit(solution)/shard_map/ppermute | solution.py:40
  67.5 3.1 %collective-permute-start.20 = (bf16[192,512]{1,0:T(8,128)(2,1)S(1)}, bf16[192,512]{1,0:T(8,128)(2,1)S(1)}, u32[]{:S(2)}, u32[]{:S(2)}) collective-permute-start(bf16[192,512]{1,0:T(8,128)(2,1)S(1)} %pad_maximum_fusion), channel_id=1, source_target_pairs={{0,1},{1,0},{2,3},{3,2},{4,5},{5,4},{6,7},{7,6},{8,9},{9,8},{10,11... | collective-permute-start | bytes 589832 | tf_op jit(solution)/shard_map/ppermute | solution.py:40
  70.6 0.3 collective-permute-start.19
  70.9 2.4 %collective-permute-start.15 = (bf16[256,512]{1,0:T(8,128)(2,1)S(1)}, bf16[256,512]{1,0:T(8,128)(2,1)S(1)}, u32[]{:S(2)}, u32[]{:S(2)}) collective-permute-start(bf16[256,512]{1,0:T(8,128)(2,1)S(1)} %collective-permute-done.11.refs_4_), channel_id=1, source_target_pairs={{0,1},{1,0},{2,3},{3,2},{4,5},{5,4},{6,7},{7,6},{8,9},{9,8},{10,11... | collective-permute-start | bytes 786440 | tf_op jit(solution)/shard_map/ppermute | solution.py:40
  73.3 1.9 %collective-permute-start.16 = (bf16[256,512]{1,0:T(8,128)(2,1)S(1)}, bf16[256,512]{1,0:T(8,128)(2,1)S(1)}, u32[]{:S(2)}, u32[]{:S(2)}) collective-permute-start(bf16[256,512]{1,0:T(8,128)(2,1)S(1)} %collective-permute-done.10.refs_5_), channel_id=1, source_target_pairs={{0,1},{1,0},{2,3},{3,2},{4,5},{5,4},{6,7},{7,6},{8,9},{9,8},{10,11... | collective-permute-start | bytes 786440 | tf_op jit(solution)/shard_map/ppermute | solution.py:40
  75.2 0.0 collective-permute-start.17
  75.2 1.7 %collective-permute-done.19.refs_17_ = bf16[192,512]{1,0:T(8,128)(2,1)S(1)} collective-permute-done((bf16[192,512]{1,0:T(8,128)(2,1)S(1)}, bf16[192,512]{1,0:T(8,128)(2,1)S(1)}, u32[]{:S(2)}, u32[]{:S(2)}) %collective-permute-start.19) | collective-permute-done | bytes 196640 | tf_op jit(solution)/shard_map/ppermute | solution.py:40
  77.0 1.3 %collective-permute-done.18.refs_12_ = bf16[128,512]{1,0:T(8,128)(2,1)S(1)} collective-permute-done((bf16[128,512]{1,0:T(8,128)(2,1)S(1)}, bf16[128,512]{1,0:T(8,128)(2,1)S(1)}, u32[]{:S(2)}, u32[]{:S(2)}) %collective-permute-start.18) | collective-permute-done | bytes 131104 | tf_op jit(solution)/shard_map/ppermute | solution.py:40
  78.3 0.0 copy-start.2
  78.3 15.1 %mesh_edges.1 = (bf16[256,512]{1,0:T(8,128)(2,1)S(1)}, bf16[64,512]{1,0:T(8,128)(2,1)S(1)}) custom-call(s32[1,1,2048]{2,1,0:T(1,128)} %refs_0_.1, s32[1,1,2048]{2,1,0:T(1,128)} %refs_1_.1, bf16[2048,512]{1,0:T(8,128)(2,1)} %bitcast.11, bf16[256,512]{1,0:T(8,128)(2,1)S(1)} %constant_dynamic-update-slice_fusion.refs_3_, ...), custom_call_target="tpu_custom_call" | custom-call | flops 13107200000 | bytes 10485760 | tf_op jit(solution)/shard_map/mesh_edges/pallas_call | solution.py:340
  93.5 0.1 collective-permute-start.21
  93.5 4.8 %collective-permute-start.22 = (bf16[64,512]{1,0:T(8,128)(2,1)S(1)}, bf16[64,512]{1,0:T(8,128)(2,1)S(1)}, u32[]{:S(2)}, u32[]{:S(2)}) collective-permute-start(bf16[64,512]{1,0:T(8,128)(2,1)S(1)} %get-tuple-element.66), channel_id=1, source_target_pairs={{0,120},{1,121},{2,122},{3,123},{4,124},{5,125},{6,126},{7,127},{8... | collective-permute-start | bytes 196616 | tf_op jit(solution)/shard_map/ppermute | solution.py:40
  98.3 2.1 %collective-permute-done.21.above = bf16[64,512]{1,0:T(8,128)(2,1)S(1)} collective-permute-done((bf16[64,512]{1,0:T(8,128)(2,1)S(1)}, bf16[64,512]{1,0:T(8,128)(2,1)S(1)}, u32[]{:S(2)}, u32[]{:S(2)}) %collective-permute-start.21) | collective-permute-done | bytes 65568 | tf_op jit(solution)/shard_map/ppermute | solution.py:40
  100.4 1.0 collective-permute-start.24
  101.5 0.1 collective-permute-start.23
  101.6 1.0 collective-permute-done.24.beside
  102.5 5.2 %collective-permute-done.23.across = bf16[192,512]{1,0:T(8,128)(2,1)S(1)} collective-permute-done((bf16[192,512]{1,0:T(8,128)(2,1)S(1)}, bf16[192,512]{1,0:T(8,128)(2,1)S(1)}, u32[]{:S(2)}, u32[]{:S(2)}) %collective-permute-start.23) | collective-permute-done | bytes 196640 | tf_op jit(solution)/shard_map/ppermute | solution.py:40
  107.8 11.7 %decoder_edges.1 = bf16[1024,512]{1,0:T(8,128)(2,1)} custom-call(s32[3,4,256]{2,1,0:T(4,128)S(1)} %copy-done.2, bf16[3,4,256,512]{3,2,1,0:T(8,128)(2,1)S(1)} %copy-done.3, bf16[64,512]{1,0:T(8,128)(2,1)S(1)} %collective-permute-done.21.above, bf16[256,512]{1,0:T(8,128)(2,1)S(1)} %get-tuple-element.67.own, bf16[64,512]{1,0:T(8,128)(2,1)S(1)} %collective-permute-done.22.below, ...), custom_call_target="tpu_custom_call" | custom-call | flops 7864320000 | bytes 9437184 | tf_op jit(solution)/shard_map/decoder_edges/pallas_call | solution.py:387
  (45 shorter events, 0.3 us)
Async XLA Ops:
  1.3 17.9 %collective-permute-start.1 = (bf16[2,256,512]{2,1,0:T(8,128)(2,1)S(1)}, bf16[2,256,512]{2,1,0:T(8,128)(2,1)S(1)}, u32[]{:S(2)}, u32[]{:S(2)}) collective-permute-start(bf16[2,256,512]{2,1,0:T(8,128)(2,1)S(1)} %get-tuple-element.73), channel_id=1, source_target_pairs={{0,8},{1,9},{2,10},{3,11},{4,12},{5,13},{6,14},{7,15},{8,16},{9,17... | collective-permute-start | bytes 1572872 | tf_op jit(solution)/shard_map/ppermute | solution.py:40
  3.0 16.2 %collective-permute-start = (bf16[2,256,512]{2,1,0:T(8,128)(2,1)S(1)}, bf16[2,256,512]{2,1,0:T(8,128)(2,1)S(1)}, u32[]{:S(2)}, u32[]{:S(2)}) collective-permute-start(bf16[2,256,512]{2,1,0:T(8,128)(2,1)S(1)} %get-tuple-element.74), channel_id=1, source_target_pairs={{0,120},{1,121},{2,122},{3,123},{4,124},{5,125},{6,126},{7,127},{8... | collective-permute-start | bytes 1572872 | tf_op jit(solution)/shard_map/ppermute | solution.py:40
  19.3 2.2 %collective-permute-start.2 = (bf16[16,512]{1,0:T(8,128)(2,1)S(1)}, bf16[16,512]{1,0:T(8,128)(2,1)S(1)}, u32[]{:S(2)}, u32[]{:S(2)}) collective-permute-start(bf16[16,512]{1,0:T(8,128)(2,1)S(1)} %reshape.31), channel_id=1, source_target_pairs={{0,1},{1,2},{2,3},{3,4},{4,5},{5,6},{6,7},{7,0},{8,9},{9,10},{10,1... | collective-permute-start | bytes 49160 | tf_op jit(solution)/shard_map/ppermute | solution.py:40
  20.7 4.4 %collective-permute-start.3 = (bf16[16,512]{1,0:T(8,128)(2,1)S(1)}, bf16[16,512]{1,0:T(8,128)(2,1)S(1)}, u32[]{:S(2)}, u32[]{:S(2)}) collective-permute-start(bf16[16,512]{1,0:T(8,128)(2,1)S(1)} %reshape.32), channel_id=1, source_target_pairs={{0,7},{1,0},{2,1},{3,2},{4,3},{5,4},{6,5},{7,6},{8,15},{9,8},{10,9... | collective-permute-start | bytes 49160 | tf_op jit(solution)/shard_map/ppermute | solution.py:40
  39.7 16.2 %copy-start.5 = (bf16[256,512]{1,0:T(8,128)(2,1)}, bf16[256,512]{1,0:T(8,128)(2,1)S(1)}, u32[]{:S(2)}) copy-start(bf16[256,512]{1,0:T(8,128)(2,1)S(1)} %get-tuple-element.65.refs_19_) | copy-start | bytes 786436
  39.8 16.2 %copy-start.6 = (bf16[256,512]{1,0:T(8,128)(2,1)}, bf16[256,512]{1,0:T(8,128)(2,1)S(1)}, u32[]{:S(2)}) copy-start(bf16[256,512]{1,0:T(8,128)(2,1)S(1)} %get-tuple-element.64.refs_18_) | copy-start | bytes 786436
  39.8 6.8 %collective-permute-start.5 = (bf16[80,512]{1,0:T(8,128)(2,1)S(1)}, bf16[80,512]{1,0:T(8,128)(2,1)S(1)}, u32[]{:S(2)}, u32[]{:S(2)}) collective-permute-start(bf16[80,512]{1,0:T(8,128)(2,1)S(1)} %get-tuple-element.43), channel_id=1, source_target_pairs={{0,8},{1,9},{2,10},{3,11},{4,12},{5,13},{6,14},{7,15},{8,16},{9,17... | collective-permute-start | bytes 245768 | tf_op jit(solution)/shard_map/ppermute | solution.py:40
  39.9 6.7 %collective-permute-start.4 = (bf16[80,512]{1,0:T(8,128)(2,1)S(1)}, bf16[80,512]{1,0:T(8,128)(2,1)S(1)}, u32[]{:S(2)}, u32[]{:S(2)}) collective-permute-start(bf16[80,512]{1,0:T(8,128)(2,1)S(1)} %get-tuple-element.43), channel_id=1, source_target_pairs={{0,120},{1,121},{2,122},{3,123},{4,124},{5,125},{6,126},{7,127},{8... | collective-permute-start | bytes 245768 | tf_op jit(solution)/shard_map/ppermute | solution.py:40
  44.8 4.1 %collective-permute-start.6 = (bf16[16,512]{1,0:T(8,128)(2,1)S(1)}, bf16[16,512]{1,0:T(8,128)(2,1)S(1)}, u32[]{:S(2)}, u32[]{:S(2)}) collective-permute-start(bf16[16,512]{1,0:T(8,128)(2,1)S(1)} %get-tuple-element.44), channel_id=1, source_target_pairs={{0,16},{1,17},{2,18},{3,19},{4,20},{5,21},{6,22},{7,23},{8,24},{9,... | collective-permute-start | bytes 49160 | tf_op jit(solution)/shard_map/ppermute | solution.py:40
  48.9 3.1 %collective-permute-start.9 = (bf16[64,512]{1,0:T(8,128)(2,1)S(1)}, bf16[64,512]{1,0:T(8,128)(2,1)S(1)}, u32[]{:S(2)}, u32[]{:S(2)}) collective-permute-start(bf16[64,512]{1,0:T(8,128)(2,1)S(1)} %pad_maximum_fusion.1), channel_id=1, source_target_pairs={{0,2},{1,3},{2,4},{3,5},{4,6},{5,7},{6,0},{7,1},{8,10},{9,11},{10,... | collective-permute-start | bytes 196616 | tf_op jit(solution)/shard_map/ppermute | solution.py:40
  48.9 4.7 %collective-permute-start.8 = (bf16[64,512]{1,0:T(8,128)(2,1)S(1)}, bf16[64,512]{1,0:T(8,128)(2,1)S(1)}, u32[]{:S(2)}, u32[]{:S(2)}) collective-permute-start(bf16[64,512]{1,0:T(8,128)(2,1)S(1)} %pad_maximum_fusion.1), channel_id=1, source_target_pairs={{0,4},{1,5},{2,6},{3,7},{4,0},{5,1},{6,2},{7,3},{8,12},{9,13},{10,... | collective-permute-start | bytes 196616 | tf_op jit(solution)/shard_map/ppermute | solution.py:40
  51.1 4.8 %collective-permute-start.7 = (bf16[64,512]{1,0:T(8,128)(2,1)S(1)}, bf16[64,512]{1,0:T(8,128)(2,1)S(1)}, u32[]{:S(2)}, u32[]{:S(2)}) collective-permute-start(bf16[64,512]{1,0:T(8,128)(2,1)S(1)} %pad_maximum_fusion.1), channel_id=1, source_target_pairs={{0,6},{1,7},{2,0},{3,1},{4,2},{5,3},{6,4},{7,5},{8,14},{9,15},{10,... | collective-permute-start | bytes 196616 | tf_op jit(solution)/shard_map/ppermute | solution.py:40
  56.0 9.9 %collective-permute-start.11 = (bf16[256,512]{1,0:T(8,128)(2,1)S(1)}, bf16[256,512]{1,0:T(8,128)(2,1)S(1)}, u32[]{:S(2)}, u32[]{:S(2)}) collective-permute-start(bf16[256,512]{1,0:T(8,128)(2,1)S(1)} %constant_dynamic-update-slice_fusion.refs_3_), channel_id=1, source_target_pairs={{0,32},{1,33},{2,34},{3,35},{4,36},{5,37},{6,38},{7,39},{8,40},{9,... | collective-permute-start | bytes 786440 | tf_op jit(solution)/shard_map/ppermute | solution.py:40
  56.1 9.8 %collective-permute-start.10 = (bf16[256,512]{1,0:T(8,128)(2,1)S(1)}, bf16[256,512]{1,0:T(8,128)(2,1)S(1)}, u32[]{:S(2)}, u32[]{:S(2)}) collective-permute-start(bf16[256,512]{1,0:T(8,128)(2,1)S(1)} %constant_dynamic-update-slice_fusion.refs_3_), channel_id=1, source_target_pairs={{0,96},{1,97},{2,98},{3,99},{4,100},{5,101},{6,102},{7,103},{8,104... | collective-permute-start | bytes 786440 | tf_op jit(solution)/shard_map/ppermute | solution.py:40
  65.9 5.0 %collective-permute-start.12 = (bf16[128,512]{1,0:T(8,128)(2,1)S(1)}, bf16[128,512]{1,0:T(8,128)(2,1)S(1)}, u32[]{:S(2)}, u32[]{:S(2)}) collective-permute-start(bf16[128,512]{1,0:T(8,128)(2,1)S(1)} %slice.52), channel_id=1, source_target_pairs={{0,96},{1,97},{2,98},{3,99},{4,100},{5,101},{6,102},{7,103},{8,104... | collective-permute-start | bytes 393224 | tf_op jit(solution)/shard_map/ppermute | solution.py:40
  66.0 7.3 %collective-permute-start.13 = (bf16[128,512]{1,0:T(8,128)(2,1)S(1)}, bf16[128,512]{1,0:T(8,128)(2,1)S(1)}, u32[]{:S(2)}, u32[]{:S(2)}) collective-permute-start(bf16[128,512]{1,0:T(8,128)(2,1)S(1)} %slice.53), channel_id=1, source_target_pairs={{0,32},{1,33},{2,34},{3,35},{4,36},{5,37},{6,38},{7,39},{8,40},{9,... | collective-permute-start | bytes 393224 | tf_op jit(solution)/shard_map/ppermute | solution.py:40
  67.5 7.7 %collective-permute-start.20 = (bf16[192,512]{1,0:T(8,128)(2,1)S(1)}, bf16[192,512]{1,0:T(8,128)(2,1)S(1)}, u32[]{:S(2)}, u32[]{:S(2)}) collective-permute-start(bf16[192,512]{1,0:T(8,128)(2,1)S(1)} %pad_maximum_fusion), channel_id=1, source_target_pairs={{0,1},{1,0},{2,3},{3,2},{4,5},{5,4},{6,7},{7,6},{8,9},{9,8},{10,11... | collective-permute-start | bytes 589832 | tf_op jit(solution)/shard_map/ppermute | solution.py:40
  70.6 6.3 %collective-permute-start.19 = (bf16[192,512]{1,0:T(8,128)(2,1)S(1)}, bf16[192,512]{1,0:T(8,128)(2,1)S(1)}, u32[]{:S(2)}, u32[]{:S(2)}) collective-permute-start(bf16[192,512]{1,0:T(8,128)(2,1)S(1)} %pad_maximum_fusion), channel_id=1, source_target_pairs={{0,7},{1,2},{2,1},{3,4},{4,3},{5,6},{6,5},{7,0},{8,15},{9,10},{10,... | collective-permute-start | bytes 589832 | tf_op jit(solution)/shard_map/ppermute | solution.py:40
  70.9 6.0 %collective-permute-start.14 = (bf16[256,512]{1,0:T(8,128)(2,1)S(1)}, bf16[256,512]{1,0:T(8,128)(2,1)S(1)}, u32[]{:S(2)}, u32[]{:S(2)}) collective-permute-start(bf16[256,512]{1,0:T(8,128)(2,1)S(1)} %constant_dynamic-update-slice_fusion.refs_3_), channel_id=1, source_target_pairs={{0,1},{1,0},{2,3},{3,2},{4,5},{5,4},{6,7},{7,6},{8,9},{9,8},{10,11... | collective-permute-start | bytes 786440 | tf_op jit(solution)/shard_map/ppermute | solution.py:40
  70.9 7.4 %collective-permute-start.15 = (bf16[256,512]{1,0:T(8,128)(2,1)S(1)}, bf16[256,512]{1,0:T(8,128)(2,1)S(1)}, u32[]{:S(2)}, u32[]{:S(2)}) collective-permute-start(bf16[256,512]{1,0:T(8,128)(2,1)S(1)} %collective-permute-done.11.refs_4_), channel_id=1, source_target_pairs={{0,1},{1,0},{2,3},{3,2},{4,5},{5,4},{6,7},{7,6},{8,9},{9,8},{10,11... | collective-permute-start | bytes 786440 | tf_op jit(solution)/shard_map/ppermute | solution.py:40
  73.3 5.0 %collective-permute-start.16 = (bf16[256,512]{1,0:T(8,128)(2,1)S(1)}, bf16[256,512]{1,0:T(8,128)(2,1)S(1)}, u32[]{:S(2)}, u32[]{:S(2)}) collective-permute-start(bf16[256,512]{1,0:T(8,128)(2,1)S(1)} %collective-permute-done.10.refs_5_), channel_id=1, source_target_pairs={{0,1},{1,0},{2,3},{3,2},{4,5},{5,4},{6,7},{7,6},{8,9},{9,8},{10,11... | collective-permute-start | bytes 786440 | tf_op jit(solution)/shard_map/ppermute | solution.py:40
  75.2 1.7 %collective-permute-start.17 = (bf16[128,512]{1,0:T(8,128)(2,1)S(1)}, bf16[128,512]{1,0:T(8,128)(2,1)S(1)}, u32[]{:S(2)}, u32[]{:S(2)}) collective-permute-start(bf16[128,512]{1,0:T(8,128)(2,1)S(1)} %collective-permute-done.13.refs_6_), channel_id=1, source_target_pairs={{0,1},{1,0},{2,3},{3,2},{4,5},{5,4},{6,7},{7,6},{8,9},{9,8},{10,11... | collective-permute-start | bytes 393224 | tf_op jit(solution)/shard_map/ppermute | solution.py:40
  76.9 1.3 %collective-permute-start.18 = (bf16[128,512]{1,0:T(8,128)(2,1)S(1)}, bf16[128,512]{1,0:T(8,128)(2,1)S(1)}, u32[]{:S(2)}, u32[]{:S(2)}) collective-permute-start(bf16[128,512]{1,0:T(8,128)(2,1)S(1)} %collective-permute-done.12.refs_7_), channel_id=1, source_target_pairs={{0,1},{1,0},{2,3},{3,2},{4,5},{5,4},{6,7},{7,6},{8,9},{9,8},{10,11... | collective-permute-start | bytes 393224 | tf_op jit(solution)/shard_map/ppermute | solution.py:40
  78.3 29.5 %copy-start = (bf16[7,512,512]{2,1,0:T(8,128)(2,1)S(1)}, bf16[7,512,512]{2,1,0:T(8,128)(2,1)}, u32[]{:S(2)}) copy-start(bf16[7,512,512]{2,1,0:T(8,128)(2,1)} %w6.1) | copy-start | bytes 11010052
  78.3 29.5 %copy-start.1 = (bf16[1024,512]{1,0:T(8,128)(2,1)S(1)}, bf16[1024,512]{1,0:T(8,128)(2,1)}, u32[]{:S(2)}) copy-start(bf16[1024,512]{1,0:T(8,128)(2,1)} %get-tuple-element.50.cells) | copy-start | bytes 3145732
  78.3 29.5 %copy-start.2 = (s32[3,4,256]{2,1,0:T(4,128)S(1)}, s32[3,4,256]{2,1,0:T(4,128)}, u32[]{:S(2)}) copy-start(s32[3,4,256]{2,1,0:T(4,128)} %snd.3) | copy-start | bytes 36868
  78.3 29.5 %copy-start.3 = (bf16[3,4,256,512]{3,2,1,0:T(8,128)(2,1)S(1)}, bf16[3,4,256,512]{3,2,1,0:T(8,128)(2,1)}, u32[]{:S(2)}) copy-start(bf16[3,4,256,512]{3,2,1,0:T(8,128)(2,1)} %get-tuple-element.53.lead) | copy-start | bytes 9437188
  78.3 29.5 %copy-start.4 = (f32[1024,512]{1,0:T(8,128)S(1)}, f32[1024,512]{1,0:T(8,128)}, u32[]{:S(2)}) copy-start(f32[1024,512]{1,0:T(8,128)} %get-tuple-element.70.self_part) | copy-start | bytes 6291460
  93.5 6.9 %collective-permute-start.21 = (bf16[64,512]{1,0:T(8,128)(2,1)S(1)}, bf16[64,512]{1,0:T(8,128)(2,1)S(1)}, u32[]{:S(2)}, u32[]{:S(2)}) collective-permute-start(bf16[64,512]{1,0:T(8,128)(2,1)S(1)} %get-tuple-element.66), channel_id=1, source_target_pairs={{0,8},{1,9},{2,10},{3,11},{4,12},{5,13},{6,14},{7,15},{8,16},{9,17... | collective-permute-start | bytes 196616 | tf_op jit(solution)/shard_map/ppermute | solution.py:40
  93.5 6.9 %collective-permute-start.22 = (bf16[64,512]{1,0:T(8,128)(2,1)S(1)}, bf16[64,512]{1,0:T(8,128)(2,1)S(1)}, u32[]{:S(2)}, u32[]{:S(2)}) collective-permute-start(bf16[64,512]{1,0:T(8,128)(2,1)S(1)} %get-tuple-element.66), channel_id=1, source_target_pairs={{0,120},{1,121},{2,122},{3,123},{4,124},{5,125},{6,126},{7,127},{8... | collective-permute-start | bytes 196616 | tf_op jit(solution)/shard_map/ppermute | solution.py:40
  100.4 2.1 %collective-permute-start.24 = (bf16[192,512]{1,0:T(8,128)(2,1)S(1)}, bf16[192,512]{1,0:T(8,128)(2,1)S(1)}, u32[]{:S(2)}, u32[]{:S(2)}) collective-permute-start(bf16[192,512]{1,0:T(8,128)(2,1)S(1)} %constant_dynamic-update-slice_fusion.7), channel_id=1, source_target_pairs={{0,1},{1,0},{2,3},{3,2},{4,5},{5,4},{6,7},{7,6},{8,9},{9,8},{10,11... | collective-permute-start | bytes 589832 | tf_op jit(solution)/shard_map/ppermute | solution.py:40
  101.5 6.3 %collective-permute-start.23 = (bf16[192,512]{1,0:T(8,128)(2,1)S(1)}, bf16[192,512]{1,0:T(8,128)(2,1)S(1)}, u32[]{:S(2)}, u32[]{:S(2)}) collective-permute-start(bf16[192,512]{1,0:T(8,128)(2,1)S(1)} %constant_dynamic-update-slice_fusion.7), channel_id=1, source_target_pairs={{0,7},{1,2},{2,1},{3,4},{4,3},{5,6},{6,5},{7,0},{8,15},{9,10},{10,... | collective-permute-start | bytes 589832 | tf_op jit(solution)/shard_map/ppermute | solution.py:40

commit v5 on v4

--- a/solution.py
+++ b/solution.py
@@ -195,10 +195,10 @@
             jax.ShapeDtypeStruct(feats.shape, BF16),
             jax.ShapeDtypeStruct(grid_next.shape, F32),
         ],
-        compiler_params=params(60),
+        compiler_params=params(24),
         cost_estimate=cost(8000, 10 << 20),
         name="decoder_lead",
-    )(feats, grid_next, *[dec_w] * 3)
+    )(stay(feats), stay(grid_next), *[stay(dec_w)] * 3)
 
 
 def edge_sum(before, hidden_weight, target):

time: 120 us -> 119 us (level)
  starting transfers between devices: 32.9 us -> 34.8 us
  waiting for transfers between devices: 29.1 us -> 27.3 us
  Pallas kernels: 53.6 us -> 52.1 us
    ppermute x25, starting transfers between devices: 32.9 us -> 34.8 us  [send(): return lax.ppermute(values, AXES, pairs)]
    ppermute x25, waiting for transfers between devices: 29.1 us -> 27.3 us  [send(): return lax.ppermute(values, AXES, pairs)]
    pallas_call x1, Pallas kernels: 7.15 us -> 5.71 us  [lead_kernel(): pl.pallas_call(lead_body, grid=(lat,), in_specs=[edges, blk, weight(1), w...]
  transfers between devices with their start and end apart: 25 -> 25, of which waited for: 13 -> 14; matrix products, arithmetic and copies ran while one was open for 2% -> 2% of each run, Pallas kernels for 10% -> 9%
where the time goes in v5:
time: 119 us; the launch traced here: 118 us
  Pallas kernels  52.1 us (44%)
  starting transfers between devices  34.8 us (29%)
  waiting for transfers between devices  27.3 us (23%)
  local copies, waits for them, and re-layouts  3.55 us (3%)
    ppermute x25, starting transfers between devices, send(): return lax.ppermute(values, AXES, pairs)  34.8 us
    ppermute x25, waiting for transfers between devices, send(): return lax.ppermute(values, AXES, pairs)  27.3 us
    pallas_call x1, Pallas kernels, proc_kernel(): pl.pallas_call(proc_body, in_specs=[HBM] * 3 + [ANY] * 15 + [HBM] * 4, ou...  15.1 us
    pallas_call x1, Pallas kernels, enc_kernel(): pl.pallas_call(enc_body, in_specs=[HBM] * 5 + [ANY] * 4 + [HBM] * 3, out_...  14.7 us
    pallas_call x1, Pallas kernels, dec_kernel(): pl.pallas_call(dec_body, grid=(lat,), in_specs=[whole(senders.shape), pl....  11.7 us
    pallas_call x1, Pallas kernels, lead_kernel(): pl.pallas_call(lead_body, grid=(lat,), in_specs=[edges, blk, weight(1), w...  5.71 us
    pallas_call x1, Pallas kernels, grid_kernel(): pl.pallas_call(grid_body, grid=(2,), in_specs=[SMEM, blk, weight(0), weig...  4.94 us
  transfers between devices with their start and end apart: 25, of which 14 were waited for; matrix products, arithmetic and copies ran while one was open for 2% of the time, Pallas kernels for 9%

profile of v5, /device:TPU:7, one launch (start us, length us, event | category | flops | bytes accessed | tf_op | source)
XLA Modules:
  0.0 118.1 jit_solution(7920364253893557379)
XLA Ops:
  0.0 1.3 %fusion.1 = (bf16[2,256,512]{2,1,0:T(8,128)(2,1)S(1)}, bf16[2,256,512]{2,1,0:T(8,128)(2,1)S(1)}) fusion(bf16[4,256,512]{2,1,0:T(8,128)(2,1)} %param.14), kind=kLoop, calls=%fused_computation.15 | loop fusion | bytes 2097152 | tf_op jit(solution)/shard_map/slice | solution.py:456
  1.3 1.7 %collective-permute-start.1 = (bf16[2,256,512]{2,1,0:T(8,128)(2,1)S(1)}, bf16[2,256,512]{2,1,0:T(8,128)(2,1)S(1)}, u32[]{:S(2)}, u32[]{:S(2)}) collective-permute-start(bf16[2,256,512]{2,1,0:T(8,128)(2,1)S(1)} %get-tuple-element.73), channel_id=1, source_target_pairs={{0,8},{1,9},{2,10},{3,11},{4,12},{5,13},{6,14},{7,15},{8,16},{9,17... | collective-permute-start | bytes 1572872 | tf_op jit(solution)/shard_map/ppermute | solution.py:40
  3.0 4.7 %collective-permute-start = (bf16[2,256,512]{2,1,0:T(8,128)(2,1)S(1)}, bf16[2,256,512]{2,1,0:T(8,128)(2,1)S(1)}, u32[]{:S(2)}, u32[]{:S(2)}) collective-permute-start(bf16[2,256,512]{2,1,0:T(8,128)(2,1)S(1)} %get-tuple-element.74), channel_id=1, source_target_pairs={{0,120},{1,121},{2,122},{3,123},{4,124},{5,125},{6,126},{7,127},{8... | collective-permute-start | bytes 1572872 | tf_op jit(solution)/shard_map/ppermute | solution.py:40
  7.6 1.3 %copy.35.blocks = s32[16,8]{1,0:T(8,128)} copy(s32[16,8]{0,1:T(8,128)} %param.19) | data formatting | bytes 1024 | tf_op args[5]
  9.0 0.8 fusion
  9.8 4.9 %grid_cells.1 = (bf16[1024,512]{1,0:T(8,128)(2,1)}, bf16[1024,512]{1,0:T(8,128)(2,1)}, s32[8,128]{1,0:T(8,128)}) custom-call(s32[16,8]{1,0:T(8,128)} %copy.35.blocks, bf16[1024,512]{1,0:T(8,128)(2,1)} %bitcast.9, bf16[9,512,512]{2,1,0:T(8,128)(2,1)} %enc_w.1, bf16[9,512,512]{2,1,0:T(8,128)(2,1)} %enc_w.1, bf16[9,512,512]{2,1,0:T(8,128)(2,1)} %enc_w.1), custom_call_target="tpu_custom_call" | custom-call | flops 2621440000 | bytes 5242880 | tf_op jit(solution)/shard_map/grid_cells/pallas_call | solution.py:164
  14.7 4.5 %collective-permute-done.1 = bf16[2,256,512]{2,1,0:T(8,128)(2,1)S(1)} collective-permute-done((bf16[2,256,512]{2,1,0:T(8,128)(2,1)S(1)}, bf16[2,256,512]{2,1,0:T(8,128)(2,1)S(1)}, u32[]{:S(2)}, u32[]{:S(2)}) %collective-permute-start.1) | collective-permute-done | bytes 524320 | tf_op jit(solution)/shard_map/ppermute | solution.py:40
  19.3 1.3 %collective-permute-start.2 = (bf16[16,512]{1,0:T(8,128)(2,1)S(1)}, bf16[16,512]{1,0:T(8,128)(2,1)S(1)}, u32[]{:S(2)}, u32[]{:S(2)}) collective-permute-start(bf16[16,512]{1,0:T(8,128)(2,1)S(1)} %reshape.31), channel_id=1, source_target_pairs={{0,1},{1,2},{2,3},{3,4},{4,5},{5,6},{6,7},{7,0},{8,9},{9,10},{10,1... | collective-permute-start | bytes 49160 | tf_op jit(solution)/shard_map/ppermute | solution.py:40
  20.7 0.9 collective-permute-done.2.west
  21.5 3.5 %collective-permute-done.3.east = bf16[16,512]{1,0:T(8,128)(2,1)S(1)} collective-permute-done((bf16[16,512]{1,0:T(8,128)(2,1)S(1)}, bf16[16,512]{1,0:T(8,128)(2,1)S(1)}, u32[]{:S(2)}, u32[]{:S(2)}) %collective-permute-start.3) | collective-permute-done | bytes 16416 | tf_op jit(solution)/shard_map/ppermute | solution.py:40
  25.0 14.7 %encoder_edges.1 = (bf16[256,512]{1,0:T(8,128)(2,1)S(1)}, bf16[256,512]{1,0:T(8,128)(2,1)S(1)}, bf16[256,512]{1,0:T(8,128)(2,1)S(1)}, bf16[80,512]{1,0:T(8,128)(...) custom-call(s32[8,128]{1,0:T(8,128)} %get-tuple-element.38.live, s32[1,1,2048]{2,1,0:T(1,128)} %snd.2, ...), custom_call_target="tpu_custom_call" | custom-call | flops 13107200000 | bytes 10485760 | tf_op jit(solution)/shard_map/encoder_edges/pallas_call | solution.py:272
  39.7 0.0 copy-start.4
  39.8 0.1 collective-permute-start.5
  39.9 5.0 %collective-permute-start.4 = (bf16[80,512]{1,0:T(8,128)(2,1)S(1)}, bf16[80,512]{1,0:T(8,128)(2,1)S(1)}, u32[]{:S(2)}, u32[]{:S(2)}) collective-permute-start(bf16[80,512]{1,0:T(8,128)(2,1)S(1)} %get-tuple-element.43), channel_id=1, source_target_pairs={{0,120},{1,121},{2,122},{3,123},{4,124},{5,125},{6,126},{7,127},{8... | collective-permute-start | bytes 245768 | tf_op jit(solution)/shard_map/ppermute | solution.py:40
  44.8 0.0 collective-permute-start.6
  44.8 1.7 %collective-permute-done.5.refs_13_ = bf16[80,512]{1,0:T(8,128)(2,1)S(1)} collective-permute-done((bf16[80,512]{1,0:T(8,128)(2,1)S(1)}, bf16[80,512]{1,0:T(8,128)(2,1)S(1)}, u32[]{:S(2)}, u32[]{:S(2)}) %collective-permute-start.5) | collective-permute-done | bytes 81952 | tf_op jit(solution)/shard_map/ppermute | solution.py:40
  46.6 0.0 collective-permute-done.4.refs_15_
  46.6 2.3 %collective-permute-done.6 = bf16[16,512]{1,0:T(8,128)(2,1)S(1)} collective-permute-done((bf16[16,512]{1,0:T(8,128)(2,1)S(1)}, bf16[16,512]{1,0:T(8,128)(2,1)S(1)}, u32[]{:S(2)}, u32[]{:S(2)}) %collective-permute-start.6) | collective-permute-done | bytes 16416 | tf_op jit(solution)/shard_map/ppermute | solution.py:40
  48.9 0.0 collective-permute-start.9
  48.9 2.2 %collective-permute-start.8 = (bf16[64,512]{1,0:T(8,128)(2,1)S(1)}, bf16[64,512]{1,0:T(8,128)(2,1)S(1)}, u32[]{:S(2)}, u32[]{:S(2)}) collective-permute-start(bf16[64,512]{1,0:T(8,128)(2,1)S(1)} %pad_maximum_fusion.1), channel_id=1, source_target_pairs={{0,4},{1,5},{2,6},{3,7},{4,0},{5,1},{6,2},{7,3},{8,12},{9,13},{10,... | collective-permute-start | bytes 196616 | tf_op jit(solution)/shard_map/ppermute | solution.py:40
  51.1 0.0 collective-permute-start.7
  51.1 0.9 collective-permute-done.9
  52.0 1.6 %collective-permute-done.8 = bf16[64,512]{1,0:T(8,128)(2,1)S(1)} collective-permute-done((bf16[64,512]{1,0:T(8,128)(2,1)S(1)}, bf16[64,512]{1,0:T(8,128)(2,1)S(1)}, u32[]{:S(2)}, u32[]{:S(2)}) %collective-permute-start.8) | collective-permute-done | bytes 65568 | tf_op jit(solution)/shard_map/ppermute | solution.py:40
  53.6 2.3 %collective-permute-done.7 = bf16[64,512]{1,0:T(8,128)(2,1)S(1)} collective-permute-done((bf16[64,512]{1,0:T(8,128)(2,1)S(1)}, bf16[64,512]{1,0:T(8,128)(2,1)S(1)}, u32[]{:S(2)}, u32[]{:S(2)}) %collective-permute-start.7) | collective-permute-done | bytes 65568 | tf_op jit(solution)/shard_map/ppermute | solution.py:40
  56.0 0.1 collective-permute-start.11
  56.1 2.7 %collective-permute-start.10 = (bf16[256,512]{1,0:T(8,128)(2,1)S(1)}, bf16[256,512]{1,0:T(8,128)(2,1)S(1)}, u32[]{:S(2)}, u32[]{:S(2)}) collective-permute-start(bf16[256,512]{1,0:T(8,128)(2,1)S(1)} %constant_dynamic-update-slice_fusion.refs_3_), channel_id=1, source_target_pairs={{0,96},{1,97},{2,98},{3,99},{4,100},{5,101},{6,102},{7,103},{8,104... | collective-permute-start | bytes 786440 | tf_op jit(solution)/shard_map/ppermute | solution.py:40
  58.7 5.7 %decoder_lead.1 = (bf16[3,4,256,512]{3,2,1,0:T(8,128)(2,1)S(1)}, f32[1024,512]{1,0:T(8,128)S(1)}) custom-call(bf16[3,4,256,512]{3,2,1,0:T(8,128)(2,1)} %feat.1, bf16[1024,512]{1,0:T(8,128)(2,1)} %get-tuple-element.50.cells, bf16[7,512,512]{2,1,0:T(8,128)(2,1)} %w6.1, bf16[7,512,512]{2,1,0:T(8,128)(2,1)} %w6.1, bf16[7,512,512]{2,1,0:T(8,128)(2,1)} %w6.1), custom_call_target="tpu_custom_call" | custom-call | flops 4194304000 | bytes 10485760 | tf_op jit(solution)/shard_map/decoder_lead/pallas_call | solution.py:189
  64.5 1.3 %collective-permute-start.12 = (bf16[128,512]{1,0:T(8,128)(2,1)S(1)}, bf16[128,512]{1,0:T(8,128)(2,1)S(1)}, u32[]{:S(2)}, u32[]{:S(2)}) collective-permute-start(bf16[128,512]{1,0:T(8,128)(2,1)S(1)} %slice.52), channel_id=1, source_target_pairs={{0,96},{1,97},{2,98},{3,99},{4,100},{5,101},{6,102},{7,103},{8,104... | collective-permute-start | bytes 393224 | tf_op jit(solution)/shard_map/ppermute | solution.py:40
  65.8 0.3 collective-permute-start.13
  66.1 3.2 %collective-permute-start.20 = (bf16[192,512]{1,0:T(8,128)(2,1)S(1)}, bf16[192,512]{1,0:T(8,128)(2,1)S(1)}, u32[]{:S(2)}, u32[]{:S(2)}) collective-permute-start(bf16[192,512]{1,0:T(8,128)(2,1)S(1)} %pad_maximum_fusion), channel_id=1, source_target_pairs={{0,1},{1,0},{2,3},{3,2},{4,5},{5,4},{6,7},{7,6},{8,9},{9,8},{10,11... | collective-permute-start | bytes 589832 | tf_op jit(solution)/shard_map/ppermute | solution.py:40
  69.3 0.6 collective-permute-start.19
  69.9 1.9 %collective-permute-start.15 = (bf16[256,512]{1,0:T(8,128)(2,1)S(1)}, bf16[256,512]{1,0:T(8,128)(2,1)S(1)}, u32[]{:S(2)}, u32[]{:S(2)}) collective-permute-start(bf16[256,512]{1,0:T(8,128)(2,1)S(1)} %collective-permute-done.11.refs_4_), channel_id=1, source_target_pairs={{0,1},{1,0},{2,3},{3,2},{4,5},{5,4},{6,7},{7,6},{8,9},{9,8},{10,11... | collective-permute-start | bytes 786440 | tf_op jit(solution)/shard_map/ppermute | solution.py:40
  71.9 3.3 %collective-permute-start.16 = (bf16[256,512]{1,0:T(8,128)(2,1)S(1)}, bf16[256,512]{1,0:T(8,128)(2,1)S(1)}, u32[]{:S(2)}, u32[]{:S(2)}) collective-permute-start(bf16[256,512]{1,0:T(8,128)(2,1)S(1)} %collective-permute-done.10.refs_5_), channel_id=1, source_target_pairs={{0,1},{1,0},{2,3},{3,2},{4,5},{5,4},{6,7},{7,6},{8,9},{9,8},{10,11... | collective-permute-start | bytes 786440 | tf_op jit(solution)/shard_map/ppermute | solution.py:40
  75.2 0.0 collective-permute-start.17
  75.2 0.4 collective-permute-done.19.refs_17_
  75.6 0.1 collective-permute-start.18
  75.7 0.8 collective-permute-done.17.refs_11_
  76.6 0.4 collective-permute-done.18.refs_12_
  77.0 0.0 copy-start.2
  77.0 15.1 %mesh_edges.1 = (bf16[256,512]{1,0:T(8,128)(2,1)S(1)}, bf16[64,512]{1,0:T(8,128)(2,1)S(1)}) custom-call(s32[1,1,2048]{2,1,0:T(1,128)} %refs_0_.1, s32[1,1,2048]{2,1,0:T(1,128)} %refs_1_.1, bf16[2048,512]{1,0:T(8,128)(2,1)} %bitcast.11, bf16[256,512]{1,0:T(8,128)(2,1)S(1)} %constant_dynamic-update-slice_fusion.refs_3_, ...), custom_call_target="tpu_custom_call" | custom-call | flops 13107200000 | bytes 10485760 | tf_op jit(solution)/shard_map/mesh_edges/pallas_call | solution.py:340
  92.1 0.1 collective-permute-start.21
  92.2 4.8 %collective-permute-start.22 = (bf16[64,512]{1,0:T(8,128)(2,1)S(1)}, bf16[64,512]{1,0:T(8,128)(2,1)S(1)}, u32[]{:S(2)}, u32[]{:S(2)}) collective-permute-start(bf16[64,512]{1,0:T(8,128)(2,1)S(1)} %get-tuple-element.66), channel_id=1, source_target_pairs={{0,120},{1,121},{2,122},{3,123},{4,124},{5,125},{6,126},{7,127},{8... | collective-permute-start | bytes 196616 | tf_op jit(solution)/shard_map/ppermute | solution.py:40
  97.0 2.1 %collective-permute-done.21.above = bf16[64,512]{1,0:T(8,128)(2,1)S(1)} collective-permute-done((bf16[64,512]{1,0:T(8,128)(2,1)S(1)}, bf16[64,512]{1,0:T(8,128)(2,1)S(1)}, u32[]{:S(2)}, u32[]{:S(2)}) %collective-permute-start.21) | collective-permute-done | bytes 65568 | tf_op jit(solution)/shard_map/ppermute | solution.py:40
  99.1 1.0 collective-permute-start.24
  100.1 0.5 collective-permute-start.23
  100.7 0.5 collective-permute-done.24.beside
  101.2 5.2 %collective-permute-done.23.across = bf16[192,512]{1,0:T(8,128)(2,1)S(1)} collective-permute-done((bf16[192,512]{1,0:T(8,128)(2,1)S(1)}, bf16[192,512]{1,0:T(8,128)(2,1)S(1)}, u32[]{:S(2)}, u32[]{:S(2)}) %collective-permute-start.23) | collective-permute-done | bytes 196640 | tf_op jit(solution)/shard_map/ppermute | solution.py:40
  106.5 11.7 %decoder_edges.1 = bf16[1024,512]{1,0:T(8,128)(2,1)} custom-call(s32[3,4,256]{2,1,0:T(4,128)S(1)} %copy-done.2, bf16[3,4,256,512]{3,2,1,0:T(8,128)(2,1)S(1)} %get-tuple-element.53.lead, bf16[64,512]{1,0:T(8,128)(2,1)S(1)} %collective-permute-done.21.above, bf16[256,512]{1,0:T(8,128)(2,1)S(1)} %get-tuple-element.67.own, ...), custom_call_target="tpu_custom_call" | custom-call | flops 7864320000 | bytes 9437184 | tf_op jit(solution)/shard_map/decoder_edges/pallas_call | solution.py:387
  (41 shorter events, 0.2 us)
Async XLA Ops:
  1.3 17.9 %collective-permute-start.1 = (bf16[2,256,512]{2,1,0:T(8,128)(2,1)S(1)}, bf16[2,256,512]{2,1,0:T(8,128)(2,1)S(1)}, u32[]{:S(2)}, u32[]{:S(2)}) collective-permute-start(bf16[2,256,512]{2,1,0:T(8,128)(2,1)S(1)} %get-tuple-element.73), channel_id=1, source_target_pairs={{0,8},{1,9},{2,10},{3,11},{4,12},{5,13},{6,14},{7,15},{8,16},{9,17... | collective-permute-start | bytes 1572872 | tf_op jit(solution)/shard_map/ppermute | solution.py:40
  3.0 16.2 %collective-permute-start = (bf16[2,256,512]{2,1,0:T(8,128)(2,1)S(1)}, bf16[2,256,512]{2,1,0:T(8,128)(2,1)S(1)}, u32[]{:S(2)}, u32[]{:S(2)}) collective-permute-start(bf16[2,256,512]{2,1,0:T(8,128)(2,1)S(1)} %get-tuple-element.74), channel_id=1, source_target_pairs={{0,120},{1,121},{2,122},{3,123},{4,124},{5,125},{6,126},{7,127},{8... | collective-permute-start | bytes 1572872 | tf_op jit(solution)/shard_map/ppermute | solution.py:40
  19.3 2.2 %collective-permute-start.2 = (bf16[16,512]{1,0:T(8,128)(2,1)S(1)}, bf16[16,512]{1,0:T(8,128)(2,1)S(1)}, u32[]{:S(2)}, u32[]{:S(2)}) collective-permute-start(bf16[16,512]{1,0:T(8,128)(2,1)S(1)} %reshape.31), channel_id=1, source_target_pairs={{0,1},{1,2},{2,3},{3,4},{4,5},{5,6},{6,7},{7,0},{8,9},{9,10},{10,1... | collective-permute-start | bytes 49160 | tf_op jit(solution)/shard_map/ppermute | solution.py:40
  20.7 4.4 %collective-permute-start.3 = (bf16[16,512]{1,0:T(8,128)(2,1)S(1)}, bf16[16,512]{1,0:T(8,128)(2,1)S(1)}, u32[]{:S(2)}, u32[]{:S(2)}) collective-permute-start(bf16[16,512]{1,0:T(8,128)(2,1)S(1)} %reshape.32), channel_id=1, source_target_pairs={{0,7},{1,0},{2,1},{3,2},{4,3},{5,4},{6,5},{7,6},{8,15},{9,8},{10,9... | collective-permute-start | bytes 49160 | tf_op jit(solution)/shard_map/ppermute | solution.py:40
  39.7 16.2 %copy-start.4 = (bf16[256,512]{1,0:T(8,128)(2,1)}, bf16[256,512]{1,0:T(8,128)(2,1)S(1)}, u32[]{:S(2)}) copy-start(bf16[256,512]{1,0:T(8,128)(2,1)S(1)} %get-tuple-element.64.refs_18_) | copy-start | bytes 786436
  39.8 24.7 %copy-start.3 = (bf16[256,512]{1,0:T(8,128)(2,1)}, bf16[256,512]{1,0:T(8,128)(2,1)S(1)}, u32[]{:S(2)}) copy-start(bf16[256,512]{1,0:T(8,128)(2,1)S(1)} %get-tuple-element.65.refs_19_) | copy-start | bytes 786436
  39.8 6.8 %collective-permute-start.5 = (bf16[80,512]{1,0:T(8,128)(2,1)S(1)}, bf16[80,512]{1,0:T(8,128)(2,1)S(1)}, u32[]{:S(2)}, u32[]{:S(2)}) collective-permute-start(bf16[80,512]{1,0:T(8,128)(2,1)S(1)} %get-tuple-element.43), channel_id=1, source_target_pairs={{0,8},{1,9},{2,10},{3,11},{4,12},{5,13},{6,14},{7,15},{8,16},{9,17... | collective-permute-start | bytes 245768 | tf_op jit(solution)/shard_map/ppermute | solution.py:40
  39.9 6.7 %collective-permute-start.4 = (bf16[80,512]{1,0:T(8,128)(2,1)S(1)}, bf16[80,512]{1,0:T(8,128)(2,1)S(1)}, u32[]{:S(2)}, u32[]{:S(2)}) collective-permute-start(bf16[80,512]{1,0:T(8,128)(2,1)S(1)} %get-tuple-element.43), channel_id=1, source_target_pairs={{0,120},{1,121},{2,122},{3,123},{4,124},{5,125},{6,126},{7,127},{8... | collective-permute-start | bytes 245768 | tf_op jit(solution)/shard_map/ppermute | solution.py:40
  44.8 4.1 %collective-permute-start.6 = (bf16[16,512]{1,0:T(8,128)(2,1)S(1)}, bf16[16,512]{1,0:T(8,128)(2,1)S(1)}, u32[]{:S(2)}, u32[]{:S(2)}) collective-permute-start(bf16[16,512]{1,0:T(8,128)(2,1)S(1)} %get-tuple-element.44), channel_id=1, source_target_pairs={{0,16},{1,17},{2,18},{3,19},{4,20},{5,21},{6,22},{7,23},{8,24},{9,... | collective-permute-start | bytes 49160 | tf_op jit(solution)/shard_map/ppermute | solution.py:40
  48.9 3.1 %collective-permute-start.9 = (bf16[64,512]{1,0:T(8,128)(2,1)S(1)}, bf16[64,512]{1,0:T(8,128)(2,1)S(1)}, u32[]{:S(2)}, u32[]{:S(2)}) collective-permute-start(bf16[64,512]{1,0:T(8,128)(2,1)S(1)} %pad_maximum_fusion.1), channel_id=1, source_target_pairs={{0,2},{1,3},{2,4},{3,5},{4,6},{5,7},{6,0},{7,1},{8,10},{9,11},{10,... | collective-permute-start | bytes 196616 | tf_op jit(solution)/shard_map/ppermute | solution.py:40
  48.9 4.7 %collective-permute-start.8 = (bf16[64,512]{1,0:T(8,128)(2,1)S(1)}, bf16[64,512]{1,0:T(8,128)(2,1)S(1)}, u32[]{:S(2)}, u32[]{:S(2)}) collective-permute-start(bf16[64,512]{1,0:T(8,128)(2,1)S(1)} %pad_maximum_fusion.1), channel_id=1, source_target_pairs={{0,4},{1,5},{2,6},{3,7},{4,0},{5,1},{6,2},{7,3},{8,12},{9,13},{10,... | collective-permute-start | bytes 196616 | tf_op jit(solution)/shard_map/ppermute | solution.py:40
  51.1 4.8 %collective-permute-start.7 = (bf16[64,512]{1,0:T(8,128)(2,1)S(1)}, bf16[64,512]{1,0:T(8,128)(2,1)S(1)}, u32[]{:S(2)}, u32[]{:S(2)}) collective-permute-start(bf16[64,512]{1,0:T(8,128)(2,1)S(1)} %pad_maximum_fusion.1), channel_id=1, source_target_pairs={{0,6},{1,7},{2,0},{3,1},{4,2},{5,3},{6,4},{7,5},{8,14},{9,15},{10,... | collective-permute-start | bytes 196616 | tf_op jit(solution)/shard_map/ppermute | solution.py:40
  56.0 8.5 %collective-permute-start.11 = (bf16[256,512]{1,0:T(8,128)(2,1)S(1)}, bf16[256,512]{1,0:T(8,128)(2,1)S(1)}, u32[]{:S(2)}, u32[]{:S(2)}) collective-permute-start(bf16[256,512]{1,0:T(8,128)(2,1)S(1)} %constant_dynamic-update-slice_fusion.refs_3_), channel_id=1, source_target_pairs={{0,32},{1,33},{2,34},{3,35},{4,36},{5,37},{6,38},{7,39},{8,40},{9,... | collective-permute-start | bytes 786440 | tf_op jit(solution)/shard_map/ppermute | solution.py:40
  56.1 8.4 %collective-permute-start.10 = (bf16[256,512]{1,0:T(8,128)(2,1)S(1)}, bf16[256,512]{1,0:T(8,128)(2,1)S(1)}, u32[]{:S(2)}, u32[]{:S(2)}) collective-permute-start(bf16[256,512]{1,0:T(8,128)(2,1)S(1)} %constant_dynamic-update-slice_fusion.refs_3_), channel_id=1, source_target_pairs={{0,96},{1,97},{2,98},{3,99},{4,100},{5,101},{6,102},{7,103},{8,104... | collective-permute-start | bytes 786440 | tf_op jit(solution)/shard_map/ppermute | solution.py:40
  64.5 5.4 %collective-permute-start.12 = (bf16[128,512]{1,0:T(8,128)(2,1)S(1)}, bf16[128,512]{1,0:T(8,128)(2,1)S(1)}, u32[]{:S(2)}, u32[]{:S(2)}) collective-permute-start(bf16[128,512]{1,0:T(8,128)(2,1)S(1)} %slice.52), channel_id=1, source_target_pairs={{0,96},{1,97},{2,98},{3,99},{4,100},{5,101},{6,102},{7,103},{8,104... | collective-permute-start | bytes 393224 | tf_op jit(solution)/shard_map/ppermute | solution.py:40
  65.8 6.1 %collective-permute-start.13 = (bf16[128,512]{1,0:T(8,128)(2,1)S(1)}, bf16[128,512]{1,0:T(8,128)(2,1)S(1)}, u32[]{:S(2)}, u32[]{:S(2)}) collective-permute-start(bf16[128,512]{1,0:T(8,128)(2,1)S(1)} %slice.53), channel_id=1, source_target_pairs={{0,32},{1,33},{2,34},{3,35},{4,36},{5,37},{6,38},{7,39},{8,40},{9,... | collective-permute-start | bytes 393224 | tf_op jit(solution)/shard_map/ppermute | solution.py:40
  66.1 9.1 %collective-permute-start.20 = (bf16[192,512]{1,0:T(8,128)(2,1)S(1)}, bf16[192,512]{1,0:T(8,128)(2,1)S(1)}, u32[]{:S(2)}, u32[]{:S(2)}) collective-permute-start(bf16[192,512]{1,0:T(8,128)(2,1)S(1)} %pad_maximum_fusion), channel_id=1, source_target_pairs={{0,1},{1,0},{2,3},{3,2},{4,5},{5,4},{6,7},{7,6},{8,9},{9,8},{10,11... | collective-permute-start | bytes 589832 | tf_op jit(solution)/shard_map/ppermute | solution.py:40
  69.3 6.3 %collective-permute-start.19 = (bf16[192,512]{1,0:T(8,128)(2,1)S(1)}, bf16[192,512]{1,0:T(8,128)(2,1)S(1)}, u32[]{:S(2)}, u32[]{:S(2)}) collective-permute-start(bf16[192,512]{1,0:T(8,128)(2,1)S(1)} %pad_maximum_fusion), channel_id=1, source_target_pairs={{0,7},{1,2},{2,1},{3,4},{4,3},{5,6},{6,5},{7,0},{8,15},{9,10},{10,... | collective-permute-start | bytes 589832 | tf_op jit(solution)/shard_map/ppermute | solution.py:40
  69.9 5.8 %collective-permute-start.14 = (bf16[256,512]{1,0:T(8,128)(2,1)S(1)}, bf16[256,512]{1,0:T(8,128)(2,1)S(1)}, u32[]{:S(2)}, u32[]{:S(2)}) collective-permute-start(bf16[256,512]{1,0:T(8,128)(2,1)S(1)} %constant_dynamic-update-slice_fusion.refs_3_), channel_id=1, source_target_pairs={{0,1},{1,0},{2,3},{3,2},{4,5},{5,4},{6,7},{7,6},{8,9},{9,8},{10,11... | collective-permute-start | bytes 786440 | tf_op jit(solution)/shard_map/ppermute | solution.py:40
  69.9 7.0 %collective-permute-start.15 = (bf16[256,512]{1,0:T(8,128)(2,1)S(1)}, bf16[256,512]{1,0:T(8,128)(2,1)S(1)}, u32[]{:S(2)}, u32[]{:S(2)}) collective-permute-start(bf16[256,512]{1,0:T(8,128)(2,1)S(1)} %collective-permute-done.11.refs_4_), channel_id=1, source_target_pairs={{0,1},{1,0},{2,3},{3,2},{4,5},{5,4},{6,7},{7,6},{8,9},{9,8},{10,11... | collective-permute-start | bytes 786440 | tf_op jit(solution)/shard_map/ppermute | solution.py:40
  71.9 5.1 %collective-permute-start.16 = (bf16[256,512]{1,0:T(8,128)(2,1)S(1)}, bf16[256,512]{1,0:T(8,128)(2,1)S(1)}, u32[]{:S(2)}, u32[]{:S(2)}) collective-permute-start(bf16[256,512]{1,0:T(8,128)(2,1)S(1)} %collective-permute-done.10.refs_5_), channel_id=1, source_target_pairs={{0,1},{1,0},{2,3},{3,2},{4,5},{5,4},{6,7},{7,6},{8,9},{9,8},{10,11... | collective-permute-start | bytes 786440 | tf_op jit(solution)/shard_map/ppermute | solution.py:40
  75.2 1.3 %collective-permute-start.17 = (bf16[128,512]{1,0:T(8,128)(2,1)S(1)}, bf16[128,512]{1,0:T(8,128)(2,1)S(1)}, u32[]{:S(2)}, u32[]{:S(2)}) collective-permute-start(bf16[128,512]{1,0:T(8,128)(2,1)S(1)} %collective-permute-done.13.refs_6_), channel_id=1, source_target_pairs={{0,1},{1,0},{2,3},{3,2},{4,5},{5,4},{6,7},{7,6},{8,9},{9,8},{10,11... | collective-permute-start | bytes 393224 | tf_op jit(solution)/shard_map/ppermute | solution.py:40
  75.6 1.3 %collective-permute-start.18 = (bf16[128,512]{1,0:T(8,128)(2,1)S(1)}, bf16[128,512]{1,0:T(8,128)(2,1)S(1)}, u32[]{:S(2)}, u32[]{:S(2)}) collective-permute-start(bf16[128,512]{1,0:T(8,128)(2,1)S(1)} %collective-permute-done.12.refs_7_), channel_id=1, source_target_pairs={{0,1},{1,0},{2,3},{3,2},{4,5},{5,4},{6,7},{7,6},{8,9},{9,8},{10,11... | collective-permute-start | bytes 393224 | tf_op jit(solution)/shard_map/ppermute | solution.py:40
  77.0 29.5 %copy-start = (bf16[7,512,512]{2,1,0:T(8,128)(2,1)S(1)}, bf16[7,512,512]{2,1,0:T(8,128)(2,1)}, u32[]{:S(2)}) copy-start(bf16[7,512,512]{2,1,0:T(8,128)(2,1)} %w6.1) | copy-start | bytes 11010052
  77.0 29.5 %copy-start.1 = (bf16[1024,512]{1,0:T(8,128)(2,1)S(1)}, bf16[1024,512]{1,0:T(8,128)(2,1)}, u32[]{:S(2)}) copy-start(bf16[1024,512]{1,0:T(8,128)(2,1)} %get-tuple-element.50.cells) | copy-start | bytes 3145732
  77.0 29.5 %copy-start.2 = (s32[3,4,256]{2,1,0:T(4,128)S(1)}, s32[3,4,256]{2,1,0:T(4,128)}, u32[]{:S(2)}) copy-start(s32[3,4,256]{2,1,0:T(4,128)} %snd.3) | copy-start | bytes 36868
  92.1 6.9 %collective-permute-start.21 = (bf16[64,512]{1,0:T(8,128)(2,1)S(1)}, bf16[64,512]{1,0:T(8,128)(2,1)S(1)}, u32[]{:S(2)}, u32[]{:S(2)}) collective-permute-start(bf16[64,512]{1,0:T(8,128)(2,1)S(1)} %get-tuple-element.66), channel_id=1, source_target_pairs={{0,8},{1,9},{2,10},{3,11},{4,12},{5,13},{6,14},{7,15},{8,16},{9,17... | collective-permute-start | bytes 196616 | tf_op jit(solution)/shard_map/ppermute | solution.py:40
  92.2 6.9 %collective-permute-start.22 = (bf16[64,512]{1,0:T(8,128)(2,1)S(1)}, bf16[64,512]{1,0:T(8,128)(2,1)S(1)}, u32[]{:S(2)}, u32[]{:S(2)}) collective-permute-start(bf16[64,512]{1,0:T(8,128)(2,1)S(1)} %get-tuple-element.66), channel_id=1, source_target_pairs={{0,120},{1,121},{2,122},{3,123},{4,124},{5,125},{6,126},{7,127},{8... | collective-permute-start | bytes 196616 | tf_op jit(solution)/shard_map/ppermute | solution.py:40
  99.1 2.1 %collective-permute-start.24 = (bf16[192,512]{1,0:T(8,128)(2,1)S(1)}, bf16[192,512]{1,0:T(8,128)(2,1)S(1)}, u32[]{:S(2)}, u32[]{:S(2)}) collective-permute-start(bf16[192,512]{1,0:T(8,128)(2,1)S(1)} %constant_dynamic-update-slice_fusion.7), channel_id=1, source_target_pairs={{0,1},{1,0},{2,3},{3,2},{4,5},{5,4},{6,7},{7,6},{8,9},{9,8},{10,11... | collective-permute-start | bytes 589832 | tf_op jit(solution)/shard_map/ppermute | solution.py:40
  100.1 6.3 %collective-permute-start.23 = (bf16[192,512]{1,0:T(8,128)(2,1)S(1)}, bf16[192,512]{1,0:T(8,128)(2,1)S(1)}, u32[]{:S(2)}, u32[]{:S(2)}) collective-permute-start(bf16[192,512]{1,0:T(8,128)(2,1)S(1)} %constant_dynamic-update-slice_fusion.7), channel_id=1, source_target_pairs={{0,7},{1,2},{2,1},{3,4},{4,3},{5,6},{6,5},{7,0},{8,15},{9,10},{10,... | collective-permute-start | bytes 589832 | tf_op jit(solution)/shard_map/ppermute | solution.py:40
